TPU v7x, 32 devices: a whole 2x2x4 slice. The times are simulated.
32 devices in a mesh: dp: 8 (over z, y), bal: 4 (over x, core).
Axes of the slice: x: 2, y: 2, z: 4, core: 2. Of those that a mesh axis runs over, the one named last changes fastest.
Arguments:
- tokens: bfloat16 [16384, 768], P(('dp', 'bal')), may hold values from -6 to 6
- segment_ids: int32 [32, 512], P(('dp', 'bal')), may hold values from 0 to 3, never falling along the last dimension, each value on 1 to 256 neighbouring positions
- mlm_labels: int32 [16384], P(('dp', 'bal')), may hold values from 0 to 30521
- mask_order: int32 [32, 512], P(('dp', 'bal')), may hold values from 0 to 511, each once within a row
- mask_count: int32 [32], P(('dp', 'bal')), may hold values from 14 to 64, as said below
- qkv_weight: bfloat16 [768, 2304], P(('dp', 'bal')), may hold values from -0.21875 to 0.21875
- query_bias: float32 [768], replicated, may hold values from -3 to 3
- value_bias: float32 [768], replicated, may hold values from -3 to 3
- out_weight: bfloat16 [768, 768], P(('dp', 'bal')), may hold values from -0.875 to 0.875
- out_bias: float32 [768], replicated, may hold values from -2 to 2
- attn_gain: float32 [768], replicated, may hold values from 0.25 to 1.75
- attn_shift: float32 [768], replicated, may hold values from -2 to 2
- up_weight: bfloat16 [768, 3072], P(('dp', 'bal')), may hold values from -0.21875 to 0.21875
- up_bias: float32 [3072], replicated, may hold values from -3 to 3
- down_weight: bfloat16 [3072, 768], P(('dp', 'bal')), may hold values from -0.109375 to 0.109375
- down_bias: float32 [768], replicated, may hold values from -2 to 2
- ffn_gain: float32 [768], replicated, may hold values from 0.25 to 1.75
- ffn_shift: float32 [768], replicated, may hold values from -2 to 2
- head_weight: bfloat16 [768, 768], P(('dp', 'bal')), may hold values from -1 to 1
- head_bias: float32 [768], replicated, may hold values from -3 to 3
- head_gain: float32 [768], replicated, may hold values from 0.25 to 1.75
- head_shift: float32 [768], replicated, may hold values from -2 to 2
- decoder: bfloat16 [768, 30522], P(('dp', 'bal')), may hold values from -0.21875 to 0.21875
- decoder_bias: float32 [30522], replicated, may hold values from -2.5 to 2.5
Outputs:
- layer_out: bfloat16 [16384, 768], P(('dp', 'bal'))
- loss: float32 [], replicated
- tokens_grad: float32 [16384, 768], P(('dp', 'bal'))
- qkv_grad: float32 [768, 2304], P(('dp', 'bal'))
- query_bias_grad: float32 [768], replicated
- value_bias_grad: float32 [768], replicated
- out_grad: float32 [768, 768], P(('dp', 'bal'))
- out_bias_grad: float32 [768], replicated
- attn_gain_grad: float32 [768], replicated
- attn_shift_grad: float32 [768], replicated
- up_grad: float32 [768, 3072], P(('dp', 'bal'))
- up_bias_grad: float32 [3072], replicated
- down_grad: float32 [3072, 768], P(('dp', 'bal'))
- down_bias_grad: float32 [768], replicated
- ffn_gain_grad: float32 [768], replicated
- ffn_shift_grad: float32 [768], replicated
- head_grad: float32 [768, 768], P(('dp', 'bal'))
- head_bias_grad: float32 [768], replicated
- head_gain_grad: float32 [768], replicated
- head_shift_grad: float32 [768], replicated
- decoder_grad: float32 [768, 30522], P(('dp', 'bal'))
- decoder_bias_grad: float32 [30522], replicated
Inputs may be any that keep to these rules, and one draw needn't show every extreme that they name: `mask_count`: the 4 counts of one index of dp (consecutive entries) sum to exactly 128; one of them is 64.
All inputs are finite; a program needn't handle non-finite values.
Results may differ from a plain program's by a relative error of at most 0.035.
Values may be sent and summed in bfloat16 or wider, within the bound.
No kernel may reach another device: no remote copies, remote signals or barrier semaphores. Data moves between devices by JAX's collectives and lax.ppermute only.
A program may use at most 384 MiB of HBM per device.

v0:
```python
import jax
import jax.numpy as jnp
from jax import lax
from jax.sharding import PartitionSpec as P

HEADS = 12
HDIM = 64
HEAD_DEV = 32
MASK_DEV = 64


EPSILON = 1e-06
MASK_FILL = -1e30


def layer_norm(hidden, gain_vec, shift_vec):
    average = jnp.mean(hidden, axis=-1, keepdims=True)
    centered = hidden - average
    variance = jnp.mean(centered * centered, axis=-1, keepdims=True)
    return centered * lax.rsqrt(variance + EPSILON) * gain_vec + shift_vec


def gelu_exact(values):
    return jax.nn.gelu(values, approximate=False)


def head_tail(inner_rows, gain_vec, shift_vec):
    return layer_norm(gelu_exact(inner_rows), gain_vec, shift_vec)


def product(left_mat, right_mat):
    return jnp.dot(left_mat, right_mat, preferred_element_type=jnp.float32)


def product_tn(left_mat, right_mat):
    return lax.dot_general(
        left_mat, right_mat, (((0,), (0,)), ((), ())), preferred_element_type=jnp.float32
    )


def product_nt(left_mat, right_mat):
    return lax.dot_general(
        left_mat, right_mat, (((1,), (1,)), ((), ())), preferred_element_type=jnp.float32
    )


def group_cols(left_mat, dp_count, bal_count):
    row_count, width = left_mat.shape
    shaped = left_mat.reshape(row_count, dp_count, bal_count, width // (dp_count * bal_count))
    return shaped.transpose(0, 2, 1, 3).reshape(row_count, width)


def reduce_pair(first_term, second_term, bal_count):
    first_split = first_term.reshape(
        bal_count, first_term.shape[0] // bal_count, first_term.shape[1]
    )
    second_split = second_term.reshape(
        bal_count, second_term.shape[0] // bal_count, second_term.shape[1]
    )
    first_recv, second_recv = (
        lax.all_to_all(
            first_split.astype(jnp.bfloat16), "bal", split_axis=0, concat_axis=0, tiled=True
        ).astype(first_split.dtype),
        lax.all_to_all(
            second_split.astype(jnp.bfloat16), "bal", split_axis=0, concat_axis=0, tiled=True
        ).astype(second_split.dtype),
    )
    first_part = jnp.sum(first_recv, axis=0)
    second_part = jnp.sum(second_recv, axis=0)
    return (
        lax.psum_scatter(
            first_part.astype(jnp.bfloat16), "dp", scatter_dimension=0, tiled=True
        ).astype(jnp.float32),
        lax.psum_scatter(
            second_part.astype(jnp.bfloat16), "dp", scatter_dimension=0, tiled=True
        ).astype(jnp.float32),
    )


def split_heads(qkv_row):
    heads_view = qkv_row.reshape(qkv_row.shape[0], 3, HEADS, HDIM)
    return (heads_view[:, 0], heads_view[:, 1], heads_view[:, 2])


def masked_scores(queries, key_rows, seg_row):
    scores = jnp.einsum(
        "qhd,khd->hqk", queries, key_rows, preferred_element_type=jnp.float32
    ) * HDIM ** (-0.5)
    same_seg = seg_row[:, None] == seg_row[None, :]
    return jnp.where(same_seg[None], scores, MASK_FILL)


def attend_row(pieces):
    qkv_row, seg_row = pieces
    queries, key_rows, value_rows = split_heads(qkv_row)
    masked = masked_scores(queries, key_rows, seg_row)
    row_peak = jnp.max(masked, axis=-1, keepdims=True)
    exp_scores = jnp.exp(masked - row_peak)
    row_total = jnp.sum(exp_scores, axis=-1, keepdims=True)
    attn_probs = (exp_scores / row_total).astype(jnp.bfloat16)
    context = jnp.einsum("hqk,khd->qhd", attn_probs, value_rows, preferred_element_type=jnp.float32)
    log_total = (row_peak + jnp.log(row_total))[..., 0]
    return (context.reshape(qkv_row.shape[0], HEADS * HDIM).astype(jnp.bfloat16), log_total)


def attend_back(pieces):
    qkv_row, seg_row, log_total, dcontext = pieces
    queries, key_rows, value_rows = split_heads(qkv_row)
    masked = masked_scores(queries, key_rows, seg_row)
    attn_probs = jnp.exp(masked - log_total[..., None])
    dcontext = dcontext.reshape(qkv_row.shape[0], HEADS, HDIM)
    dprobs = jnp.einsum("qhd,khd->hqk", dcontext, value_rows, preferred_element_type=jnp.float32)
    dscores = attn_probs * (dprobs - jnp.sum(attn_probs * dprobs, axis=-1, keepdims=True))
    dscores = dscores.astype(jnp.bfloat16)
    score_scale = HDIM ** (-0.5)
    dqueries = (
        jnp.einsum("hqk,khd->qhd", dscores, key_rows, preferred_element_type=jnp.float32)
        * score_scale
    )
    dkey_rows = (
        jnp.einsum("hqk,qhd->khd", dscores, queries, preferred_element_type=jnp.float32)
        * score_scale
    )
    dvalues = jnp.einsum(
        "hqk,qhd->khd",
        attn_probs.astype(jnp.bfloat16),
        dcontext,
        preferred_element_type=jnp.float32,
    )
    joined = jnp.stack([dqueries, dkey_rows, dvalues], axis=1)
    return joined.reshape(qkv_row.shape[0], 3 * HEADS * HDIM).astype(jnp.bfloat16)


def per_device(
    tokens,
    segment_ids,
    mlm_labels,
    mask_order,
    mask_count,
    qkv_weight,
    query_bias,
    value_bias,
    out_weight,
    out_bias,
    attn_gain,
    attn_shift,
    up_weight,
    up_bias,
    down_weight,
    down_bias,
    ffn_gain,
    ffn_shift,
    head_weight,
    head_bias,
    head_gain,
    head_shift,
    decoder,
    decoder_bias,
):
    model_width = tokens.shape[1]
    tok_rows = tokens.shape[0]
    seqlen = segment_ids.shape[1]
    packed_rows = segment_ids.shape[0]
    bal_size = lax.axis_size("bal")
    dp_size = lax.axis_size("dp")
    bal_place = lax.axis_index("bal")
    device_count = dp_size * bal_size
    inv_count = 1.0 / (HEAD_DEV * device_count)
    gathered = (
        lax.all_gather(qkv_weight, ("dp", "bal"), axis=0, tiled=True),
        lax.all_gather(out_weight, ("dp", "bal"), axis=0, tiled=True),
        lax.all_gather(up_weight, ("dp", "bal"), axis=0, tiled=True),
        lax.all_gather(down_weight, ("dp", "bal"), axis=0, tiled=True),
        lax.all_gather(head_weight, ("dp", "bal"), axis=0, tiled=True),
    )
    qkv_full, out_full, up_full, down_full, head_full = gathered
    merged_bias = jnp.concatenate([query_bias, jnp.zeros_like(query_bias), value_bias])
    qkv_rows = (product(tokens, qkv_full) + merged_bias).astype(jnp.bfloat16)
    qkv_seqs = qkv_rows.reshape(packed_rows, seqlen, 3 * model_width)
    context, log_totals = lax.map(attend_row, (qkv_seqs, segment_ids))
    context = context.reshape(tok_rows, model_width)
    attn_sum = product(context, out_full) + out_bias
    resid_one = tokens.astype(jnp.float32) + attn_sum
    normed_one, norm_one_back = jax.vjp(layer_norm, resid_one, attn_gain, attn_shift)
    normed_one = normed_one.astype(jnp.bfloat16)
    up_rows = product(normed_one, up_full) + up_bias
    hidden, gelu_back = jax.vjp(gelu_exact, up_rows)
    hidden = hidden.astype(jnp.bfloat16)
    down_rows = product(hidden, down_full) + down_bias
    resid_two = normed_one.astype(jnp.float32) + down_rows
    output, norm_two_back = jax.vjp(layer_norm, resid_two, ffn_gain, ffn_shift)
    layer_out = output.astype(jnp.bfloat16)
    counts = lax.all_gather(mask_count, "bal", axis=0, tiled=True)
    starts = jnp.cumsum(counts) - counts
    peer_ids = jnp.arange(bal_size)
    offset = jnp.sum(jnp.where(peer_ids < bal_place, counts, 0))
    count_here = mask_count[0]
    per_peer = MASK_DEV // bal_size
    slot_steps = jnp.arange(per_peer)
    listed = mask_order[0, :MASK_DEV]
    listed_rows = jnp.take(layer_out, listed, axis=0)
    listed_ids = jnp.take(mlm_labels, listed)
    digit_pair = jnp.stack([listed_ids // 256, listed_ids % 256], axis=1).astype(jnp.bfloat16)
    first_out = (offset - peer_ids + bal_size - 1) // bal_size
    local_slot = peer_ids[:, None] + bal_size * (first_out[:, None] + slot_steps[None, :]) - offset
    send_valid = local_slot < count_here
    picked = jnp.clip(local_slot, 0, MASK_DEV - 1)
    send_rows = jnp.where(send_valid[..., None], listed_rows[picked], 0)
    send_digits = jnp.where(send_valid[..., None], digit_pair[picked], 0)
    recv_rows, recv_digits = (
        lax.all_to_all(send_rows, "bal", split_axis=0, concat_axis=0, tiled=True),
        lax.all_to_all(send_digits, "bal", split_axis=0, concat_axis=0, tiled=True),
    )
    head_slot = jnp.arange(HEAD_DEV)
    global_here = bal_place + bal_size * head_slot
    owner_mask = (global_here[None, :] >= starts[:, None]) & (
        global_here[None, :] < (starts + counts)[:, None]
    )
    first_in = (starts - bal_place + bal_size - 1) // bal_size
    src_slot = jnp.clip(head_slot[None, :] - first_in[:, None], 0, per_peer - 1)
    rows_pick = recv_rows[peer_ids[:, None], src_slot]
    head_in = jnp.sum(
        jnp.where(owner_mask[..., None], rows_pick.astype(jnp.float32), 0.0), axis=0
    ).astype(jnp.bfloat16)
    digits_pick = recv_digits[peer_ids[:, None], src_slot].astype(jnp.float32)
    digit_sum = jnp.sum(jnp.where(owner_mask[..., None], digits_pick, 0.0), axis=0)
    head_ids = (digit_sum[:, 0] * 256.0 + digit_sum[:, 1]).astype(jnp.int32)
    inner_rows = product(head_in, head_full) + head_bias
    head_normed, tail_back = jax.vjp(head_tail, inner_rows, head_gain, head_shift)
    head_normed = head_normed.astype(jnp.bfloat16)
    vocab_size = decoder.shape[1]
    logits = (
        product(head_normed, lax.all_gather(decoder, ("dp", "bal"), axis=0, tiled=True))
        + decoder_bias
    )
    row_peak = jnp.max(logits, axis=1, keepdims=True)
    exp_logits = jnp.exp(logits - row_peak)
    row_total = jnp.sum(exp_logits, axis=1, keepdims=True)
    log_total = row_peak[:, 0] + jnp.log(row_total[:, 0])
    vocab_ids = lax.broadcasted_iota(jnp.int32, logits.shape, 1)
    is_label = vocab_ids == head_ids[:, None]
    target = jnp.sum(jnp.where(is_label, logits, 0.0), axis=1)
    loss_part = jnp.sum(log_total - target)
    dlogits = ((exp_logits / row_total - is_label.astype(jnp.float32)) * inv_count).astype(
        jnp.bfloat16
    )
    decoder_bias_part = jnp.sum(dlogits, axis=0, dtype=jnp.float32)
    dhead_normed = product_nt(dlogits, lax.all_gather(decoder, ("dp", "bal"), axis=0, tiled=True))
    dinner_full, head_gain_part, head_shift_part = tail_back(dhead_normed)
    dinner = dinner_full.astype(jnp.bfloat16)
    head_term = product_tn(group_cols(head_in, dp_size, bal_size), dinner)
    head_bias_part = jnp.sum(dinner, axis=0, dtype=jnp.float32)
    dhead_in = product_nt(dinner, head_full).astype(jnp.bfloat16)
    back_slot = first_in[:, None] + slot_steps[None, :]
    back_global = bal_place + bal_size * back_slot
    back_valid = (back_global >= starts[:, None]) & (back_global < (starts + counts)[:, None])
    back_send = jnp.where(back_valid[..., None], dhead_in[jnp.clip(back_slot, 0, HEAD_DEV - 1)], 0)
    back_recv = lax.all_to_all(back_send, "bal", split_axis=0, concat_axis=0, tiled=True)
    own_global = offset + jnp.arange(MASK_DEV)
    own_dest = own_global % bal_size
    own_step = own_global // bal_size - first_out[own_dest]
    flat_index = jnp.clip(own_dest * per_peer + own_step, 0, MASK_DEV - 1)
    own_valid = jnp.arange(MASK_DEV) < count_here
    returned = jnp.where(
        own_valid[:, None], back_recv.reshape(MASK_DEV, model_width)[flat_index], 0
    )
    token_ids = jnp.arange(tok_rows)
    scatter_mat = (token_ids[:, None] == listed[None, :]).astype(jnp.bfloat16)
    dlayer_out = product(scatter_mat, returned)
    regathered = (
        lax.all_gather(qkv_weight, ("dp", "bal"), axis=0, tiled=True),
        lax.all_gather(out_weight, ("dp", "bal"), axis=0, tiled=True),
        lax.all_gather(up_weight, ("dp", "bal"), axis=0, tiled=True),
        lax.all_gather(down_weight, ("dp", "bal"), axis=0, tiled=True),
    )
    qkv_back, out_back, up_back, down_back = regathered
    dresid_two, ffn_gain_part, ffn_shift_part = norm_two_back(dlayer_out)
    ddown_rows = dresid_two.astype(jnp.bfloat16)
    down_term = product_tn(group_cols(hidden, dp_size, bal_size), ddown_rows)
    down_bias_part = jnp.sum(ddown_rows, axis=0, dtype=jnp.float32)
    dhidden = product_nt(ddown_rows, down_back)
    dup_rows = gelu_back(dhidden)[0].astype(jnp.bfloat16)
    up_term = product_tn(group_cols(normed_one, dp_size, bal_size), dup_rows)
    up_bias_part = jnp.sum(dup_rows, axis=0, dtype=jnp.float32)
    dnormed_one = dresid_two + product_nt(dup_rows, up_back)
    dresid_one, attn_gain_part, attn_shift_part = norm_one_back(dnormed_one)
    dattn_sum = dresid_one.astype(jnp.bfloat16)
    out_term = product_tn(group_cols(context, dp_size, bal_size), dattn_sum)
    out_bias_part = jnp.sum(dattn_sum, axis=0, dtype=jnp.float32)
    dcontext = product_nt(dattn_sum, out_back).astype(jnp.bfloat16)
    dqkv_rows = lax.map(
        attend_back,
        (qkv_seqs, segment_ids, log_totals, dcontext.reshape(packed_rows, seqlen, model_width)),
    )
    dqkv_rows = dqkv_rows.reshape(tok_rows, 3 * model_width)
    qkv_term = product_tn(group_cols(tokens, dp_size, bal_size), dqkv_rows)
    query_part = jnp.sum(dqkv_rows[:, :model_width], axis=0, dtype=jnp.float32)
    value_part = jnp.sum(dqkv_rows[:, 2 * model_width :], axis=0, dtype=jnp.float32)
    tokens_grad = dresid_one + product_nt(dqkv_rows, qkv_back)
    qkv_grad, up_grad = reduce_pair(qkv_term, up_term, bal_size)
    down_grad, out_grad = reduce_pair(down_term, out_term, bal_size)
    block_width = vocab_size // 3
    grouped_normed = group_cols(head_normed, dp_size, bal_size)
    block_terms = product_tn(grouped_normed, dlogits[:, 0:block_width])
    head_grad, first_block = reduce_pair(head_term, block_terms, bal_size)
    second_term = product_tn(grouped_normed, dlogits[:, block_width : 2 * block_width])
    third_term = product_tn(grouped_normed, dlogits[:, 2 * block_width :])
    second_block, third_block = reduce_pair(second_term, third_term, bal_size)
    decoder_grad = jnp.concatenate([first_block, second_block, third_block], axis=1)
    small_sums = lax.psum(
        (
            query_part,
            value_part,
            out_bias_part,
            attn_gain_part,
            attn_shift_part,
            up_bias_part,
            down_bias_part,
            ffn_gain_part,
            ffn_shift_part,
            head_bias_part,
            head_gain_part,
            head_shift_part,
            decoder_bias_part,
            loss_part,
        ),
        ("dp", "bal"),
    )
    return (
        layer_out,
        small_sums[13] * inv_count,
        tokens_grad,
        qkv_grad,
        small_sums[0],
        small_sums[1],
        out_grad,
        small_sums[2],
        small_sums[3],
        small_sums[4],
        up_grad,
        small_sums[5],
        down_grad,
        small_sums[6],
        small_sums[7],
        small_sums[8],
        head_grad,
        small_sums[9],
        small_sums[10],
        small_sums[11],
        decoder_grad,
        small_sums[12],
    )


def solution(mesh):
    placed = (
        P(("dp", "bal"), None),
        P(("dp", "bal"), None),
        P(("dp", "bal")),
        P(("dp", "bal"), None),
        P(("dp", "bal")),
        P(("dp", "bal"), None),
        P(),
        P(),
        P(("dp", "bal"), None),
        P(),
        P(),
        P(),
        P(("dp", "bal"), None),
        P(),
        P(("dp", "bal"), None),
        P(),
        P(),
        P(),
        P(("dp", "bal"), None),
        P(),
        P(),
        P(),
        P(("dp", "bal"), None),
        P(),
    )
    return jax.shard_map(
        per_device,
        mesh=mesh,
        in_specs=placed,
        out_specs=(
            P(("dp", "bal"), None),
            P(),
            P(("dp", "bal"), None),
            P(("dp", "bal"), None),
            P(),
            P(),
            P(("dp", "bal"), None),
            P(),
            P(),
            P(),
            P(("dp", "bal"), None),
            P(),
            P(("dp", "bal"), None),
            P(),
            P(),
            P(),
            P(("dp", "bal"), None),
            P(),
            P(),
            P(),
            P(("dp", "bal"), None),
            P(),
        ),
        check_vma=False,
    )
```

profile of v0, /device:TPU:0, one launch (start us, length us, event | category | flops | bytes accessed | tf_op | source)
XLA Modules:
  0.0 1790.3 jit_solution(13292351085531968582)
XLA Ops:
  13.8 6.3 all-reduce
  45.2 28.6 %all-gather.7.cloned.1.call-done = bf16[768,2304]{1,0:T(8,128)(2,1)} async-done(((bf16[24,2304]{1,0:T(8,128)(2,1)}), bf16[768,2304]{1,0:T(8,128)(2,1)}) %all-gather.7.cloned.1.call-update) | async-done | bytes 3538960 | tf_op jit(solution)/shard_map/all_gather | solution.py:170
  73.8 5.4 fusion.12
  89.4 4.3 fusion.19
  93.7 35.9 %all-gather.9.cloned.1.call-done = bf16[768,768]{1,0:T(8,128)(2,1)} async-done(((bf16[24,768]{1,0:T(8,128)(2,1)}), bf16[768,768]{1,0:T(8,128)(2,1)}) %all-gather.9.cloned.1.call-update) | async-done | bytes 1179664 | tf_op jit(solution)/shard_map/all_gather | solution.py:171
  133.0 62.1 %all-gather.11.cloned.1.call-done = bf16[768,3072]{1,0:T(8,128)(2,1)} async-done(((bf16[24,3072]{1,0:T(8,128)(2,1)}), bf16[768,3072]{1,0:T(8,128)(2,1)}) %all-gather.11.cloned.1.call-update) | async-done | bytes 4718608 | tf_op jit(solution)/shard_map/all_gather | solution.py:172
  195.1 19.0 %multiply_convert_fusion.1 = (bf16[512,3072]{1,0:T(8,128)(2,1)}, f32[512,3072]{1,0:T(8,128)}, f32[512,3072]{1,0:T(8,128)}) fusion(f32[3072]{0:T(1024)S(1)} %copy-done.68, bf16[512,768]{1,0:T(8,128)(2,1)S(1)} %add_convert_fusion.2, bf16[768,3072]{1,0:T(8,128)(2,1)} %all-gather.11.cloned.1.call-done), kind=kOutput, calls=%fused_computation.26 | convolution fusion | flops 2519728128 | bytes 21245952 | tf_op jit(solution)/shard_map/dot_general | solution.py:32
  214.1 46.2 %all-gather.13.cloned.1.call-done = bf16[3072,768]{1,0:T(8,128)(2,1)} async-done(((bf16[96,768]{1,0:T(8,128)(2,1)}), bf16[3072,768]{1,0:T(8,128)(2,1)}) %all-gather.13.cloned.1.call-update) | async-done | bytes 4718608 | tf_op jit(solution)/shard_map/all_gather | solution.py:173
  260.4 6.2 fusion.74
  291.9 24.1 %all-gather.15.cloned.1.call-done = bf16[768,768]{1,0:T(8,128)(2,1)} async-done(((bf16[24,768]{1,0:T(8,128)(2,1)}), bf16[768,768]{1,0:T(8,128)(2,1)}) %all-gather.15.cloned.1.call-update) | async-done | bytes 1179664 | tf_op jit(solution)/shard_map/all_gather | solution.py:174
  319.4 257.7 %all-gather.17.cloned.1.call-done = bf16[768,30522]{1,0:T(8,128)(2,1)} async-done(((bf16[24,30522]{1,0:T(8,128)(2,1)}), bf16[768,30522]{1,0:T(8,128)(2,1)}) %all-gather.17.cloned.1.call-update) | async-done | bytes 46881808 | tf_op jit(solution)/shard_map/all_gather | solution.py:233
  577.1 20.6 %fusion.75 = (f32[32]{0:T(128)S(1)}, f32[32,30522]{1,0:T(8,128)}) fusion(f32[30522]{0:T(1024)} %param.47, bf16[32,768]{1,0:T(8,128)(2,1)} %add_convert_fusion.6, bf16[768,30522]{1,0:T(8,128)(2,1)} %all-gather.17.cloned.1.call-done), kind=kOutput, calls=%fused_computation.228 | convolution fusion | flops 1502170624 | bytes 50959976 | tf_op jit(solution)/shard_map/dot_general | solution.py:32
  597.8 3.9 fusion.14
  603.8 21.3 %fusion.66 = (f32[768]{0:T(1024)}, f32[32]{0:T(128)S(1)}, f32[32,768]{1,0:T(8,128)}) fusion(f32[768]{0:T(1024)S(1)} %copy-done.31, f32[32,768]{1,0:T(8,128)S(1)} %get-tuple-element.99, f32[32]{0:T(128)S(1)} %broadcast_multiply_fusion.2, bf16[32,30522]{1,0:T(8,128)(2,1)S(1)} %get-tuple-element.83, bf16[768,30522]{1,0:T(8,128)(2,1)} %all-gather.17.cloned.1.call-done), kind=kOutput, calls=%fused_computation.221 | convolution fusion | flops 1500339456 | bytes 49038208 | tf_op jit(solution)/shard_map/dot_general | solution.py:42
  640.1 4.7 all-to-all-start.7
  650.0 9.4 convert_reduce_fusion
  669.4 11.3 multiply_reduce_fusion
  682.0 6.9 multiply_convert_fusion
  693.8 3.9 fusion.16
  701.2 4.0 multiply_bitcast_fusion.1
  706.9 3.8 convolution_convert_fusion.4
  710.7 6.2 all-to-all-done.4
  725.4 6.1 convolution_convert_fusion.3
  731.5 31.5 %all-to-all-done.3 = bf16[4,192,2304]{2,1,0:T(8,128)(2,1)S(1)} async-done(((bf16[4,192,2304]{2,1,0:T(8,128)(2,1)}), bf16[4,192,2304]{2,1,0:T(8,128)(2,1)S(1)}, u32[]{:S(2)}, u32[]{:S(2)}) %all-to-all-start.3) | async-done | bytes 3538976 | tf_op jit(solution)/shard_map/all_to_all | solution.py:61
  764.7 5.0 all-to-all-start.5
  774.1 4.2 convolution_convert_fusion.5
  778.3 45.3 %all-to-all-done.5 = bf16[4,192,3072]{2,1,0:T(8,128)(2,1)} async-done(((bf16[4,192,3072]{2,1,0:T(8,128)(2,1)}), bf16[4,192,3072]{2,1,0:T(8,128)(2,1)}, u32[]{:S(2)}, u32[]{:S(2)}) %all-to-all-start.5) | async-done | bytes 4718624 | tf_op jit(solution)/shard_map/all_to_all | solution.py:64
  823.6 4.9 all-to-all-start.6
  829.4 7.8 convolution_convert_fusion.2
  837.2 45.2 %all-to-all-done.6 = bf16[4,768,768]{2,1,0:T(8,128)(2,1)} async-done(((bf16[4,768,768]{2,1,0:T(8,128)(2,1)}), bf16[4,768,768]{2,1,0:T(8,128)(2,1)}, u32[]{:S(2)}, u32[]{:S(2)}) %all-to-all-start.6) | async-done | bytes 4718624 | tf_op jit(solution)/shard_map/all_to_all | solution.py:61
  882.4 7.0 all-to-all-start.8
  889.4 7.7 convolution_convert_fusion.1
  897.1 164.1 %all-to-all-done.8 = bf16[4,192,10174]{2,1,0:T(8,128)(2,1)} async-done(((bf16[4,192,10174]{2,1,0:T(8,128)(2,1)}), bf16[4,192,10174]{2,1,0:T(8,128)(2,1)}, u32[]{:S(2)}, u32[]{:S(2)}) %all-to-all-start.8) | async-done | bytes 15627296 | tf_op jit(solution)/shard_map/all_to_all | solution.py:64
  1061.2 6.8 all-to-all-start.9
  1075.2 4.6 reduce_sum.470
  1079.9 4.4 reduce_sum.472
  1084.4 11.5 reduce_sum.480
  1095.9 7.8 convolution_convert_fusion
  1103.7 136.2 %all-to-all-done.9 = bf16[4,192,10174]{2,1,0:T(8,128)(2,1)} async-done(((bf16[4,192,10174]{2,1,0:T(8,128)(2,1)}), bf16[4,192,10174]{2,1,0:T(8,128)(2,1)}, u32[]{:S(2)}, u32[]{:S(2)}) %all-to-all-start.9) | async-done | bytes 15627296 | tf_op jit(solution)/shard_map/all_to_all | solution.py:61
  1239.9 6.8 all-to-all-start.10
  1246.8 11.5 reduce_sum.481
  1258.6 159.9 %all-to-all-done.10 = bf16[4,192,10174]{2,1,0:T(8,128)(2,1)} async-done(((bf16[4,192,10174]{2,1,0:T(8,128)(2,1)}), bf16[4,192,10174]{2,1,0:T(8,128)(2,1)}, u32[]{:S(2)}, u32[]{:S(2)}) %all-to-all-start.10) | async-done | bytes 15627296 | tf_op jit(solution)/shard_map/all_to_all | solution.py:64
  1418.5 11.5 reduce_sum.482
  1431.8 5.9 add_add_fusion.4
  1438.1 41.6 %all-reduce.1 = (f32[]{:T(128)}, f32[768]{0:T(1024)}, f32[768]{0:T(1024)}, f32[768]{0:T(1024)}, f32[768]{0:T(1024)}, /*index=5*/f32[768]{0:T(1024)}, f32[3072]{0...) all-reduce(f32[]{:T(128)} %subtract_reduce_fusion, ...), channel_id=1, replica_groups=mesh['dp'=8,'bal'=4] {'dp','bal'}, use_global_device_ids=true, to_apply=%region_16.17 | all-reduce | flops 11521 | bytes 92168 | tf_op jit(solution)/shard_map/psum | solution.py:310
  1488.1 77.0 %reduce-scatter.21.cloned.1.call-done = bf16[24,10174]{1,0:T(8,128)(2,1)} async-done(((bf16[192,10174]{1,0:T(8,128)(2,1)}), bf16[24,10174]{1,0:T(8,128)(2,1)}) %reduce-scatter.21.cloned.1.call-update) | async-done | bytes 488368 | tf_op jit(solution)/shard_map/reduce_scatter | solution.py:71
  1565.1 87.6 %reduce-scatter.23.cloned.1.call-done = bf16[24,10174]{1,0:T(8,128)(2,1)} async-done(((bf16[192,10174]{1,0:T(8,128)(2,1)}), bf16[24,10174]{1,0:T(8,128)(2,1)}) %reduce-scatter.23.cloned.1.call-update) | async-done | bytes 488368 | tf_op jit(solution)/shard_map/reduce_scatter | solution.py:74
  1657.2 123.4 %all-reduce.4.cloned.1.call-done = f32[30522]{0:T(1024)} async-done(((f32[30522]{0:T(1024)}), f32[30522]{0:T(1024)}) %all-reduce.4.cloned.1.call-update) | async-done | bytes 122104 | tf_op jit(solution)/shard_map/psum | solution.py:310
  (319 shorter events, 155.2 us)
Async XLA Ops:
  7.2 66.6 %copy-start.19 = (bf16[512,768]{1,0:T(8,128)(2,1)S(1)}, bf16[512,768]{1,0:T(8,128)(2,1)}, u32[]{:S(2)}) copy-start(bf16[512,768]{1,0:T(8,128)(2,1)} %param.24) | copy-start | bytes 2359300
  7.2 66.6 %all-gather.7.cloned.1.call-start = ((), (), s32[]{:S(2)}) async-start(), calls=%async_computation.19 | async-start | bytes 3649536 | tf_op jit(solution)/shard_map/all_gather | solution.py:170
  8.0 121.6 %all-gather.9.cloned.1.call-start = ((), (), s32[]{:S(2)}) async-start(), calls=%async_computation.20 | async-start | bytes 1216512 | tf_op jit(solution)/shard_map/all_gather | solution.py:171
  8.7 186.4 %all-gather.11.cloned.1.call-start = ((), (), s32[]{:S(2)}) async-start(), calls=%async_computation.21 | async-start | bytes 4866048 | tf_op jit(solution)/shard_map/all_gather | solution.py:172
  9.4 250.9 %all-gather.13.cloned.1.call-start = ((), (), s32[]{:S(2)}) async-start(), calls=%async_computation.22 | async-start | bytes 4866048 | tf_op jit(solution)/shard_map/all_gather | solution.py:173
  10.0 306.0 %all-gather.15.cloned.1.call-start = ((), (), s32[]{:S(2)}) async-start(), calls=%async_computation.23 | async-start | bytes 1216512 | tf_op jit(solution)/shard_map/all_gather | solution.py:174
  10.6 566.5 %all-gather.17.cloned.1.call-start = ((), (), s32[]{:S(2)}) async-start(), calls=%async_computation.24 | async-start | bytes 48457728 | tf_op jit(solution)/shard_map/all_gather | solution.py:233
  27.4 15.8 all-to-all-start.1
  39.8 34.1 %copy-start.55 = (pred[4,32]{1,0:T(4,128)(4,1)}, pred[4,32]{1,0:T(4,128)(4,1)S(1)}, u32[]{:S(2)}) copy-start(pred[4,32]{1,0:T(4,128)(4,1)S(1)} %compare_and_fusion.1) | copy-start | bytes 388
  89.4 40.2 %copy-start.70 = (f32[768]{0:T(1024)S(1)}, f32[768]{0:T(1024)}, u32[]{:S(2)}) copy-start(f32[768]{0:T(1024)} %param.33) | copy-start | bytes 9220
  93.7 38.9 %copy-start.48 = (f32[768]{0:T(1024)S(1)}, f32[768]{0:T(1024)}, u32[]{:S(2)}) copy-start(f32[768]{0:T(1024)} %param.34) | copy-start | bytes 9220
  93.7 38.9 %copy-start.60 = (f32[768]{0:T(1024)S(1)}, f32[768]{0:T(1024)}, u32[]{:S(2)}) copy-start(f32[768]{0:T(1024)} %param.35) | copy-start | bytes 9220
  129.6 65.5 %copy-start.68 = (f32[3072]{0:T(1024)S(1)}, f32[3072]{0:T(1024)}, u32[]{:S(2)}) copy-start(f32[3072]{0:T(1024)} %param.37) | copy-start | bytes 36868
  132.6 81.5 %copy-start.37 = (f32[512]{0:T(512)}, f32[512]{0:T(512)S(1)}, u32[]{:S(2)}) copy-start(f32[512]{0:T(512)S(1)} %multiply_reduce_fusion.6) | copy-start | bytes 6148
  132.6 81.5 %copy-start.35 = (f32[512]{0:T(512)}, f32[512]{0:T(512)S(1)}, u32[]{:S(2)}) copy-start(f32[512]{0:T(512)S(1)} %fusion.51) | copy-start | bytes 6148
  133.0 81.1 %copy-start.15 = (bf16[512,768]{1,0:T(8,128)(2,1)}, bf16[512,768]{1,0:T(8,128)(2,1)S(1)}, u32[]{:S(2)}) copy-start(bf16[512,768]{1,0:T(8,128)(2,1)S(1)} %add_convert_fusion.2) | copy-start | bytes 2359300
  276.1 7.8 all-to-all-start
  280.9 37.7 %copy-start.31 = (f32[768]{0:T(1024)S(1)}, f32[768]{0:T(1024)}, u32[]{:S(2)}) copy-start(f32[768]{0:T(1024)} %param.44) | copy-start | bytes 9220
  281.0 37.7 %copy-start.64 = (f32[768]{0:T(1024)S(1)}, f32[768]{0:T(1024)}, u32[]{:S(2)}) copy-start(f32[768]{0:T(1024)} %param.45) | copy-start | bytes 9220
  319.4 278.4 %copy-start.57 = (s32[32]{0:T(128)S(1)}, s32[32]{0:T(128)}, u32[]{:S(2)}) copy-start(s32[32]{0:T(128)} %fusion.44) | copy-start | bytes 388
  601.6 23.4 %copy-start.58 = (f32[32]{0:T(128)}, f32[32]{0:T(128)S(1)}, u32[]{:S(2)}) copy-start(f32[32]{0:T(128)S(1)} %get-tuple-element.55) | copy-start | bytes 388
  603.8 21.3 %copy-start.5 = (bf16[32,30522]{1,0:T(8,128)(2,1)}, bf16[32,30522]{1,0:T(8,128)(2,1)S(1)}, u32[]{:S(2)}) copy-start(bf16[32,30522]{1,0:T(8,128)(2,1)S(1)} %get-tuple-element.83) | copy-start | bytes 5860228
  603.8 25.2 %copy-start.17 = (bf16[768,768]{1,0:T(8,128)(2,1)S(1)}, bf16[768,768]{1,0:T(8,128)(2,1)}, u32[]{:S(2)}) copy-start(bf16[768,768]{1,0:T(8,128)(2,1)} %all-gather.15.cloned.1.call-done) | copy-start | bytes 3538948
  603.8 25.7 %copy-start.51 = (s32[1024]{0:T(1024)S(1)}, s32[1024]{0:T(1024)}, u32[]{:S(2)}) copy-start(s32[1024]{0:T(1024)} %pad_clamp_fusion.1) | copy-start | bytes 12292
  603.8 27.1 %copy-start.65 = (pred[4,16]{1,0:T(4,128)(4,1)S(1)}, pred[4,16]{1,0:T(4,128)(4,1)}, u32[]{:S(2)}) copy-start(pred[4,16]{1,0:T(4,128)(4,1)} %get-tuple-element.126) | copy-start | bytes 196
  625.1 21.2 %copy-start.34 = (f32[512]{0:T(512)S(1)}, f32[512]{0:T(512)}, u32[]{:S(2)}) copy-start(f32[512]{0:T(512)} %copy-done.33) | copy-start | bytes 6148
  632.5 7.6 all-to-all-start.2
  640.1 57.6 %all-to-all-start.7 = ((bf16[4,192,768]{2,1,0:T(8,128)(2,1)}), bf16[4,192,768]{2,1,0:T(8,128)(2,1)}, u32[]{:S(2)}, u32[]{:S(2)}) async-start(bf16[4,192,768]{2,1,0:T(8,128)(2,1)} %convolution_convert_fusion.7), calls=%async_computation.11 | async-start | bytes 2359296 | tf_op jit(solution)/shard_map/all_to_all | solution.py:61
  697.6 19.4 %all-to-all-start.4 = ((bf16[4,192,768]{2,1,0:T(8,128)(2,1)}), bf16[4,192,768]{2,1,0:T(8,128)(2,1)S(1)}, u32[]{:S(2)}, u32[]{:S(2)}) async-start(bf16[4,192,768]{2,1,0:T(8,128)(2,1)} %convolution_convert_fusion.6), calls=%async_computation.5 | async-start | bytes 2359296 | tf_op jit(solution)/shard_map/all_to_all | solution.py:64
  718.1 44.9 %all-to-all-start.3 = ((bf16[4,192,2304]{2,1,0:T(8,128)(2,1)}), bf16[4,192,2304]{2,1,0:T(8,128)(2,1)S(1)}, u32[]{:S(2)}, u32[]{:S(2)}) async-start(bf16[4,192,2304]{2,1,0:T(8,128)(2,1)} %bitcast.191), calls=%async_computation.3 | async-start | bytes 7077888 | tf_op jit(solution)/shard_map/all_to_all | solution.py:61
  764.7 58.8 %all-to-all-start.5 = ((bf16[4,192,3072]{2,1,0:T(8,128)(2,1)}), bf16[4,192,3072]{2,1,0:T(8,128)(2,1)}, u32[]{:S(2)}, u32[]{:S(2)}) async-start(bf16[4,192,3072]{2,1,0:T(8,128)(2,1)} %convolution_convert_fusion.3), calls=%async_computation.7 | async-start | bytes 9437184 | tf_op jit(solution)/shard_map/all_to_all | solution.py:64
  778.3 50.3 %copy-start.27 = (bf16[32,768]{1,0:T(8,128)(2,1)S(1)}, bf16[32,768]{1,0:T(8,128)(2,1)}, u32[]{:S(2)}) copy-start(bf16[32,768]{1,0:T(8,128)(2,1)} %add_convert_fusion.6) | copy-start | bytes 147460
  778.3 51.2 %copy-start.6 = (bf16[32,30522]{1,0:T(8,128)(2,1)S(1)}, bf16[32,30522]{1,0:T(8,128)(2,1)}, u32[]{:S(2)}) copy-start(bf16[32,30522]{1,0:T(8,128)(2,1)} %copy-done.5) | copy-start | bytes 5860228
  823.6 58.8 %all-to-all-start.6 = ((bf16[4,768,768]{2,1,0:T(8,128)(2,1)}), bf16[4,768,768]{2,1,0:T(8,128)(2,1)}, u32[]{:S(2)}, u32[]{:S(2)}) async-start(bf16[4,768,768]{2,1,0:T(8,128)(2,1)} %convolution_convert_fusion.5), calls=%async_computation.9 | async-start | bytes 9437184 | tf_op jit(solution)/shard_map/all_to_all | solution.py:61
  882.4 178.8 %all-to-all-start.8 = ((bf16[4,192,10174]{2,1,0:T(8,128)(2,1)}), bf16[4,192,10174]{2,1,0:T(8,128)(2,1)}, u32[]{:S(2)}, u32[]{:S(2)}) async-start(bf16[4,192,10174]{2,1,0:T(8,128)(2,1)} %convolution_convert_fusion.2), calls=%async_computation.13 | async-start | bytes 31457280 | tf_op jit(solution)/shard_map/all_to_all | solution.py:64
  897.1 173.3 %copy-start.14 = (bf16[4,192,768]{2,1,0:T(8,128)(2,1)S(1)}, bf16[4,192,768]{2,1,0:T(8,128)(2,1)}, u32[]{:S(2)}) copy-start(bf16[4,192,768]{2,1,0:T(8,128)(2,1)} %copy-done.13) | copy-start | bytes 3538948
  1061.2 178.6 %all-to-all-start.9 = ((bf16[4,192,10174]{2,1,0:T(8,128)(2,1)}), bf16[4,192,10174]{2,1,0:T(8,128)(2,1)}, u32[]{:S(2)}, u32[]{:S(2)}) async-start(bf16[4,192,10174]{2,1,0:T(8,128)(2,1)} %convolution_convert_fusion.1), calls=%async_computation.15 | async-start | bytes 31457280 | tf_op jit(solution)/shard_map/all_to_all | solution.py:61
  1068.0 412.3 %reduce-scatter.17.cloned.1.call-start = ((), (), s32[]{:S(2)}) async-start(), calls=%async_computation.29 | async-start | bytes 331776 | tf_op jit(solution)/shard_map/reduce_scatter | solution.py:71
  1070.3 411.4 %reduce-scatter.11.cloned.1.call-start = ((), (), s32[]{:S(2)}) async-start(), calls=%async_computation.26 | async-start | bytes 331776 | tf_op jit(solution)/shard_map/reduce_scatter | solution.py:74
  1071.4 411.8 %reduce-scatter.9.cloned.1.call-start = ((), (), s32[]{:S(2)}) async-start(), calls=%async_computation.25 | async-start | bytes 995328 | tf_op jit(solution)/shard_map/reduce_scatter | solution.py:71
  1075.2 409.6 %reduce-scatter.13.cloned.1.call-start = ((), (), s32[]{:S(2)}) async-start(), calls=%async_computation.27 | async-start | bytes 1327104 | tf_op jit(solution)/shard_map/reduce_scatter | solution.py:74
  1079.8 406.6 %reduce-scatter.15.cloned.1.call-start = ((), (), s32[]{:S(2)}) async-start(), calls=%async_computation.28 | async-start | bytes 1327104 | tf_op jit(solution)/shard_map/reduce_scatter | solution.py:71
  1084.4 403.7 %reduce-scatter.19.cloned.1.call-start = ((), (), s32[]{:S(2)}) async-start(), calls=%async_computation.30 | async-start | bytes 4423680 | tf_op jit(solution)/shard_map/reduce_scatter | solution.py:74
  1239.9 178.7 %all-to-all-start.10 = ((bf16[4,192,10174]{2,1,0:T(8,128)(2,1)}), bf16[4,192,10174]{2,1,0:T(8,128)(2,1)}, u32[]{:S(2)}, u32[]{:S(2)}) async-start(bf16[4,192,10174]{2,1,0:T(8,128)(2,1)} %convolution_convert_fusion), calls=%async_computation.17 | async-start | bytes 31457280 | tf_op jit(solution)/shard_map/all_to_all | solution.py:64
  1246.7 318.4 %reduce-scatter.21.cloned.1.call-start = ((), (), s32[]{:S(2)}) async-start(), calls=%async_computation.31 | async-start | bytes 4423680 | tf_op jit(solution)/shard_map/reduce_scatter | solution.py:71
  1258.3 394.4 %reduce-scatter.23.cloned.1.call-start = ((), (), s32[]{:S(2)}) async-start(), calls=%async_computation.32 | async-start | bytes 4423680 | tf_op jit(solution)/shard_map/reduce_scatter | solution.py:74
  1430.0 350.6 %all-reduce.4.cloned.1.call-start = ((), (), s32[]{:S(2)}) async-start(), calls=%async_computation.33 | async-start | bytes 245760 | tf_op jit(solution)/shard_map/psum | solution.py:310
  1486.4 295.7 %copy-start.1 = (s32[512]{0:T(512)S(1)}, s32[512]{0:T(512)}, u32[]{:S(2)}) copy-start(s32[512]{0:T(512)} %param.26) | copy-start | bytes 6148
  (55 other events, 280.1 us)
Sparse Core Ops, SparseCore 0:
  11.0 62.8 all-gather.6
  76.7 52.8 all-gather.8
  132.5 62.5 all-gather.10
  197.9 62.4 all-gather.12
  263.1 52.8 all-gather.14
  318.8 258.3 all-gather.16
  1072.7 58.3 reduce-scatter.16
  1135.0 57.6 reduce-scatter.10
  1196.1 60.2 reduce-scatter.8
  1259.7 62.9 reduce-scatter.12
  1326.1 62.9 reduce-scatter.14
  1392.6 84.3 reduce-scatter.18
  1481.1 83.9 reduce-scatter.20
  1568.7 83.9 reduce-scatter.22
  1659.6 120.9 all-reduce.3
where the time goes:
time: 1800 us; the launch traced here: 1790 us
  waiting for transfers between devices  1340 us (74%)
  matrix products  171 us (10%)
  other arithmetic  106 us (6%)
  local copies, waits for them, and re-layouts  56.7 us (3%)
  starting transfers between devices  53.5 us (3%)
  blocking collectives  48 us (3%)
    all_to_all x4, waiting for transfers between devices, reduce_pair(): lax.all_to_all(second_split.astype(jnp.bfloat16), 'bal', split_axis=0, co...  376 us
    all_gather x1, waiting for transfers between devices, per_device(): lax.all_gather(decoder, ('dp', 'bal'), axis=0, tiled=True)  258 us
    all_to_all x4, waiting for transfers between devices, reduce_pair(): lax.all_to_all(first_split.astype(jnp.bfloat16), 'bal', split_axis=0, con...  213 us
    psum x1, waiting for transfers between devices, per_device(): lax.psum((query_part, value_part, out_bias_part, attn_gain_part, attn_shi...  123 us
    reduce_scatter x4, waiting for transfers between devices, reduce_pair(): lax.psum_scatter(second_part.astype(jnp.bfloat16), 'dp', scatter_dimensio...  87.6 us
    reduce_scatter x4, waiting for transfers between devices, reduce_pair(): lax.psum_scatter(first_part.astype(jnp.bfloat16), 'dp', scatter_dimension...  77 us
    all_gather x1, waiting for transfers between devices, per_device(): lax.all_gather(up_weight, ('dp', 'bal'), axis=0, tiled=True)  62.1 us
    dot_general x7, matrix products, product(): return jnp.dot(left_mat, right_mat, preferred_element_type=jnp.float32)  58.6 us
  transfers between devices with their start and end apart: 26, of which 18 were waited for; matrix products, arithmetic and copies ran while one was open for 15% of the time, Pallas kernels for 0%

commit v1 on v0

v1 whole, which is shorter than its diff:
```python
import jax
import jax.numpy as jnp
from jax import lax
from jax.sharding import PartitionSpec as P

HEADS = 12
HDIM = 64
HEAD_DEV = 32
MASK_DEV = 64


EPSILON = 1e-06
MASK_FILL = -1e30
AXES = ("dp", "bal")
LOW = jnp.bfloat16


def gelu_exact(values):
    return jax.nn.gelu(values, approximate=False)


def product(left_mat, right_mat):
    return jnp.dot(left_mat, right_mat, preferred_element_type=jnp.float32)


def product_tn(left_mat, right_mat):
    return lax.dot_general(
        left_mat, right_mat, (((0,), (0,)), ((), ())), preferred_element_type=jnp.float32
    )


def product_nt(left_mat, right_mat):
    return lax.dot_general(
        left_mat, right_mat, (((1,), (1,)), ((), ())), preferred_element_type=jnp.float32
    )


def pick_exact(onehot, rows):
    return jnp.dot(onehot, rows, precision=lax.Precision.HIGHEST)


def norm_parts(hidden):
    average = jnp.mean(hidden, axis=-1, keepdims=True)
    centered = hidden - average
    inv_std = lax.rsqrt(jnp.mean(centered * centered, axis=-1, keepdims=True) + EPSILON)
    return centered * inv_std, inv_std


def norm_back(normal, inv_std, gain_vec, grad):
    scaled = grad * gain_vec
    first = jnp.mean(scaled, axis=-1, keepdims=True)
    second = jnp.mean(scaled * normal, axis=-1, keepdims=True)
    return (
        inv_std * (scaled - first - normal * second),
        jnp.sum(grad * normal, axis=0),
        jnp.sum(grad, axis=0),
    )


class Grid:
    def __init__(self, dp_size, bal_size):
        self.high = 4 if dp_size % 4 == 0 else 1
        self.low = dp_size // self.high
        self.wide = bal_size // 2
        self.sizes = (self.high, self.low, self.wide, 2)
        self.count = dp_size * bal_size
        dp_place, bal_place = lax.axis_index("dp"), lax.axis_index("bal")
        self.place = (
            dp_place // self.low,
            dp_place % self.low,
            bal_place // 2,
            bal_place % 2,
        )
        self.crossed = self.low == self.wide

    def index(self, spot):
        high, low, wide, core = spot
        return ((high * self.low + low) * self.wide + wide) * 2 + core

    def spots(self):
        for high in range(self.high):
            for low in range(self.low):
                for wide in range(self.wide):
                    for core in range(2):
                        yield (high, low, wide, core)

    def shift(self, value, axis_of, step):
        pairs = []
        for spot in self.spots():
            axis = axis_of[spot[3]]
            target = list(spot)
            target[axis] = (spot[axis] + step) % self.sizes[axis]
            pairs.append((self.index(spot), self.index(target)))
        return lax.ppermute(value, AXES, pairs)

    def own(self, axis_of):
        first, second = self.place[axis_of[0]], self.place[axis_of[1]]
        return first if axis_of[0] == axis_of[1] else jnp.where(self.place[3] == 0, first, second)

    def orders(self):
        return ((1, 2), (2, 1)) if self.crossed else ((1, 1), (2, 2))

    def gather_stage(self, value, axis_of):
        size = self.sizes[axis_of[0]]
        me = self.own(axis_of)
        parts = [value] + [self.shift(value, axis_of, step) for step in range(1, size)]
        rel = (me - jnp.arange(size)) % size
        rel = rel.reshape((size,) + (1,) * value.ndim)
        out = parts[-1][None]
        for step in range(size - 2, -1, -1):
            out = jnp.where(rel == step, parts[step][None], out)
        return out

    def scatter_stage(self, value, axis_of, axis):
        size = self.sizes[axis_of[0]]
        me = self.own(axis_of)

        def piece(step):
            return lax.dynamic_index_in_dim(value, (me + step) % size, axis, keepdims=False)

        total = piece(0).astype(jnp.float32)
        for step in range(1, size):
            total = total + self.shift(piece(step), axis_of, step).astype(jnp.float32)
        return total.astype(value.dtype)

    def gather(self, rows):
        height, width = rows.shape
        half = width // 2
        core = self.place[3]
        keep = lax.dynamic_slice_in_dim(rows, core * half, half, 1)
        give = lax.dynamic_slice_in_dim(rows, (1 - core) * half, half, 1)
        taken = self.shift(give, (3, 3), 1)
        is_own = (jnp.arange(2) == core)[:, None, None]
        part = jnp.where(is_own, keep[None], taken[None])
        part = self.gather_stage(part, (0, 0))
        first, second = self.orders()
        part = self.gather_stage(part, first)
        part = self.gather_stage(part, second)
        straight = part.transpose(2, 1, 0, 3, 4, 5)
        if self.crossed:
            turned = part.transpose(2, 0, 1, 3, 4, 5)
            straight = jnp.where(core == 0, straight, turned)
        mine = straight.reshape(self.count * height, half)
        other = self.shift(mine, (3, 3), 1)
        return jnp.concatenate(
            [jnp.where(core == 0, mine, other), jnp.where(core == 0, other, mine)], axis=1
        )

    def scatter(self, terms):
        total_rows, width = terms.shape
        height = total_rows // self.count
        half = width // 2
        core = self.place[3]
        keep = lax.dynamic_slice_in_dim(terms, core * half, half, 1)
        give = lax.dynamic_slice_in_dim(terms, (1 - core) * half, half, 1)
        taken = self.shift(give, (3, 3), 1)
        part = (keep.astype(jnp.float32) + taken.astype(jnp.float32)).astype(terms.dtype)
        part = part.reshape(self.high, self.low, self.wide, 2, height, half)
        first, second = self.orders()
        if self.crossed:
            part = jnp.where(core == 0, part, part.transpose(0, 2, 1, 3, 4, 5))
        part = self.scatter_stage(part, second, 2)
        part = self.scatter_stage(part, first, 1)
        part = self.scatter_stage(part, (0, 0), 0)
        mine = lax.dynamic_index_in_dim(part, core, 0, keepdims=False)
        away = lax.dynamic_index_in_dim(part, 1 - core, 0, keepdims=False)
        other = self.shift(away, (3, 3), 1)
        return jnp.concatenate(
            [jnp.where(core == 0, mine, other), jnp.where(core == 0, other, mine)], axis=1
        )

    def gather_group(self, rows):
        part = self.gather_stage(rows, (2, 2))
        part = self.gather_stage(part, (3, 3))
        part = part.transpose(1, 0, 2, 3)
        return part.reshape(self.wide * 2 * rows.shape[0], rows.shape[1])

    def total(self, value):
        for axis in (3, 2, 1, 0):
            size = self.sizes[axis]
            moved = [self.shift(value, (axis, axis), step) for step in range(1, size)]
            for piece in moved:
                value = value + piece
        return value


def heads_of(rows):
    return rows.reshape(rows.shape[0], HEADS, HDIM)


def attention_probs(queries, key_rows, query_seg, key_seg):
    scores = jnp.einsum(
        "qhd,khd->hqk", queries, key_rows, preferred_element_type=jnp.float32
    ) * HDIM ** (-0.5)
    same_seg = query_seg[:, None] == key_seg[None, :]
    masked = jnp.where(same_seg[None], scores, MASK_FILL)
    row_peak = jnp.max(masked, axis=-1, keepdims=True)
    exp_scores = jnp.exp(masked - row_peak)
    return exp_scores / jnp.sum(exp_scores, axis=-1, keepdims=True)


def per_device(
    tokens,
    segment_ids,
    mlm_labels,
    mask_order,
    mask_count,
    qkv_weight,
    query_bias,
    value_bias,
    out_weight,
    out_bias,
    attn_gain,
    attn_shift,
    up_weight,
    up_bias,
    down_weight,
    down_bias,
    ffn_gain,
    ffn_shift,
    head_weight,
    head_bias,
    head_gain,
    head_shift,
    decoder,
    decoder_bias,
):
    model_width = tokens.shape[1]
    tok_rows = tokens.shape[0]
    vocab_size = decoder.shape[1]
    bal_size = lax.axis_size("bal")
    dp_size = lax.axis_size("dp")
    bal_place = lax.axis_index("bal")
    dp_place = lax.axis_index("dp")
    grid = Grid(dp_size, bal_size)
    device_count = dp_size * bal_size
    my_place = dp_place * bal_size + bal_place
    group_slots = HEAD_DEV * bal_size
    slot_count = HEAD_DEV * device_count
    inv_count = 1.0 / slot_count
    part_vocab = -(-(-(-vocab_size // device_count)) // 128) * 128
    seg_row = segment_ids[0]

    listed = mask_order[0, :MASK_DEV]
    pick_mat = listed[:, None] == jnp.arange(tok_rows)[None, :]
    listed_ids = jnp.sum(jnp.where(pick_mat, mlm_labels[None, :], 0), axis=1)
    listed_seg = jnp.sum(jnp.where(pick_mat, seg_row[None, :], 0), axis=1)
    info = jnp.concatenate([listed_ids, mask_count, jnp.zeros((63,), jnp.int32)])
    info = jnp.broadcast_to(info[None, None, :], (device_count, 1, 2 * MASK_DEV))
    info = lax.all_to_all(info, AXES, split_axis=0, concat_axis=0, tiled=True)
    info = info.reshape(dp_size, bal_size, 2 * MASK_DEV)
    counts = info[:, :, MASK_DEV]
    starts = jnp.cumsum(counts, axis=1) - counts
    steps = jnp.arange(MASK_DEV)
    slot_of = jnp.where(steps < counts[..., None], starts[..., None] + steps, -1)
    slot_of = slot_of.reshape(dp_size, 1, bal_size * MASK_DEV)
    ids_flat = info[:, :, :MASK_DEV].reshape(dp_size, 1, bal_size * MASK_DEV)
    slot_ids = jnp.arange(group_slots)[None, :, None]
    labels = jnp.sum(jnp.where(slot_of == slot_ids, ids_flat, 0), axis=2).reshape(slot_count)
    group_slot_of = lax.dynamic_index_in_dim(slot_of, dp_place, 0, keepdims=False)
    my_slots = bal_place * HEAD_DEV + jnp.arange(HEAD_DEV)
    to_head = (group_slot_of == my_slots[:, None]).astype(LOW)
    own_slot_of = lax.dynamic_slice_in_dim(group_slot_of[0], bal_place * MASK_DEV, MASK_DEV)
    from_head = (own_slot_of[:, None] == jnp.arange(group_slots)[None, :]).astype(LOW)

    qkv_full = grid.gather(qkv_weight)
    both = grid.gather(jnp.concatenate([out_weight, head_weight], axis=1))
    out_full, head_full = both[:, :model_width], both[:, model_width:]
    up_full = grid.gather(up_weight)
    down_full = grid.gather(down_weight)
    padded = jnp.pad(decoder, ((0, 0), (0, part_vocab * device_count - vocab_size)))
    padded = padded.reshape(decoder.shape[0], device_count, part_vocab).transpose(1, 0, 2)
    words = lax.all_to_all(padded, AXES, split_axis=0, concat_axis=0, tiled=True)
    words = words.reshape(model_width, part_vocab)
    padded_bias = jnp.pad(decoder_bias, (0, part_vocab * device_count - vocab_size))
    words_bias = lax.dynamic_slice_in_dim(padded_bias, my_place * part_vocab, part_vocab)

    merged_bias = jnp.concatenate([query_bias, jnp.zeros_like(query_bias), value_bias])
    qkv_rows = (product(tokens, qkv_full) + merged_bias).astype(LOW)
    queries, key_rows, value_rows = (
        heads_of(qkv_rows[:, i * model_width : (i + 1) * model_width]) for i in range(3)
    )
    attn_probs = attention_probs(queries, key_rows, seg_row, seg_row).astype(LOW)
    context = jnp.einsum("hqk,khd->qhd", attn_probs, value_rows, preferred_element_type=jnp.float32)
    context = context.reshape(tok_rows, model_width).astype(LOW)
    resid_one = tokens.astype(jnp.float32) + product(context, out_full) + out_bias
    normed_one = (norm_parts(resid_one)[0] * attn_gain + attn_shift).astype(LOW)
    up_rows = product(normed_one, up_full) + up_bias
    hidden = gelu_exact(up_rows).astype(LOW)
    resid_two = normed_one.astype(jnp.float32) + product(hidden, down_full) + down_bias
    layer_out = (norm_parts(resid_two)[0] * ffn_gain + ffn_shift).astype(LOW)

    pick_low = pick_mat.astype(LOW)
    pick_full = pick_mat.astype(jnp.float32)
    listed_rows = product(pick_low, layer_out).astype(LOW)
    group_rows = grid.gather_group(listed_rows)
    head_in = product(to_head, group_rows).astype(LOW)
    inner_rows = product(head_in, head_full) + head_bias
    head_act, act_back = jax.vjp(gelu_exact, inner_rows)
    head_normal, head_inv = norm_parts(head_act)
    head_normed = (head_normal * head_gain + head_shift).astype(LOW)
    all_normed = grid.gather(head_normed)
    logits = product(all_normed, words) + words_bias
    vocab_ids = my_place * part_vocab + jnp.arange(part_vocab)
    logits = jnp.where(vocab_ids[None, :] < vocab_size, logits, MASK_FILL)
    part_peak = jnp.max(logits, axis=1)
    part_log = part_peak + jnp.log(jnp.sum(jnp.exp(logits - part_peak[:, None]), axis=1))
    spread = jnp.broadcast_to(part_log[None], (device_count, slot_count))
    all_logs = lax.all_to_all(spread, AXES, split_axis=0, concat_axis=0, tiled=True)
    peak = jnp.max(all_logs, axis=0)
    log_total = peak + jnp.log(jnp.sum(jnp.exp(all_logs - peak), axis=0))
    is_label = vocab_ids[None, :] == labels[:, None]
    target_part = jnp.sum(jnp.where(is_label, logits, 0.0))
    loss_part = jnp.where(my_place == 0, jnp.sum(log_total), 0.0) - target_part
    dlogits = (
        (jnp.exp(logits - log_total[:, None]) - is_label.astype(jnp.float32)) * inv_count
    ).astype(LOW)
    dhead_normed = grid.scatter(product_nt(dlogits, words).astype(LOW)).astype(jnp.float32)
    words_grad = product_tn(all_normed, dlogits).astype(LOW)
    words_bias_grad = jnp.sum(dlogits, axis=0, dtype=jnp.float32)
    dhead_act, head_gain_part, head_shift_part = norm_back(
        head_normal, head_inv, head_gain, dhead_normed
    )
    dinner = act_back(dhead_act)[0].astype(LOW)
    head_bias_part = jnp.sum(dinner, axis=0, dtype=jnp.float32)
    head_term = product_tn(head_in, dinner)
    dhead_in = product_nt(dinner, head_full).astype(LOW)
    dlayer_out = product(from_head, grid.gather_group(dhead_in))

    low_rows = product(pick_low, jnp.concatenate([normed_one, context, qkv_rows], axis=1)).astype(LOW)
    normed_s = low_rows[:, :model_width]
    context_s = low_rows[:, model_width : 2 * model_width]
    queries_s = heads_of(low_rows[:, 2 * model_width : 3 * model_width])
    resid_one_s = pick_exact(pick_full, resid_one)
    resid_two_s = pick_exact(pick_full, resid_two)
    normal_two, inv_two = norm_parts(resid_two_s)
    dresid_two, ffn_gain_part, ffn_shift_part = norm_back(normal_two, inv_two, ffn_gain, dlayer_out)
    ddown_rows = dresid_two.astype(LOW)
    up_s = product(normed_s, up_full) + up_bias
    hidden_s, gelu_back = jax.vjp(gelu_exact, up_s)
    down_term = product_tn(hidden_s.astype(LOW), ddown_rows)
    down_bias_part = jnp.sum(ddown_rows, axis=0, dtype=jnp.float32)
    dup_rows = gelu_back(product_nt(ddown_rows, down_full))[0].astype(LOW)
    up_term = product_tn(normed_s, dup_rows)
    up_bias_part = jnp.sum(dup_rows, axis=0, dtype=jnp.float32)
    dnormed_one = dresid_two + product_nt(dup_rows, up_full)
    normal_one, inv_one = norm_parts(resid_one_s)
    dresid_one, attn_gain_part, attn_shift_part = norm_back(
        normal_one, inv_one, attn_gain, dnormed_one
    )
    dattn_sum = dresid_one.astype(LOW)
    out_term = product_tn(context_s, dattn_sum)
    out_bias_part = jnp.sum(dattn_sum, axis=0, dtype=jnp.float32)
    dcontext = heads_of(product_nt(dattn_sum, out_full).astype(LOW))
    probs_s = attention_probs(queries_s, key_rows, listed_seg, seg_row)
    dprobs = jnp.einsum("qhd,khd->hqk", dcontext, value_rows, preferred_element_type=jnp.float32)
    dscores = probs_s * (dprobs - jnp.sum(probs_s * dprobs, axis=-1, keepdims=True))
    dscores = dscores.astype(LOW)
    score_scale = HDIM ** (-0.5)
    dqueries_s = (
        jnp.einsum("hqk,khd->qhd", dscores, key_rows, preferred_element_type=jnp.float32)
        * score_scale
    )
    dkey_rows = (
        jnp.einsum("hqk,qhd->khd", dscores, queries_s, preferred_element_type=jnp.float32)
        * score_scale
    )
    dvalues = jnp.einsum(
        "hqk,qhd->khd", probs_s.astype(LOW), dcontext, preferred_element_type=jnp.float32
    )
    dqueries_s = dqueries_s.reshape(MASK_DEV, model_width).astype(LOW)
    dkey_rows = dkey_rows.reshape(tok_rows, model_width).astype(LOW)
    dvalues = dvalues.reshape(tok_rows, model_width).astype(LOW)
    dqueries = product_tn(pick_low, dqueries_s).astype(LOW)
    dqkv_rows = jnp.concatenate([dqueries, dkey_rows, dvalues], axis=1)
    qkv_term = product_tn(tokens, dqkv_rows)
    query_part = jnp.sum(dqueries_s, axis=0, dtype=jnp.float32)
    value_part = jnp.sum(dvalues, axis=0, dtype=jnp.float32)
    tokens_grad = pick_exact(pick_full.T, dresid_one) + product_nt(dqkv_rows, qkv_full)

    words_back = lax.all_to_all(
        words_grad.reshape(device_count, decoder.shape[0], part_vocab),
        AXES,
        split_axis=0,
        concat_axis=0,
        tiled=True,
    )
    decoder_grad = words_back.transpose(1, 0, 2).reshape(decoder.shape[0], -1)
    decoder_grad = decoder_grad[:, :vocab_size].astype(jnp.float32)
    decoder_bias_grad = grid.gather(words_bias_grad[None]).reshape(-1)[:vocab_size]
    down_grad = grid.scatter(down_term.astype(LOW)).astype(jnp.float32)
    up_grad = grid.scatter(up_term.astype(LOW)).astype(jnp.float32)
    both_term = jnp.concatenate([out_term, head_term], axis=1)
    both_grad = grid.scatter(both_term.astype(LOW)).astype(jnp.float32)
    qkv_grad = grid.scatter(qkv_term.astype(LOW)).astype(jnp.float32)
    small = [
        query_part,
        value_part,
        out_bias_part,
        attn_gain_part,
        attn_shift_part,
        up_bias_part,
        down_bias_part,
        ffn_gain_part,
        ffn_shift_part,
        head_bias_part,
        head_gain_part,
        head_shift_part,
        jnp.full((128,), loss_part),
    ]
    packed = grid.total(jnp.concatenate(small))
    sums = []
    for piece in small:
        sums.append(packed[: piece.shape[0]])
        packed = packed[piece.shape[0] :]
    return (
        layer_out,
        sums[12][0] * inv_count,
        tokens_grad,
        qkv_grad,
        sums[0],
        sums[1],
        both_grad[:, :model_width],
        sums[2],
        sums[3],
        sums[4],
        up_grad,
        sums[5],
        down_grad,
        sums[6],
        sums[7],
        sums[8],
        both_grad[:, model_width:],
        sums[9],
        sums[10],
        sums[11],
        decoder_grad,
        decoder_bias_grad,
    )


def solution(mesh):
    cut, rows = P(("dp", "bal"), None), P(("dp", "bal"))
    whole = P()
    return jax.shard_map(
        per_device,
        mesh=mesh,
        in_specs=(
            cut, cut, rows, cut, rows, cut, whole, whole, cut, whole, whole, whole,
            cut, whole, cut, whole, whole, whole, cut, whole, whole, whole, cut, whole,
        ),
        out_specs=(
            cut, whole, cut, cut, whole, whole, cut, whole, whole, whole, cut,
            whole, cut, whole, whole, whole, cut, whole, whole, whole, cut, whole,
        ),
        check_vma=False,
    )
```

time: 1800 us -> 580 us (0.32)
  waiting for transfers between devices: 1340 us -> 238 us
  matrix products: 171 us -> 100 us
  starting transfers between devices: 53.5 us -> 121 us
  blocking collectives: 48 us -> 0 us
  other arithmetic: 106 us -> 58.7 us
    all_to_all x11 -> x4, waiting for transfers between devices: 591 us -> 6.35 us  [the longest x1 6.34 us: per_device(): lax.all_to_all(spread, AXES, split_axis=0, concat_axis=0, tiled=True)]
    all_gather x6 -> x0, waiting for transfers between devices: 455 us -> none  [the longest x1 258 us: per_device(): lax.all_gather(decoder, ('dp', 'bal'), axis=0, tiled=True)]
    ppermute x0 -> x87, waiting for transfers between devices: none -> 231 us  [shift(): return lax.ppermute(value, AXES, pairs)]
    reduce_scatter x8 -> x0, waiting for transfers between devices: 165 us -> none  [the longest x4 87.6 us: reduce_pair(): lax.psum_scatter(second_part.astype(jnp.bfloat16), 'dp', scatter_dimensio...]
    psum x1 -> x0, waiting for transfers between devices: 123 us -> none  [per_device(): lax.psum((query_part, value_part, out_bias_part, attn_gain_part, attn_shi...]
    ppermute x0 -> x87, starting transfers between devices: none -> 102 us  [shift(): return lax.ppermute(value, AXES, pairs)]
    reduce_sum x21 -> x12, other arithmetic: 64.7 us -> 10.6 us  [the longest x1 3.56 us: per_device(): words_bias_grad = jnp.sum(dlogits, axis=0, dtype=jnp.float32)]
    psum x1 -> x0, blocking collectives: 41.6 us -> none  [per_device(): lax.psum((query_part, value_part, out_bias_part, attn_gain_part, attn_shi...]
  transfers between devices with their start and end apart: 26 -> 91, of which waited for: 18 -> 45; matrix products, arithmetic and copies ran while one was open for 15% -> 31% of each run, Pallas kernels for 0% -> 0%
where the time goes in v1:
time: 580 us; the launch traced here: 574 us
  waiting for transfers between devices  238 us (41%)
  starting transfers between devices  121 us (21%)
  matrix products  100 us (17%)
  other arithmetic  58.7 us (10%)
  local copies, waits for them, and re-layouts  49 us (8%)
  between operations  7.07 us (1%)
    ppermute x87, waiting for transfers between devices, shift(): return lax.ppermute(value, AXES, pairs)  231 us
    ppermute x87, starting transfers between devices, shift(): return lax.ppermute(value, AXES, pairs)  102 us
    dot_general x10, matrix products, product(): return jnp.dot(left_mat, right_mat, preferred_element_type=jnp.float32)  39.9 us
    dot_general x7, matrix products, product_tn(): lax.dot_general(left_mat, right_mat, (((0,), (0,)), ((), ())), preferred_...  16.9 us
    unnamed x271, local copies, waits for them, and re-layouts  14.6 us
    dot_general x6, matrix products, product_nt(): lax.dot_general(left_mat, right_mat, (((1,), (1,)), ((), ())), preferred_...  14.4 us
    sub x2, matrix products, attention_probs(): exp_scores = jnp.exp(masked - row_peak)  14.1 us
  transfers between devices with their start and end apart: 91, of which 45 were waited for; matrix products, arithmetic and copies ran while one was open for 31% of the time, Pallas kernels for 0%

profile of v1, /device:TPU:0, one launch (start us, length us, event | category | flops | bytes accessed | tf_op | source)
XLA Modules:
  0.0 574.5 jit_solution(14340981873442872638)
XLA Ops:
  9.3 7.3 %all-to-all-start = ((s32[32,1,128]{2,1,0:T(1,128)}), s32[32,1,128]{2,1,0:T(1,128)S(1)}, u32[]{:S(2)}, u32[]{:S(2)}) async-start(s32[32,1,128]{2,1,0:T(1,128)} %broadcast_in_dim.1369), calls=%async_computation | async-start | bytes 32768 | tf_op jit(solution)/shard_map/all_to_all | solution.py:250
  30.6 5.3 all-to-all-start.1
  38.5 3.6 collective-permute-start.10
  47.5 20.5 %collective-permute-done.3 = bf16[2,24,1152]{2,1,0:T(8,128)(2,1)S(1)} collective-permute-done((bf16[2,24,1152]{2,1,0:T(8,128)(2,1)S(1)}, bf16[2,24,1152]{2,1,0:T(8,128)(2,1)S(1)}, u32[]{:S(2)}, u32[]{:S(2)}) %collective-permute-start.3) | collective-permute-done | bytes 110624 | tf_op jit(solution)/shard_map/ppermute | solution.py:94
  68.0 20.0 %collective-permute-start.8 = (bf16[2,24,768]{2,1,0:T(8,128)(2,1)S(1)}, bf16[2,24,768]{2,1,0:T(8,128)(2,1)S(1)}, u32[]{:S(2)}, u32[]{:S(2)}) collective-permute-start(bf16[2,24,768]{2,1,0:T(8,128)(2,1)S(1)} %broadcast_select_fusion.29), channel_id=1, source_target_pairs={{0,8},{1,9},{2,10},{3,11},{4,12},{5,13},{6,14},{7,15},{8,16},{9,17... | collective-permute-start | bytes 221192 | tf_op jit(solution)/shard_map/ppermute | solution.py:94
  95.4 3.2 collective-permute-done.24
  98.6 9.4 %collective-permute-done.23 = bf16[2,96,384]{2,1,0:T(8,128)(2,1)S(1)} collective-permute-done((bf16[2,96,384]{2,1,0:T(8,128)(2,1)S(1)}, bf16[2,96,384]{2,1,0:T(8,128)(2,1)S(1)}, u32[]{:S(2)}, u32[]{:S(2)}) %collective-permute-start.23) | collective-permute-done | bytes 147488 | tf_op jit(solution)/shard_map/ppermute | solution.py:94
  117.2 14.1 %collective-permute-done.25 = bf16[4,2,96,384]{3,2,1,0:T(8,128)(2,1)S(1)} collective-permute-done((bf16[4,2,96,384]{3,2,1,0:T(8,128)(2,1)S(1)}, bf16[4,2,96,384]{3,2,1,0:T(8,128)(2,1)S(1)}, u32[]{:S(2)}, u32[]{:S(2)}) %collective-permute-start.25) | collective-permute-done | bytes 589856 | tf_op jit(solution)/shard_map/ppermute | solution.py:94
  133.4 10.5 %collective-permute-done.18 = bf16[4,2,24,1536]{3,2,1,0:T(8,128)(2,1)S(1)} collective-permute-done((bf16[4,2,24,1536]{3,2,1,0:T(8,128)(2,1)S(1)}, bf16[4,2,24,1536]{3,2,1,0:T(8,128)(2,1)S(1)}, u32[]{:S(2)}, u32[]{:S(2)}) %collective-permute-start.18) | collective-permute-done | bytes 589856 | tf_op jit(solution)/shard_map/ppermute | solution.py:94
  146.8 19.9 %collective-permute-done.12 = bf16[2,4,2,24,768]{4,3,2,0,1:T(8,128)(2,1)S(1)} collective-permute-done((bf16[2,4,2,24,768]{4,3,2,0,1:T(8,128)(2,1)S(1)}, bf16[2,4,2,24,768]{4,3,2,0,1:T(8,128)(2,1)S(1)}, u32[]{:S(2)}, u32[]{:S(2)}) %collective-permute-start.12) | collective-permute-done | bytes 589856 | tf_op jit(solution)/shard_map/ppermute | solution.py:94
  172.1 3.1 fusion.22
  177.3 10.6 %fusion.186 = (f32[12,512]{1,0:T(8,128)S(1)}, f32[12,512,512]{1,2,0:T(8,128)}) fusion(pred[512,512]{0,1:T(8,128)(4,1)S(1)} %broadcast_compare_fusion, bf16[512,12,64]{0,2,1:T(8,128)(2,1)} %bitcast.339, bf16[512,12,64]{0,2,1:T(8,128)(2,1)S(1)} %bitcast.334), kind=kOutput, calls=%fused_computation.496 | convolution fusion | flops 415236608 | bytes 14442496 | tf_op jit(solution)/shard_map/sub | solution.py:198
  187.9 6.1 %fusion.42 = bf16[12,64,512]{2,1,0:T(8,128)(2,1)S(1)} fusion(bf16[512,12,64]{0,2,1:T(8,128)(2,1)} %bitcast.337, f32[12,512,512]{1,2,0:T(8,128)} %get-tuple-element.247, f32[12,512]{1,0:T(8,128)S(1)} %get-tuple-element.246), kind=kOutput, calls=%fused_computation.114 | convolution fusion | flops 409337856 | bytes 14180352 | tf_op jit(solution)/shard_map/hqk,khd->qhd/dot_general | solution.py:284
  197.4 5.1 broadcast_select_fusion.1
  202.5 4.9 broadcast_select_fusion.3
  207.4 23.0 %fusion.188 = (f32[512]{0:T(512)S(1)}, f32[512,768]{0,1:T(8,128)S(1)}) fusion(f32[768]{0:T(1024)S(1)} %copy-done.114, bf16[3072,384]{1,0:T(8,128)(2,1)} %get-tuple-element.186, bf16[3072,384]{1,0:T(8,128)(2,1)} %get-tuple-element.185, bf16[512,768]{0,1:T(8,128)(2,1)} %add_convert_fusion.5, f32[3072]{0:T(1024)S(1)} %copy-done.111, ...), kind=kOutput, calls=%fused_computation.498 | convolution fusion | flops 4956093952 | bytes 11813888 | tf_op jit(solution)/shard_map/dot_general | solution.py:23
  234.3 3.0 collective-permute-done.28
  248.5 3.5 fusion.191
  252.1 3.8 collective-permute-start.33
  265.9 4.2 collective-permute-done.34
  272.3 5.9 %collective-permute-done.35 = bf16[2,4,2,32,384]{4,3,2,0,1:T(8,128)(2,1)S(1)} collective-permute-done((bf16[2,4,2,32,384]{4,3,2,0,1:T(8,128)(2,1)S(1)}, bf16[2,4,2,32,384]{4,3,2,0,1:T(8,128)(2,1)S(1)}, u32[]{:S(2)}, u32[]{:S(2)}) %collective-permute-start.35) | collective-permute-done | bytes 393248 | tf_op jit(solution)/shard_map/ppermute | solution.py:94
  283.5 3.5 fusion.31
  289.1 3.0 fusion.21
  292.8 3.2 all-to-all-start.2
  297.9 6.3 %all-to-all-done.2 = f32[32,1,1024]{2,1,0:T(1,128)S(1)} async-done(((f32[32,1,1024]{2,1,0:T(1,128)}), f32[32,1,1024]{2,1,0:T(1,128)S(1)}, u32[]{:S(2)}, u32[]{:S(2)}) %all-to-all-start.2) | async-done | bytes 131104 | tf_op jit(solution)/shard_map/all_to_all | solution.py:309
  304.9 3.6 convert_reduce_fusion
  308.5 3.4 convolution_convert_fusion.5
  312.7 3.0 convolution_convert_fusion.4
  315.7 3.4 all-to-all-start.3
  320.5 3.6 collective-permute-start.83
  325.2 20.3 %collective-permute-done.83 = f32[2,1,512]{2,0,1:T(2,128)S(1)} collective-permute-done((f32[2,1,512]{2,0,1:T(2,128)S(1)}, f32[2,1,512]{2,0,1:T(2,128)S(1)}, u32[]{:S(2)}, u32[]{:S(2)}) %collective-permute-start.83) | collective-permute-done | bytes 4128 | tf_op jit(solution)/shard_map/ppermute | solution.py:94
  345.4 11.8 %collective-permute-done.82 = f32[2,1,512]{2,0,1:T(2,128)S(1)} collective-permute-done((f32[2,1,512]{2,0,1:T(2,128)S(1)}, f32[2,1,512]{2,0,1:T(2,128)S(1)}, u32[]{:S(2)}, u32[]{:S(2)}) %collective-permute-start.82) | collective-permute-done | bytes 4128 | tf_op jit(solution)/shard_map/ppermute | solution.py:94
  362.5 4.3 collective-permute-done.38
  368.0 4.7 collective-permute-done.39
  390.8 3.6 convert_reduce_fusion.2
  408.6 3.6 convolution_convert_fusion.1
  412.3 5.2 convolution_convert_fusion
  423.4 3.6 convolution_convert_fusion.2
  430.3 3.6 fusion.41
  460.1 5.0 collective-permute-done.60
  468.2 3.8 collective-permute-done.61
  487.1 6.7 %collective-permute-done.53 = bf16[4,2,2,24,1152]{4,3,2,1,0:T(8,128)(2,1)S(1)} collective-permute-done((bf16[4,2,2,24,1152]{4,3,2,1,0:T(8,128)(2,1)S(1)}, bf16[4,2,2,24,1152]{4,3,2,1,0:T(8,128)(2,1)S(1)}, u32[]{:S(2)}, u32[]{:S(2)}) %collective-permute-start.53) | collective-permute-done | bytes 884768 | tf_op jit(solution)/shard_map/ppermute | solution.py:94
  497.4 9.9 %collective-permute-done.54 = bf16[4,2,24,1152]{3,2,1,0:T(8,128)(2,1)S(1)} collective-permute-done((bf16[4,2,24,1152]{3,2,1,0:T(8,128)(2,1)S(1)}, bf16[4,2,24,1152]{3,2,1,0:T(8,128)(2,1)S(1)}, u32[]{:S(2)}, u32[]{:S(2)}) %collective-permute-start.54) | collective-permute-done | bytes 442400 | tf_op jit(solution)/shard_map/ppermute | solution.py:94
  512.9 5.1 collective-permute-done.56
  521.6 19.3 %collective-permute-done.74 = bf16[4,2,2,96,384]{4,3,2,1,0:T(8,128)(2,1)S(1)} collective-permute-done((bf16[4,2,2,96,384]{4,3,2,1,0:T(8,128)(2,1)S(1)}, bf16[4,2,2,96,384]{4,3,2,1,0:T(8,128)(2,1)S(1)}, u32[]{:S(2)}, u32[]{:S(2)}) %collective-permute-start.74) | collective-permute-done | bytes 1179680 | tf_op jit(solution)/shard_map/ppermute | solution.py:94
  546.7 4.5 collective-permute-done.75
  555.6 3.6 collective-permute-done.70
  560.8 10.2 %collective-permute-done.77 = bf16[2,96,384]{2,1,0:T(8,128)(2,1)S(1)} collective-permute-done((bf16[2,96,384]{2,1,0:T(8,128)(2,1)S(1)}, bf16[2,96,384]{2,1,0:T(8,128)(2,1)S(1)}, u32[]{:S(2)}, u32[]{:S(2)}) %collective-permute-start.77) | collective-permute-done | bytes 147488 | tf_op jit(solution)/shard_map/ppermute | solution.py:94
  (670 shorter events, 219.1 us)
Async XLA Ops:
  1.8 43.6 %collective-permute-start.21 = (bf16[96,384]{1,0:T(8,128)(2,1)S(1)}, bf16[96,384]{1,0:T(8,128)(2,1)S(1)}, u32[]{:S(2)}, u32[]{:S(2)}) collective-permute-start(bf16[96,384]{1,0:T(8,128)(2,1)S(1)} %get-tuple-element.220), channel_id=1, source_target_pairs={{0,1},{1,0},{2,3},{3,2},{4,5},{5,4},{6,7},{7,6},{8,9},{9,8},{10,11... | collective-permute-start | bytes 221192 | tf_op jit(solution)/shard_map/ppermute | solution.py:94
  3.2 38.9 %collective-permute-start = (bf16[24,1152]{1,0:T(8,128)(2,1)S(1)}, bf16[24,1152]{1,0:T(8,128)(2,1)S(1)}, u32[]{:S(2)}, u32[]{:S(2)}) collective-permute-start(bf16[24,1152]{1,0:T(8,128)(2,1)S(1)} %get-tuple-element.226), channel_id=1, source_target_pairs={{0,1},{1,0},{2,3},{3,2},{4,5},{5,4},{6,7},{7,6},{8,9},{9,8},{10,11... | collective-permute-start | bytes 165896 | tf_op jit(solution)/shard_map/ppermute | solution.py:94
  4.8 33.6 %collective-permute-start.7 = (bf16[24,768]{1,0:T(8,128)(2,1)S(1)}, bf16[24,768]{1,0:T(8,128)(2,1)S(1)}, u32[]{:S(2)}, u32[]{:S(2)}) collective-permute-start(bf16[24,768]{1,0:T(8,128)(2,1)S(1)} %get-tuple-element.230), channel_id=1, source_target_pairs={{0,1},{1,0},{2,3},{3,2},{4,5},{5,4},{6,7},{7,6},{8,9},{9,8},{10,11... | collective-permute-start | bytes 110600 | tf_op jit(solution)/shard_map/ppermute | solution.py:94
  6.3 36.8 %collective-permute-start.14 = (bf16[24,1536]{1,0:T(8,128)(2,1)S(1)}, bf16[24,1536]{1,0:T(8,128)(2,1)S(1)}, u32[]{:S(2)}, u32[]{:S(2)}) collective-permute-start(bf16[24,1536]{1,0:T(8,128)(2,1)S(1)} %get-tuple-element.218), channel_id=1, source_target_pairs={{0,1},{1,0},{2,3},{3,2},{4,5},{5,4},{6,7},{7,6},{8,9},{9,8},{10,11... | collective-permute-start | bytes 221192 | tf_op jit(solution)/shard_map/ppermute | solution.py:94
  9.3 21.3 %all-to-all-start = ((s32[32,1,128]{2,1,0:T(1,128)}), s32[32,1,128]{2,1,0:T(1,128)S(1)}, u32[]{:S(2)}, u32[]{:S(2)}) async-start(s32[32,1,128]{2,1,0:T(1,128)} %broadcast_in_dim.1369), calls=%async_computation | async-start | bytes 32768 | tf_op jit(solution)/shard_map/all_to_all | solution.py:250
  30.6 252.5 %all-to-all-start.1 = ((bf16[32,24,1024]{2,1,0:T(8,128)(2,1)}), bf16[32,24,1024]{2,1,0:T(8,128)(2,1)}, u32[]{:S(2)}, u32[]{:S(2)}) async-start(bf16[32,24,1024]{2,1,0:T(8,128)(2,1)} %copy.181), calls=%async_computation.1 | async-start | bytes 3145728 | tf_op jit(solution)/shard_map/all_to_all | solution.py:273
  38.5 51.1 %collective-permute-start.10 = (bf16[2,24,768]{2,1,0:T(8,128)(2,1)S(1)}, bf16[2,24,768]{2,1,0:T(8,128)(2,1)S(1)}, u32[]{:S(2)}, u32[]{:S(2)}) collective-permute-start(bf16[2,24,768]{2,1,0:T(8,128)(2,1)S(1)} %broadcast_select_fusion.29), channel_id=1, source_target_pairs={{0,24},{1,25},{2,26},{3,27},{4,28},{5,29},{6,30},{7,31},{8,0},{9,1... | collective-permute-start | bytes 221192 | tf_op jit(solution)/shard_map/ppermute | solution.py:94
  42.1 49.5 %collective-permute-start.9 = (bf16[2,24,768]{2,1,0:T(8,128)(2,1)S(1)}, bf16[2,24,768]{2,1,0:T(8,128)(2,1)S(1)}, u32[]{:S(2)}, u32[]{:S(2)}) collective-permute-start(bf16[2,24,768]{2,1,0:T(8,128)(2,1)S(1)} %broadcast_select_fusion.29), channel_id=1, source_target_pairs={{0,16},{1,17},{2,18},{3,19},{4,20},{5,21},{6,22},{7,23},{8,24},{9,... | collective-permute-start | bytes 221192 | tf_op jit(solution)/shard_map/ppermute | solution.py:94
  42.2 25.8 %collective-permute-start.3 = (bf16[2,24,1152]{2,1,0:T(8,128)(2,1)S(1)}, bf16[2,24,1152]{2,1,0:T(8,128)(2,1)S(1)}, u32[]{:S(2)}, u32[]{:S(2)}) collective-permute-start(bf16[2,24,1152]{2,1,0:T(8,128)(2,1)S(1)} %broadcast_select_fusion.27), channel_id=1, source_target_pairs={{0,24},{1,25},{2,26},{3,27},{4,28},{5,29},{6,30},{7,31},{8,0},{9,1... | collective-permute-start | bytes 331784 | tf_op jit(solution)/shard_map/ppermute | solution.py:94
  43.1 46.2 %collective-permute-start.2 = (bf16[2,24,1152]{2,1,0:T(8,128)(2,1)S(1)}, bf16[2,24,1152]{2,1,0:T(8,128)(2,1)S(1)}, u32[]{:S(2)}, u32[]{:S(2)}) collective-permute-start(bf16[2,24,1152]{2,1,0:T(8,128)(2,1)S(1)} %broadcast_select_fusion.27), channel_id=1, source_target_pairs={{0,16},{1,17},{2,18},{3,19},{4,20},{5,21},{6,22},{7,23},{8,24},{9,... | collective-permute-start | bytes 331784 | tf_op jit(solution)/shard_map/ppermute | solution.py:94
  45.4 43.9 %collective-permute-start.1 = (bf16[2,24,1152]{2,1,0:T(8,128)(2,1)S(1)}, bf16[2,24,1152]{2,1,0:T(8,128)(2,1)S(1)}, u32[]{:S(2)}, u32[]{:S(2)}) collective-permute-start(bf16[2,24,1152]{2,1,0:T(8,128)(2,1)S(1)} %broadcast_select_fusion.27), channel_id=1, source_target_pairs={{0,8},{1,9},{2,10},{3,11},{4,12},{5,13},{6,14},{7,15},{8,16},{9,17... | collective-permute-start | bytes 331784 | tf_op jit(solution)/shard_map/ppermute | solution.py:94
  68.0 26.0 %collective-permute-start.8 = (bf16[2,24,768]{2,1,0:T(8,128)(2,1)S(1)}, bf16[2,24,768]{2,1,0:T(8,128)(2,1)S(1)}, u32[]{:S(2)}, u32[]{:S(2)}) collective-permute-start(bf16[2,24,768]{2,1,0:T(8,128)(2,1)S(1)} %broadcast_select_fusion.29), channel_id=1, source_target_pairs={{0,8},{1,9},{2,10},{3,11},{4,12},{5,13},{6,14},{7,15},{8,16},{9,17... | collective-permute-start | bytes 221192 | tf_op jit(solution)/shard_map/ppermute | solution.py:94
  89.3 18.8 %collective-permute-start.23 = (bf16[2,96,384]{2,1,0:T(8,128)(2,1)S(1)}, bf16[2,96,384]{2,1,0:T(8,128)(2,1)S(1)}, u32[]{:S(2)}, u32[]{:S(2)}) collective-permute-start(bf16[2,96,384]{2,1,0:T(8,128)(2,1)S(1)} %broadcast_select_fusion.25), channel_id=1, source_target_pairs={{0,16},{1,17},{2,18},{3,19},{4,20},{5,21},{6,22},{7,23},{8,24},{9,... | collective-permute-start | bytes 442376 | tf_op jit(solution)/shard_map/ppermute | solution.py:94
  89.6 19.0 %collective-permute-start.22 = (bf16[2,96,384]{2,1,0:T(8,128)(2,1)S(1)}, bf16[2,96,384]{2,1,0:T(8,128)(2,1)S(1)}, u32[]{:S(2)}, u32[]{:S(2)}) collective-permute-start(bf16[2,96,384]{2,1,0:T(8,128)(2,1)S(1)} %broadcast_select_fusion.25), channel_id=1, source_target_pairs={{0,8},{1,9},{2,10},{3,11},{4,12},{5,13},{6,14},{7,15},{8,16},{9,17... | collective-permute-start | bytes 442376 | tf_op jit(solution)/shard_map/ppermute | solution.py:94
  91.6 19.6 %collective-permute-start.17 = (bf16[2,24,1536]{2,1,0:T(8,128)(2,1)S(1)}, bf16[2,24,1536]{2,1,0:T(8,128)(2,1)S(1)}, u32[]{:S(2)}, u32[]{:S(2)}) collective-permute-start(bf16[2,24,1536]{2,1,0:T(8,128)(2,1)S(1)} %broadcast_select_fusion.26), channel_id=1, source_target_pairs={{0,24},{1,25},{2,26},{3,27},{4,28},{5,29},{6,30},{7,31},{8,0},{9,1... | collective-permute-start | bytes 442376 | tf_op jit(solution)/shard_map/ppermute | solution.py:94
  94.0 16.1 %collective-permute-start.4 = (bf16[4,2,24,1152]{3,2,1,0:T(8,128)(2,1)S(1)}, bf16[4,2,24,1152]{3,2,1,0:T(8,128)(2,1)S(1)}, u32[]{:S(2)}, u32[]{:S(2)}) collective-permute-start(bf16[4,2,24,1152]{3,2,1,0:T(8,128)(2,1)S(1)} %select_select_fusion.2), channel_id=1, source_target_pairs={{0,4},{1,3},{2,6},{3,1},{4,0},{5,7},{6,2},{7,5},{8,12},{9,11},{10,... | collective-permute-start | bytes 1327112 | tf_op jit(solution)/shard_map/ppermute | solution.py:94
  98.6 14.6 %collective-permute-start.16 = (bf16[2,24,1536]{2,1,0:T(8,128)(2,1)S(1)}, bf16[2,24,1536]{2,1,0:T(8,128)(2,1)S(1)}, u32[]{:S(2)}, u32[]{:S(2)}) collective-permute-start(bf16[2,24,1536]{2,1,0:T(8,128)(2,1)S(1)} %broadcast_select_fusion.26), channel_id=1, source_target_pairs={{0,16},{1,17},{2,18},{3,19},{4,20},{5,21},{6,22},{7,23},{8,24},{9,... | collective-permute-start | bytes 442376 | tf_op jit(solution)/shard_map/ppermute | solution.py:94
  108.6 36.8 %collective-permute-start.11 = (bf16[4,2,24,768]{3,2,1,0:T(8,128)(2,1)S(1)}, bf16[4,2,24,768]{3,2,1,0:T(8,128)(2,1)S(1)}, u32[]{:S(2)}, u32[]{:S(2)}) collective-permute-start(bf16[4,2,24,768]{3,2,1,0:T(8,128)(2,1)S(1)} %select_select_fusion.3), channel_id=1, source_target_pairs={{0,4},{1,3},{2,6},{3,1},{4,0},{5,7},{6,2},{7,5},{8,12},{9,11},{10,... | collective-permute-start | bytes 884744 | tf_op jit(solution)/shard_map/ppermute | solution.py:94
  110.1 21.1 %collective-permute-start.25 = (bf16[4,2,96,384]{3,2,1,0:T(8,128)(2,1)S(1)}, bf16[4,2,96,384]{3,2,1,0:T(8,128)(2,1)S(1)}, u32[]{:S(2)}, u32[]{:S(2)}) collective-permute-start(bf16[4,2,96,384]{3,2,1,0:T(8,128)(2,1)S(1)} %select_select_fusion), channel_id=1, source_target_pairs={{0,4},{1,3},{2,6},{3,1},{4,0},{5,7},{6,2},{7,5},{8,12},{9,11},{10,... | collective-permute-start | bytes 1769480 | tf_op jit(solution)/shard_map/ppermute | solution.py:94
  111.1 21.6 %collective-permute-start.5 = (bf16[2,4,2,24,1152]{4,3,2,0,1:T(8,128)(2,1)S(1)}, bf16[2,4,2,24,1152]{4,3,2,0,1:T(8,128)(2,1)S(1)}, u32[]{:S(2)}, u32[]{:S(2)}) collective-permute-start(bf16[2,4,2,24,1152]{4,3,2,0,1:T(8,128)(2,1)S(1)} %broadcast_select_fusion.12), channel_id=1, source_target_pairs={{0,2},{1,5},{2,0},{3,7},{4,6},{5,1},{6,4},{7,3},{8,10},{9,13},{10,... | collective-permute-start | bytes 2654216 | tf_op jit(solution)/shard_map/ppermute | solution.py:94
  115.7 28.2 %collective-permute-start.18 = (bf16[4,2,24,1536]{3,2,1,0:T(8,128)(2,1)S(1)}, bf16[4,2,24,1536]{3,2,1,0:T(8,128)(2,1)S(1)}, u32[]{:S(2)}, u32[]{:S(2)}) collective-permute-start(bf16[4,2,24,1536]{3,2,1,0:T(8,128)(2,1)S(1)} %select_select_fusion.1), channel_id=1, source_target_pairs={{0,4},{1,3},{2,6},{3,1},{4,0},{5,7},{6,2},{7,5},{8,12},{9,11},{10,... | collective-permute-start | bytes 1769480 | tf_op jit(solution)/shard_map/ppermute | solution.py:94
  131.4 35.6 %collective-permute-start.26 = (bf16[2,4,2,96,384]{4,3,2,0,1:T(8,128)(2,1)S(1)}, bf16[2,4,2,96,384]{4,3,2,0,1:T(8,128)(2,1)S(1)}, u32[]{:S(2)}, u32[]{:S(2)}) collective-permute-start(bf16[2,4,2,96,384]{4,3,2,0,1:T(8,128)(2,1)S(1)} %broadcast_select_fusion.6), channel_id=1, source_target_pairs={{0,2},{1,5},{2,0},{3,7},{4,6},{5,1},{6,4},{7,3},{8,10},{9,13},{10,... | collective-permute-start | bytes 3538952 | tf_op jit(solution)/shard_map/ppermute | solution.py:94
  133.3 38.5 %collective-permute-start.6 = (bf16[768,1152]{1,0:T(8,128)(2,1)S(1)}, bf16[768,1152]{1,0:T(8,128)(2,1)S(1)}, u32[]{:S(2)}, u32[]{:S(2)}) collective-permute-start(bf16[768,1152]{1,0:T(8,128)(2,1)S(1)} %fusion.38), channel_id=1, source_target_pairs={{0,1},{1,0},{2,3},{3,2},{4,5},{5,4},{6,7},{7,6},{8,9},{9,8},{10,11... | collective-permute-start | bytes 5308424 | tf_op jit(solution)/shard_map/ppermute | solution.py:94
  144.0 25.8 %collective-permute-start.19 = (bf16[2,4,2,24,1536]{4,3,2,0,1:T(8,128)(2,1)S(1)}, bf16[2,4,2,24,1536]{4,3,2,0,1:T(8,128)(2,1)S(1)}, u32[]{:S(2)}, u32[]{:S(2)}) collective-permute-start(bf16[2,4,2,24,1536]{4,3,2,0,1:T(8,128)(2,1)S(1)} %broadcast_select_fusion.8), channel_id=1, source_target_pairs={{0,2},{1,5},{2,0},{3,7},{4,6},{5,1},{6,4},{7,3},{8,10},{9,13},{10,... | collective-permute-start | bytes 3538952 | tf_op jit(solution)/shard_map/ppermute | solution.py:94
  145.5 21.2 %collective-permute-start.12 = (bf16[2,4,2,24,768]{4,3,2,0,1:T(8,128)(2,1)S(1)}, bf16[2,4,2,24,768]{4,3,2,0,1:T(8,128)(2,1)S(1)}, u32[]{:S(2)}, u32[]{:S(2)}) collective-permute-start(bf16[2,4,2,24,768]{4,3,2,0,1:T(8,128)(2,1)S(1)} %broadcast_select_fusion.16), channel_id=1, source_target_pairs={{0,2},{1,5},{2,0},{3,7},{4,6},{5,1},{6,4},{7,3},{8,10},{9,13},{10,... | collective-permute-start | bytes 1769480 | tf_op jit(solution)/shard_map/ppermute | solution.py:94
  167.0 27.0 %collective-permute-start.13 = (bf16[768,768]{1,0:T(8,128)(2,1)S(1)}, bf16[768,768]{1,0:T(8,128)(2,1)S(1)}, u32[]{:S(2)}, u32[]{:S(2)}) collective-permute-start(bf16[768,768]{1,0:T(8,128)(2,1)S(1)} %fusion.51), channel_id=1, source_target_pairs={{0,1},{1,0},{2,3},{3,2},{4,5},{5,4},{6,7},{7,6},{8,9},{9,8},{10,11... | collective-permute-start | bytes 3538952 | tf_op jit(solution)/shard_map/ppermute | solution.py:94
  169.4 28.0 %collective-permute-start.27 = (bf16[3072,384]{1,0:T(8,128)(2,1)}, bf16[3072,384]{1,0:T(8,128)(2,1)}, u32[]{:S(2)}, u32[]{:S(2)}) collective-permute-start(bf16[3072,384]{1,0:T(8,128)(2,1)} %fusion.34), channel_id=1, source_target_pairs={{0,1},{1,0},{2,3},{3,2},{4,5},{5,4},{6,7},{7,6},{8,9},{9,8},{10,11... | collective-permute-start | bytes 7077896 | tf_op jit(solution)/shard_map/ppermute | solution.py:94
  171.8 30.7 %collective-permute-start.20 = (bf16[768,1536]{1,0:T(8,128)(2,1)}, bf16[768,1536]{1,0:T(8,128)(2,1)}, u32[]{:S(2)}, u32[]{:S(2)}) collective-permute-start(bf16[768,1536]{1,0:T(8,128)(2,1)} %fusion.35), channel_id=1, source_target_pairs={{0,1},{1,0},{2,3},{3,2},{4,5},{5,4},{6,7},{7,6},{8,9},{9,8},{10,11... | collective-permute-start | bytes 7077896 | tf_op jit(solution)/shard_map/ppermute | solution.py:94
  312.0 46.5 %collective-permute-start.37 = (bf16[1024,384]{1,0:T(8,128)(2,1)S(1)}, bf16[1024,384]{1,0:T(8,128)(2,1)S(1)}, u32[]{:S(2)}, u32[]{:S(2)}) collective-permute-start(bf16[1024,384]{1,0:T(8,128)(2,1)S(1)} %constant_dynamic-slice_fusion.2), channel_id=1, source_target_pairs={{0,1},{1,0},{2,3},{3,2},{4,5},{5,4},{6,7},{7,6},{8,9},{9,8},{10,11... | collective-permute-start | bytes 2359304 | tf_op jit(solution)/shard_map/ppermute | solution.py:94
  315.7 141.1 %all-to-all-start.3 = ((bf16[32,24,1024]{2,1,0:T(8,128)(2,1)}), bf16[32,24,1024]{2,1,0:T(8,128)(2,1)}, u32[]{:S(2)}, u32[]{:S(2)}) async-start(bf16[32,24,1024]{2,1,0:T(8,128)(2,1)} %bitcast.114), calls=%async_computation.3 | async-start | bytes 3145728 | tf_op jit(solution)/shard_map/all_to_all | solution.py:381
  320.5 25.0 %collective-permute-start.83 = (f32[2,1,512]{2,0,1:T(2,128)S(1)}, f32[2,1,512]{2,0,1:T(2,128)S(1)}, u32[]{:S(2)}, u32[]{:S(2)}) collective-permute-start(f32[2,1,512]{2,0,1:T(2,128)S(1)} %broadcast_select_fusion.35), channel_id=1, source_target_pairs={{0,24},{1,25},{2,26},{3,27},{4,28},{5,29},{6,30},{7,31},{8,0},{9,1... | collective-permute-start | bytes 12296 | tf_op jit(solution)/shard_map/ppermute | solution.py:94
  324.0 33.2 %collective-permute-start.82 = (f32[2,1,512]{2,0,1:T(2,128)S(1)}, f32[2,1,512]{2,0,1:T(2,128)S(1)}, u32[]{:S(2)}, u32[]{:S(2)}) collective-permute-start(f32[2,1,512]{2,0,1:T(2,128)S(1)} %broadcast_select_fusion.35), channel_id=1, source_target_pairs={{0,16},{1,17},{2,18},{3,19},{4,20},{5,21},{6,22},{7,23},{8,24},{9,... | collective-permute-start | bytes 12296 | tf_op jit(solution)/shard_map/ppermute | solution.py:94
  324.0 33.2 %collective-permute-start.81 = (f32[2,1,512]{2,0,1:T(2,128)S(1)}, f32[2,1,512]{2,0,1:T(2,128)S(1)}, u32[]{:S(2)}, u32[]{:S(2)}) collective-permute-start(f32[2,1,512]{2,0,1:T(2,128)S(1)} %broadcast_select_fusion.35), channel_id=1, source_target_pairs={{0,8},{1,9},{2,10},{3,11},{4,12},{5,13},{6,14},{7,15},{8,16},{9,17... | collective-permute-start | bytes 12296 | tf_op jit(solution)/shard_map/ppermute | solution.py:94
  361.3 14.0 %collective-permute-start.85 = (f32[2,4,2,1,512]{4,2,0,1,3:T(2,128)S(1)}, f32[2,4,2,1,512]{4,2,0,1,3:T(2,128)S(1)}, u32[]{:S(2)}, u32[]{:S(2)}) collective-permute-start(f32[2,4,2,1,512]{4,2,0,1,3:T(2,128)S(1)} %broadcast_select_fusion.31), channel_id=1, source_target_pairs={{0,2},{1,5},{2,0},{3,7},{4,6},{5,1},{6,4},{7,3},{8,10},{9,13},{10,... | collective-permute-start | bytes 98312 | tf_op jit(solution)/shard_map/ppermute | solution.py:94
  417.9 17.0 %collective-permute-start.46 = (f32[11648]{0:T(1024)S(1)}, f32[11648]{0:T(1024)S(1)}, u32[]{:S(2)}, u32[]{:S(2)}) collective-permute-start(f32[11648]{0:T(1024)S(1)} %constant_dynamic-update-slice_fusion.4), channel_id=1, source_target_pairs={{0,1},{1,0},{2,3},{3,2},{4,5},{5,4},{6,7},{7,6},{8,9},{9,8},{10,11... | collective-permute-start | bytes 139784 | tf_op jit(solution)/shard_map/ppermute | solution.py:94
  434.4 31.8 %collective-permute-start.52 = (bf16[768,1152]{1,0:T(8,128)(2,1)}, bf16[768,1152]{1,0:T(8,128)(2,1)}, u32[]{:S(2)}, u32[]{:S(2)}) collective-permute-start(bf16[768,1152]{1,0:T(8,128)(2,1)} %dynamic-slice_bitcast_fusion), channel_id=1, source_target_pairs={{0,1},{1,0},{2,3},{3,2},{4,5},{5,4},{6,7},{7,6},{8,9},{9,8},{10,11... | collective-permute-start | bytes 5308424 | tf_op jit(solution)/shard_map/ppermute | solution.py:94
  438.1 14.5 %collective-permute-start.59 = (bf16[768,768]{0,1:T(8,128)(2,1)S(1)}, bf16[768,768]{0,1:T(8,128)(2,1)S(1)}, u32[]{:S(2)}, u32[]{:S(2)}) collective-permute-start(bf16[768,768]{0,1:T(8,128)(2,1)S(1)} %fusion.46), channel_id=1, source_target_pairs={{0,1},{1,0},{2,3},{3,2},{4,5},{5,4},{6,7},{7,6},{8,9},{9,8},{10,11... | collective-permute-start | bytes 3538952 | tf_op jit(solution)/shard_map/ppermute | solution.py:94
  447.4 35.7 %collective-permute-start.66 = (bf16[768,1536]{1,0:T(8,128)(2,1)}, bf16[768,1536]{1,0:T(8,128)(2,1)}, u32[]{:S(2)}, u32[]{:S(2)}) collective-permute-start(bf16[768,1536]{1,0:T(8,128)(2,1)} %constant_dynamic-slice_fusion.1), channel_id=1, source_target_pairs={{0,1},{1,0},{2,3},{3,2},{4,5},{5,4},{6,7},{7,6},{8,9},{9,8},{10,11... | collective-permute-start | bytes 7077896 | tf_op jit(solution)/shard_map/ppermute | solution.py:94
  448.8 46.2 %collective-permute-start.73 = (bf16[3072,384]{1,0:T(8,128)(2,1)}, bf16[3072,384]{1,0:T(8,128)(2,1)}, u32[]{:S(2)}, u32[]{:S(2)}) collective-permute-start(bf16[3072,384]{1,0:T(8,128)(2,1)} %constant_dynamic-slice_fusion), channel_id=1, source_target_pairs={{0,1},{1,0},{2,3},{3,2},{4,5},{5,4},{6,7},{7,6},{8,9},{9,8},{10,11... | collective-permute-start | bytes 7077896 | tf_op jit(solution)/shard_map/ppermute | solution.py:94
  480.7 13.1 %collective-permute-start.53 = (bf16[4,2,2,24,1152]{4,3,2,1,0:T(8,128)(2,1)S(1)}, bf16[4,2,2,24,1152]{4,3,2,1,0:T(8,128)(2,1)S(1)}, u32[]{:S(2)}, u32[]{:S(2)}) collective-permute-start(bf16[4,2,2,24,1152]{4,3,2,1,0:T(8,128)(2,1)S(1)} %dynamic-slice_bitcast_fusion.3), channel_id=1, source_target_pairs={{0,2},{1,5},{2,0},{3,7},{4,6},{5,1},{6,4},{7,3},{8,10},{9,13},{10,... | collective-permute-start | bytes 2654216 | tf_op jit(solution)/shard_map/ppermute | solution.py:94
  486.0 34.0 %collective-permute-start.67 = (bf16[4,2,2,24,1536]{4,3,2,1,0:T(8,128)(2,1)S(1)}, bf16[4,2,2,24,1536]{4,3,2,1,0:T(8,128)(2,1)S(1)}, u32[]{:S(2)}, u32[]{:S(2)}) collective-permute-start(bf16[4,2,2,24,1536]{4,3,2,1,0:T(8,128)(2,1)S(1)} %dynamic-slice_bitcast_fusion.2), channel_id=1, source_target_pairs={{0,2},{1,5},{2,0},{3,7},{4,6},{5,1},{6,4},{7,3},{8,10},{9,13},{10,... | collective-permute-start | bytes 3538952 | tf_op jit(solution)/shard_map/ppermute | solution.py:94
  494.1 13.2 %collective-permute-start.54 = (bf16[4,2,24,1152]{3,2,1,0:T(8,128)(2,1)S(1)}, bf16[4,2,24,1152]{3,2,1,0:T(8,128)(2,1)S(1)}, u32[]{:S(2)}, u32[]{:S(2)}) collective-permute-start(bf16[4,2,24,1152]{3,2,1,0:T(8,128)(2,1)S(1)} %dynamic-slice_bitcast_fusion.7), channel_id=1, source_target_pairs={{0,4},{1,3},{2,6},{3,1},{4,0},{5,7},{6,2},{7,5},{8,12},{9,11},{10,... | collective-permute-start | bytes 1327112 | tf_op jit(solution)/shard_map/ppermute | solution.py:94
  518.3 22.6 %collective-permute-start.74 = (bf16[4,2,2,96,384]{4,3,2,1,0:T(8,128)(2,1)S(1)}, bf16[4,2,2,96,384]{4,3,2,1,0:T(8,128)(2,1)S(1)}, u32[]{:S(2)}, u32[]{:S(2)}) collective-permute-start(bf16[4,2,2,96,384]{4,3,2,1,0:T(8,128)(2,1)S(1)} %dynamic-slice_bitcast_fusion.1), channel_id=1, source_target_pairs={{0,2},{1,5},{2,0},{3,7},{4,6},{5,1},{6,4},{7,3},{8,10},{9,13},{10,... | collective-permute-start | bytes 3538952 | tf_op jit(solution)/shard_map/ppermute | solution.py:94
  520.5 21.8 %collective-permute-start.68 = (bf16[4,2,24,1536]{3,2,1,0:T(8,128)(2,1)S(1)}, bf16[4,2,24,1536]{3,2,1,0:T(8,128)(2,1)S(1)}, u32[]{:S(2)}, u32[]{:S(2)}) collective-permute-start(bf16[4,2,24,1536]{3,2,1,0:T(8,128)(2,1)S(1)} %dynamic-slice_bitcast_fusion.5), channel_id=1, source_target_pairs={{0,4},{1,3},{2,6},{3,1},{4,0},{5,7},{6,2},{7,5},{8,12},{9,11},{10,... | collective-permute-start | bytes 1769480 | tf_op jit(solution)/shard_map/ppermute | solution.py:94
  543.4 15.8 %collective-permute-start.70 = (bf16[2,24,1536]{2,1,0:T(8,128)(2,1)S(1)}, bf16[2,24,1536]{2,1,0:T(8,128)(2,1)S(1)}, u32[]{:S(2)}, u32[]{:S(2)}) collective-permute-start(bf16[2,24,1536]{2,1,0:T(8,128)(2,1)S(1)} %get-tuple-element.199), channel_id=1, source_target_pairs={{0,16},{1,17},{2,18},{3,19},{4,20},{5,21},{6,22},{7,23},{8,24},{9,... | collective-permute-start | bytes 442376 | tf_op jit(solution)/shard_map/ppermute | solution.py:94
  544.8 14.4 %collective-permute-start.69 = (bf16[2,24,1536]{2,1,0:T(8,128)(2,1)S(1)}, bf16[2,24,1536]{2,1,0:T(8,128)(2,1)S(1)}, u32[]{:S(2)}, u32[]{:S(2)}) collective-permute-start(bf16[2,24,1536]{2,1,0:T(8,128)(2,1)S(1)} %get-tuple-element.197), channel_id=1, source_target_pairs={{0,8},{1,9},{2,10},{3,11},{4,12},{5,13},{6,14},{7,15},{8,16},{9,17... | collective-permute-start | bytes 442376 | tf_op jit(solution)/shard_map/ppermute | solution.py:94
  552.2 18.7 %collective-permute-start.77 = (bf16[2,96,384]{2,1,0:T(8,128)(2,1)S(1)}, bf16[2,96,384]{2,1,0:T(8,128)(2,1)S(1)}, u32[]{:S(2)}, u32[]{:S(2)}) collective-permute-start(bf16[2,96,384]{2,1,0:T(8,128)(2,1)S(1)} %get-tuple-element.196), channel_id=1, source_target_pairs={{0,16},{1,17},{2,18},{3,19},{4,20},{5,21},{6,22},{7,23},{8,24},{9,... | collective-permute-start | bytes 442376 | tf_op jit(solution)/shard_map/ppermute | solution.py:94
  553.7 17.3 %collective-permute-start.76 = (bf16[2,96,384]{2,1,0:T(8,128)(2,1)S(1)}, bf16[2,96,384]{2,1,0:T(8,128)(2,1)S(1)}, u32[]{:S(2)}, u32[]{:S(2)}) collective-permute-start(bf16[2,96,384]{2,1,0:T(8,128)(2,1)S(1)} %get-tuple-element.194), channel_id=1, source_target_pairs={{0,8},{1,9},{2,10},{3,11},{4,12},{5,13},{6,14},{7,15},{8,16},{9,17... | collective-permute-start | bytes 442376 | tf_op jit(solution)/shard_map/ppermute | solution.py:94
  (170 other events, 1826.2 us)

commit v2 on v1

v2 whole, which is shorter than its diff:
```python
import functools

import jax
import jax.numpy as jnp
from jax import lax
from jax.experimental import pallas as pl
from jax.experimental.pallas import tpu as pltpu
from jax.sharding import PartitionSpec as P

HDIM = 64
HEAD_DEV = 32
MASK_DEV = 64


EPSILON = 1e-06
MASK_FILL = -1e30
AXES = ("dp", "bal")
LOW = jnp.bfloat16


def gelu_exact(values):
    return jax.nn.gelu(values, approximate=False)


def product(left_mat, right_mat):
    return jnp.dot(left_mat, right_mat, preferred_element_type=jnp.float32)


def product_tn(left_mat, right_mat):
    return lax.dot_general(
        left_mat, right_mat, (((0,), (0,)), ((), ())), preferred_element_type=jnp.float32
    )


def product_nt(left_mat, right_mat):
    return lax.dot_general(
        left_mat, right_mat, (((1,), (1,)), ((), ())), preferred_element_type=jnp.float32
    )


def norm_parts(hidden):
    average = jnp.mean(hidden, axis=-1, keepdims=True)
    centered = hidden - average
    inv_std = lax.rsqrt(jnp.mean(centered * centered, axis=-1, keepdims=True) + EPSILON)
    return centered * inv_std, inv_std


def norm_back(normal, inv_std, gain_vec, grad):
    scaled = grad * gain_vec
    first = jnp.mean(scaled, axis=-1, keepdims=True)
    second = jnp.mean(scaled * normal, axis=-1, keepdims=True)
    return (
        inv_std * (scaled - first - normal * second),
        jnp.sum(grad * normal, axis=0),
        jnp.sum(grad, axis=0),
    )


class Grid:
    def __init__(self, dp_size, bal_size):
        self.high = 4 if dp_size % 4 == 0 else 1
        self.low = dp_size // self.high
        self.wide = bal_size // 2
        self.sizes = (self.high, self.low, self.wide, 2)
        self.count = dp_size * bal_size
        dp_place, bal_place = lax.axis_index("dp"), lax.axis_index("bal")
        self.place = (
            dp_place // self.low,
            dp_place % self.low,
            bal_place // 2,
            bal_place % 2,
        )
        self.crossed = self.low == self.wide

    def index(self, spot):
        high, low, wide, core = spot
        return ((high * self.low + low) * self.wide + wide) * 2 + core

    def spots(self):
        for high in range(self.high):
            for low in range(self.low):
                for wide in range(self.wide):
                    for core in range(2):
                        yield (high, low, wide, core)

    def shift(self, value, axis_of, step):
        pairs = []
        for spot in self.spots():
            axis = axis_of[spot[3]]
            target = list(spot)
            target[axis] = (spot[axis] + step) % self.sizes[axis]
            pairs.append((self.index(spot), self.index(target)))
        return lax.ppermute(value, AXES, pairs)

    def own(self, axis_of):
        first, second = self.place[axis_of[0]], self.place[axis_of[1]]
        return first if axis_of[0] == axis_of[1] else jnp.where(self.place[3] == 0, first, second)

    def orders(self):
        return ((1, 2), (2, 1)) if self.crossed else ((1, 1), (2, 2))

    def gather_stage(self, value, axis_of):
        size = self.sizes[axis_of[0]]
        me = self.own(axis_of)
        parts = [value] + [self.shift(value, axis_of, step) for step in range(1, size)]

        def join(hold):
            rel = (me + hold - jnp.arange(size)) % size
            rel = rel.reshape((size,) + (1,) * value.ndim)
            out = parts[-1][None]
            for step in range(size - 2, -1, -1):
                out = jnp.where(rel == step, parts[step][None], out)
            return out

        return join

    def halves(self, first, second):
        is_first = self.place[3] == 0
        return jnp.where(is_first, first, second), jnp.where(is_first, second, first)

    def gather_steps(self, height):
        core = self.place[3]
        first, second = self.orders()

        def start(pair):
            keep, give = pair
            taken = self.shift(give, (3, 3), 1)

            def join(hold):
                is_own = (jnp.arange(2) == core + hold)[:, None, None]
                return jnp.where(is_own, keep[None], taken[None])

            return join

        def third(part):
            other = self.gather_stage(part, second)

            def straight(hold):
                joined = other(hold)
                out = joined.transpose(2, 1, 0, 3, 4, 5)
                if self.crossed:
                    turned = joined.transpose(2, 0, 1, 3, 4, 5)
                    out = jnp.where(core == 0, out, turned)
                return out.reshape(self.count * height, part.shape[-1])

            return straight

        def last(mine):
            other = self.shift(mine, (3, 3), 1)
            return lambda hold: (mine, other)

        return [
            start,
            lambda part: self.gather_stage(part, (0, 0)),
            lambda part: self.gather_stage(part, first),
            third,
            last,
        ]

    def scatter_steps(self, height, taken=None):
        core = self.place[3]
        first, second = self.orders()

        def total(pieces, hold=0):
            out = jnp.asarray(hold).astype(jnp.float32)
            for piece in pieces:
                out = out + piece.astype(jnp.float32)
            return out.astype(LOW)

        def start(pair):
            keep, give = pair
            came = self.shift(give, (3, 3), 1) if taken is None else taken
            shape = (self.high, self.low, self.wide, 2, height, keep.shape[1])
            return lambda hold: ([keep.reshape(shape), came.reshape(shape)], hold)

        def stage(axis_of, piece, hold):
            size = self.sizes[axis_of[0]]
            moved = [self.shift(total(piece(step), hold), axis_of, step) for step in range(1, size)]
            return lambda hold: (piece(0) + moved, hold)

        def cut(given, axis_of, axis):
            parts, hold = given
            size, me = self.sizes[axis_of[0]], self.own(axis_of)

            def piece(step):
                spot = (me + step) % size
                return [lax.dynamic_index_in_dim(part, spot, axis, keepdims=False) for part in parts]

            return stage(axis_of, piece, hold)

        def one(given):
            parts, hold = given
            if not self.crossed:
                return cut(given, second, 2)

            def piece(step):
                def of(part):
                    wide = (self.place[2] + step) % self.wide
                    low = (self.place[1] + step) % self.low
                    return jnp.where(
                        core == 0,
                        lax.dynamic_index_in_dim(part, wide, 2, keepdims=False),
                        lax.dynamic_index_in_dim(part, low, 1, keepdims=False),
                    )

                return [of(part) for part in parts]

            return stage(second, piece, hold)

        def last(given):
            parts, hold = given
            mine = total([lax.dynamic_index_in_dim(part, core, 0, keepdims=False) for part in parts])
            away = total(
                [lax.dynamic_index_in_dim(part, 1 - core, 0, keepdims=False) for part in parts], hold
            )
            other = self.shift(away, (3, 3), 1)
            return lambda hold: (mine, other)

        return [
            start,
            one,
            lambda given: cut(given, first, 1),
            lambda given: cut(given, (0, 0), 0),
            last,
        ]

    def gather_group(self, rows):
        parts = []
        for wide in range(self.wide):
            for core in range(2):
                if wide == 0 and core == 0:
                    parts.append(rows)
                    continue
                pairs = []
                for spot in self.spots():
                    target = (spot[0], spot[1], (spot[2] + wide) % self.wide, (spot[3] + core) % 2)
                    pairs.append((self.index(spot), self.index(target)))
                parts.append(lax.ppermute(rows, AXES, pairs))
        bal_size = self.wide * 2
        wide_from = (self.place[2] - jnp.arange(bal_size) // 2) % self.wide
        core_from = (self.place[3] - jnp.arange(bal_size) % 2) % 2
        rel = (wide_from * 2 + core_from)[:, None, None]
        out = parts[-1][None]
        for step in range(bal_size - 2, -1, -1):
            out = jnp.where(rel == step, parts[step][None], out)
        return out.reshape(bal_size * rows.shape[0], rows.shape[1])

    def total_steps(self):
        def stage(axis):
            def run(part):
                moved = [self.shift(part, (axis, axis), step) for step in range(1, self.sizes[axis])]

                def join(hold):
                    out = part + jnp.asarray(hold).astype(part.dtype)
                    for piece in moved:
                        out = out + piece
                    return out

                return join

            return run

        return [stage(axis) for axis in (3, 2, 1, 0)]


class Transfer:
    def __init__(self, part, steps):
        self.part = part
        self.steps = list(steps)
        self.join = self.steps.pop(0)(part)

    def step(self, *others):
        self.part = self.join(sum((nothing(other) for other in others), 0))
        self.join = self.steps.pop(0)(self.part)

    def finish(self, *others):
        while self.steps:
            self.step(*others)
            others = ()
        self.part = self.join(sum((nothing(other) for other in others), 0))
        return self.part


def nothing(value):
    hold = 0
    for piece in jax.tree.leaves(value):
        if piece.ndim:
            spot = piece[(0,) * piece.ndim]
            hold = hold + (spot != spot).astype(jnp.int32)
    return hold


def once(value, *others):
    for other in others:
        value = value + nothing(other).astype(value.dtype)
    return value


def erf_fast(value):
    value = jnp.clip(value, -3.832506856900711, 3.832506856900711)
    square = value * value
    top = jnp.float32(0.00022905065861350646)
    for number in (0.0034082910107109506, 0.050955695062380861, 0.18520832239976145, 1.128379143519084):
        top = top * square + number
    low = jnp.float32(-1.1791602954361697e-7)
    for number in (
        0.000023547966471313185,
        0.0010179625278914885,
        0.014070470171167667,
        0.11098505178285362,
        0.49746925110067538,
        1.0,
    ):
        low = low * square + number
    return value * top / low


def gelu_fast(value):
    return 0.5 * value * (1.0 + erf_fast(value * 0.7071067811865476))


def gelu_slope(value):
    bell = jnp.exp(value * value * -0.5) * 0.3989422804014327
    return 0.5 * (1.0 + erf_fast(value * 0.7071067811865476)) + value * bell


def call_after(kernel, others, in_specs, **settings):
    others = jax.tree.leaves(others)

    def run(*refs):
        kernel(*refs[len(others) :])

    call = pl.pallas_call(
        run, in_specs=[pl.BlockSpec(memory_space=pl.ANY)] * len(others) + in_specs, **settings
    )
    return lambda *operands: call(*others, *operands)


def full_block(*shape):
    return pl.BlockSpec(shape, lambda step: (0,) * len(shape))


def feed_forward_kernel(
    context_ref,
    tokens_ref,
    out_ref,
    vectors_ref,
    up_first_ref,
    up_second_ref,
    up_bias_ref,
    down_first_ref,
    down_second_ref,
    layer_ref,
    normed_ref,
    one_ref,
    total_ref,
):
    step = pl.program_id(0)
    half = up_first_ref.shape[0]

    @pl.when(step == 0)
    def _():
        attn = jnp.dot(context_ref[...], out_ref[...], preferred_element_type=jnp.float32)
        resid = tokens_ref[...].astype(jnp.float32) + attn + vectors_ref[0:1, :]
        one_ref[...] = resid
        normed = norm_parts(resid)[0] * vectors_ref[1:2, :] + vectors_ref[2:3, :]
        normed = normed.astype(LOW)
        normed_ref[...] = normed
        total_ref[...] = normed.astype(jnp.float32) + vectors_ref[3:4, :]

    normed = normed_ref[...]
    up = product(normed[:, :half], up_first_ref[...]) + product(normed[:, half:], up_second_ref[...])
    hidden = gelu_fast(up + up_bias_ref[...]).astype(LOW)
    total_ref[...] += product(hidden[:, :half], down_first_ref[...]) + product(
        hidden[:, half:], down_second_ref[...]
    )

    @pl.when(step == pl.num_programs(0) - 1)
    def _():
        layer = norm_parts(total_ref[...])[0] * vectors_ref[4:5, :] + vectors_ref[5:6, :]
        layer_ref[...] = layer.astype(LOW)


def weight_blocks(width, steps):
    def cut(row, first):
        return pl.BlockSpec((width // 2, width), lambda step: (row, first + step))

    return [
        cut(0, 0),
        cut(1, 0),
        pl.BlockSpec((1, width), lambda step: (0, step)),
        cut(0, steps),
        cut(1, steps),
    ]


def feed_forward(context, tokens, out_full, vectors, packed, up_bias, others=()):
    rows, width = tokens.shape
    steps = packed.shape[1] // (2 * width)
    block = full_block(rows, width)
    return call_after(
        feed_forward_kernel,
        others,
        [block, block, full_block(width, width), full_block(8, width)] + weight_blocks(width, steps),
        grid=(steps,),
        out_specs=[block, block, block, block],
        out_shape=[
            jax.ShapeDtypeStruct((rows, width), LOW),
            jax.ShapeDtypeStruct((rows, width), LOW),
            jax.ShapeDtypeStruct((rows, width), jnp.float32),
            jax.ShapeDtypeStruct((rows, width), jnp.float32),
        ],
        compiler_params=pltpu.CompilerParams(vmem_limit_bytes=24 * 1024 * 1024),
        cost_estimate=pl.CostEstimate(
            flops=4 * rows * width * width * steps,
            bytes_accessed=4 * width * width * steps,
            transcendentals=rows * width * steps,
        ),
    )(context, tokens, out_full, vectors, packed, packed, up_bias[None, :], packed, packed)


def feed_back_kernel(
    grad_ref,
    one_ref,
    two_ref,
    normed_ref,
    vectors_ref,
    up_first_ref,
    up_second_ref,
    up_bias_ref,
    down_first_ref,
    down_second_ref,
    ddown_ref,
    done_ref,
    up_sum_ref,
    sums_ref,
    total_ref,
):
    step = pl.program_id(0)

    def norm_grad(resid, gain, grad, row):
        normal, inv_std = norm_parts(resid)
        dresid, gain_part, shift_part = norm_back(normal, inv_std, gain, grad)
        sums_ref[row : row + 1, :] = gain_part[None]
        sums_ref[row + 1 : row + 2, :] = shift_part[None]
        sums_ref[row + 2 : row + 3, :] = jnp.sum(
            dresid.astype(LOW).astype(jnp.float32), axis=0, keepdims=True
        )
        return dresid

    @pl.when(step == 0)
    def _():
        sums_ref[...] = jnp.zeros_like(sums_ref)
        dtwo = norm_grad(two_ref[...], vectors_ref[4:5, :], grad_ref[...].astype(jnp.float32), 0)
        total_ref[...] = dtwo
        ddown_ref[...] = dtwo.astype(LOW)

    half = up_first_ref.shape[0]
    normed, ddown = normed_ref[...], ddown_ref[...]
    up = product(normed[:, :half], up_first_ref[...]) + product(normed[:, half:], up_second_ref[...])
    dhidden = jnp.concatenate(
        [product_nt(ddown, down_first_ref[...]), product_nt(ddown, down_second_ref[...])], axis=1
    )
    dup = (gelu_slope(up + up_bias_ref[...]) * dhidden).astype(LOW)
    up_sum_ref[...] = jnp.sum(dup.astype(jnp.float32), axis=0, keepdims=True)
    total_ref[:, :half] += product_nt(dup, up_first_ref[...])
    total_ref[:, half:] += product_nt(dup, up_second_ref[...])

    @pl.when(step == pl.num_programs(0) - 1)
    def _():
        done_ref[...] = norm_grad(one_ref[...], vectors_ref[1:2, :], total_ref[...], 3).astype(LOW)


def feed_back(grad, resid_one, resid_two, normed, vectors, packed, up_bias):
    rows, width = normed.shape
    steps = packed.shape[1] // (2 * width)
    block = full_block(rows, width)
    return pl.pallas_call(
        feed_back_kernel,
        grid=(steps,),
        in_specs=[
            block,
            block,
            block,
            block,
            full_block(8, width),
            *weight_blocks(width, steps),
        ],
        out_specs=[
            block,
            block,
            pl.BlockSpec((1, width), lambda step: (0, step)),
            full_block(8, width),
        ],
        out_shape=[
            jax.ShapeDtypeStruct((rows, width), LOW),
            jax.ShapeDtypeStruct((rows, width), LOW),
            jax.ShapeDtypeStruct((1, width * steps), jnp.float32),
            jax.ShapeDtypeStruct((8, width), jnp.float32),
        ],
        scratch_shapes=[pltpu.VMEM((rows, width), jnp.float32)],
        compiler_params=pltpu.CompilerParams(vmem_limit_bytes=24 * 1024 * 1024),
        cost_estimate=pl.CostEstimate(
            flops=6 * rows * width * width * steps,
            bytes_accessed=4 * width * width * steps,
            transcendentals=rows * width * steps,
        ),
    )(grad, resid_one, resid_two, normed, vectors, packed, packed, up_bias[None, :], packed, packed)


def attention_kernel(
    tokens_ref, weight_ref, bias_ref, seg_column_ref, seg_ref, qkv_ref, context_ref
):
    width = context_ref.shape[1]
    rows = tokens_ref.shape[0]
    qkv = jnp.dot(tokens_ref[...], weight_ref[...], preferred_element_type=jnp.float32)
    qkv_ref[...] = (qkv + bias_ref[...]).astype(LOW)
    block = rows // 2
    for head in range(width // HDIM):
        lanes = [slice(i * width + head * HDIM, i * width + (head + 1) * HDIM) for i in range(3)]
        key, value = qkv_ref[:, lanes[1]], qkv_ref[:, lanes[2]]
        for part in range(2):
            spot = slice(part * block, (part + 1) * block)
            query = qkv_ref[spot, lanes[0]] * jnp.asarray(HDIM ** (-0.5), LOW)
            scores = lax.dot_general(
                query, key, (((1,), (1,)), ((), ())), preferred_element_type=jnp.float32
            )
            scores = jnp.where(seg_column_ref[spot, :] == seg_ref[...], scores, MASK_FILL)
            exp_scores = jnp.exp(scores - jnp.max(scores, axis=-1, keepdims=True))
            probs = exp_scores * (1.0 / jnp.sum(exp_scores, axis=-1, keepdims=True))
            context_ref[spot, lanes[0]] = jnp.dot(
                probs.astype(LOW), value, preferred_element_type=jnp.float32
            ).astype(LOW)


def attention(tokens, weight, bias, seg_row, others=()):
    rows = tokens.shape[0]
    width = bias.shape[1] // 3
    return call_after(
        attention_kernel,
        others,
        [
            full_block(rows, tokens.shape[1]),
            full_block(tokens.shape[1], 3 * width),
            full_block(1, 3 * width),
            full_block(rows, 1),
            full_block(1, rows),
        ],
        grid=(1,),
        out_specs=[full_block(rows, 3 * width), full_block(rows, width)],
        out_shape=[
            jax.ShapeDtypeStruct((rows, 3 * width), LOW),
            jax.ShapeDtypeStruct((rows, width), LOW),
        ],
        compiler_params=pltpu.CompilerParams(vmem_limit_bytes=24 * 1024 * 1024),
        cost_estimate=pl.CostEstimate(
            flops=2 * rows * width * (3 * tokens.shape[1] + 2 * rows),
            bytes_accessed=2 * rows * tokens.shape[1] + 2 * weight.size,
            transcendentals=rows * rows * width // HDIM,
        ),
    )(tokens, weight, bias, seg_row[:, None], seg_row[None, :])


def attention_back_kernel(
    scale,
    queries_ref,
    qkv_in_ref,
    grad_ref,
    listed_seg_ref,
    seg_ref,
    pick_ref,
    dqkv_ref,
    sums_ref,
    dqueries_ref,
):
    width = queries_ref.shape[1]
    same_seg = listed_seg_ref[...] == seg_ref[...]

    def dot(left, right, left_dim, right_dim):
        return lax.dot_general(
            left,
            right,
            (((left_dim,), (right_dim,)), ((), ())),
            preferred_element_type=jnp.float32,
        )

    for head in range(width // HDIM):
        lanes = slice(head * HDIM, (head + 1) * HDIM)
        query = queries_ref[:, lanes]
        key = qkv_in_ref[:, width + head * HDIM : width + (head + 1) * HDIM]
        value = qkv_in_ref[:, 2 * width + head * HDIM : 2 * width + (head + 1) * HDIM]
        grad = grad_ref[:, lanes]
        scores = jnp.where(same_seg, dot(query, key, 1, 1) * scale, MASK_FILL)
        exp_scores = jnp.exp(scores - jnp.max(scores, axis=-1, keepdims=True))
        probs = exp_scores / jnp.sum(exp_scores, axis=-1, keepdims=True)
        dprobs = dot(grad, value, 1, 1)
        dscores = probs * (dprobs - jnp.sum(probs * dprobs, axis=-1, keepdims=True))
        dscores = dscores.astype(LOW)
        dqueries_ref[:, lanes] = (dot(dscores, key, 1, 0) * scale).astype(LOW)
        dqkv_ref[:, width + head * HDIM : width + (head + 1) * HDIM] = (
            dot(dscores, query, 0, 0) * scale
        ).astype(LOW)
        dqkv_ref[:, 2 * width + head * HDIM : 2 * width + (head + 1) * HDIM] = dot(
            probs.astype(LOW), grad, 0, 0
        ).astype(LOW)
    dqueries = dqueries_ref[...]
    dqkv_ref[:, :width] = dot(pick_ref[...], dqueries, 0, 0).astype(LOW)
    sums_ref[...] = jnp.zeros_like(sums_ref)
    sums_ref[0:1, :] = jnp.sum(dqueries.astype(jnp.float32), axis=0, keepdims=True)
    sums_ref[1:2, :] = jnp.sum(
        dqkv_ref[:, 2 * width :].astype(jnp.float32), axis=0, keepdims=True
    )


def attention_back(queries, parts, grad, listed_seg, seg_row, pick, others=()):
    listed, width = queries.shape
    rows = parts.shape[0]
    return call_after(
        functools.partial(attention_back_kernel, HDIM ** (-0.5)),
        others,
        [pl.BlockSpec(memory_space=pltpu.VMEM)] * 6,
        out_shape=[
            jax.ShapeDtypeStruct((rows, 3 * width), LOW),
            jax.ShapeDtypeStruct((8, width), jnp.float32),
        ],
        scratch_shapes=[pltpu.VMEM((listed, width), LOW)],
        compiler_params=pltpu.CompilerParams(vmem_limit_bytes=24 * 1024 * 1024),
        cost_estimate=pl.CostEstimate(
            flops=10 * listed * rows * width,
            bytes_accessed=10 * rows * width,
            transcendentals=listed * rows * width // HDIM,
        ),
    )(queries, parts, grad, listed_seg[:, None], seg_row[None, :], pick)


def heads_of(rows):
    return rows.reshape(rows.shape[0], rows.shape[1] // HDIM, HDIM)


def attention_probs(queries, key_rows, query_seg, key_seg):
    scores = jnp.einsum(
        "qhd,khd->hqk", queries, key_rows, preferred_element_type=jnp.float32
    ) * HDIM ** (-0.5)
    same_seg = query_seg[:, None] == key_seg[None, :]
    masked = jnp.where(same_seg[None], scores, MASK_FILL)
    row_peak = jnp.max(masked, axis=-1, keepdims=True)
    exp_scores = jnp.exp(masked - row_peak)
    return exp_scores / jnp.sum(exp_scores, axis=-1, keepdims=True)


def per_device(
    tokens,
    segment_ids,
    mlm_labels,
    mask_order,
    mask_count,
    qkv_weight,
    query_bias,
    value_bias,
    out_weight,
    out_bias,
    attn_gain,
    attn_shift,
    up_weight,
    up_bias,
    down_weight,
    down_bias,
    ffn_gain,
    ffn_shift,
    head_weight,
    head_bias,
    head_gain,
    head_shift,
    decoder,
    decoder_bias,
):
    model_width = tokens.shape[1]
    tok_rows = tokens.shape[0]
    vocab_size = decoder.shape[1]
    bal_size = lax.axis_size("bal")
    dp_size = lax.axis_size("dp")
    bal_place = lax.axis_index("bal")
    dp_place = lax.axis_index("dp")
    grid = Grid(dp_size, bal_size)
    device_count = dp_size * bal_size
    my_place = dp_place * bal_size + bal_place
    group_slots = HEAD_DEV * bal_size
    slot_count = HEAD_DEV * device_count
    inv_count = 1.0 / slot_count
    part_vocab = -(-(-(-vocab_size // device_count)) // 128) * 128
    seg_row = segment_ids[0]

    listed = mask_order[0, :MASK_DEV]
    pick_mat = listed[:, None] == jnp.arange(tok_rows)[None, :]
    pick_low = pick_mat.astype(LOW)

    def pick(rows):
        return product(pick_low, rows).astype(LOW)

    listed_ids = jnp.sum(jnp.where(pick_mat, mlm_labels[None, :], 0), axis=1)
    listed_seg = jnp.sum(jnp.where(pick_mat, seg_row[None, :], 0), axis=1)

    shard_rows = qkv_weight.shape[0]
    my_units = down_weight.shape[0]
    units = my_units * device_count
    ratio = my_units // shard_rows
    half = model_width // 2

    def unit_order(rows):
        split = rows.reshape(rows.shape[0], device_count, ratio, shard_rows)
        return split.transpose(0, 2, 1, 3).reshape(rows.shape[0], units)

    down_wide = down_weight.reshape(ratio, shard_rows, model_width).transpose(1, 0, 2)
    down_wide = down_wide.reshape(shard_rows, ratio * model_width)
    packed = lax.all_gather(
        jnp.concatenate([unit_order(up_weight), down_wide], axis=1), AXES, axis=0, tiled=True
    )
    up_offsets = unit_order(up_bias[None])[0]
    my_columns = up_weight.reshape(shard_rows, device_count, my_units).transpose(1, 0, 2)
    my_offsets = lax.dynamic_slice_in_dim(up_bias, my_place * my_units, my_units)

    def by_heads(rows):
        split = rows.reshape(rows.shape[0], 3, 2, half)
        return grid.halves(
            split[:, :, 0].reshape(rows.shape[0], 3 * half),
            split[:, :, 1].reshape(rows.shape[0], 3 * half),
        )

    def with_half(rows, half_rows):
        return [jnp.concatenate(pair, axis=1) for pair in zip(rows, half_rows)]

    info = jnp.concatenate([listed_ids, mask_count, jnp.zeros((63,), jnp.int32)])
    info = grid.gather_group(info[None])
    weights_run = Transfer(
        with_half(by_heads(qkv_weight), grid.halves(out_weight, head_weight)),
        grid.gather_steps(shard_rows),
    )
    qkv_width = 3 * half
    weights_run.step()
    weights_run.step(info)
    weights_run.step()
    weights_run.step()
    weights_run.finish()
    all_mine, all_other = weights_run.part
    out_full, head_full = grid.halves(all_mine[:, qkv_width:], all_other[:, qkv_width:])

    counts = info[:, MASK_DEV]
    starts = jnp.cumsum(counts) - counts
    steps = jnp.arange(MASK_DEV)
    slot_of = jnp.where(steps[None] < counts[:, None], starts[:, None] + steps[None], -1)
    own_slot_of = lax.dynamic_index_in_dim(slot_of, bal_place, 0, keepdims=False)
    slot_of = slot_of.reshape(1, bal_size * MASK_DEV)
    my_slots = bal_place * HEAD_DEV + jnp.arange(HEAD_DEV)
    is_mine = slot_of == my_slots[:, None]
    to_head = is_mine.astype(LOW)
    from_head = (own_slot_of[:, None] == jnp.arange(group_slots)[None, :]).astype(LOW)
    my_labels = jnp.sum(jnp.where(is_mine, info[:, :MASK_DEV].reshape(1, -1), 0), axis=1)
    tokens_s = pick(tokens)

    padded = jnp.pad(decoder, ((0, 0), (0, part_vocab * device_count - vocab_size)))
    padded = padded.reshape(decoder.shape[0], device_count, part_vocab).transpose(1, 0, 2)
    bias_mine, bias_other = by_heads(
        jnp.concatenate([query_bias, jnp.zeros_like(query_bias), value_bias])[None]
    )
    parts_mine, context_mine = attention(
        tokens, all_mine, bias_mine, seg_row, [to_head, from_head, tokens_s, padded]
    )
    parts_other, context_other = attention(tokens, all_other, bias_other, seg_row, [context_mine])
    context = jnp.concatenate(grid.halves(context_mine, context_other), axis=1)
    words = lax.all_to_all(padded, AXES, split_axis=0, concat_axis=0, tiled=True)

    picked = [tokens_s, *grid.halves(pick(context_mine), pick(context_other))]
    group_rows = grid.gather_group(jnp.concatenate(picked, axis=1))
    queries_mine, queries_other = pick(parts_mine[:, :half]), pick(parts_other[:, :half])
    my_columns = lax.all_to_all(my_columns, AXES, split_axis=0, concat_axis=0, tiled=True)
    my_columns = my_columns.reshape(model_width, my_units)
    slot_rows = product(to_head, group_rows).astype(LOW)
    tokens_own, context_own = slot_rows[:, :model_width], slot_rows[:, model_width:]
    vectors = jnp.stack(
        [out_bias, attn_gain, attn_shift, down_bias, ffn_gain, ffn_shift, out_bias, out_bias]
    )
    head_in, normed_own, resid_one, resid_two = feed_forward(
        context_own, tokens_own, out_full, vectors, packed, up_offsets, [my_columns, words, queries_mine, queries_other]
    )

    inner_rows = product(head_in, head_full) + head_bias
    head_act, act_back = jax.vjp(gelu_exact, inner_rows)
    head_normal, head_inv = norm_parts(head_act)
    head_normed = (head_normal * head_gain + head_shift).astype(LOW)
    head_run = Transfer(
        grid.halves(head_normed[:, :half], head_normed[:, half:]), grid.gather_steps(HEAD_DEV)
    )
    part_rows = tok_rows // 2
    layer_parts = []

    def layer_part(*others):
        spot = slice(len(layer_parts) * part_rows, (len(layer_parts) + 1) * part_rows)
        part = feed_forward(
            context[spot], tokens[spot], out_full, vectors, packed, up_offsets, others
        )
        layer_parts.append(part[0])
        return part[0]

    head_run.step()
    head_run.step()
    head_run.step()
    head_run.step()
    normed_mine, normed_other = head_run.finish()
    words = words.reshape(model_width, part_vocab)
    words_mine, words_other = grid.halves(words[:half], words[half:])
    padded_bias = jnp.pad(decoder_bias, (0, part_vocab * device_count - vocab_size))
    words_bias = lax.dynamic_slice_in_dim(padded_bias, my_place * part_vocab, part_vocab)
    logits = product(normed_mine, words_mine) + product(normed_other, words_other) + words_bias
    vocab_ids = my_place * part_vocab + jnp.arange(part_vocab)
    logits = jnp.where(vocab_ids[None, :] < vocab_size, logits, MASK_FILL)
    part_peak = jnp.max(logits, axis=1)
    part_log = part_peak + jnp.log(jnp.sum(jnp.exp(logits - part_peak[:, None]), axis=1))
    spread = jnp.concatenate(
        [part_log, my_labels.astype(jnp.float32), jnp.zeros((128 - HEAD_DEV,), jnp.float32)]
    )
    spread = jnp.broadcast_to(spread[None, None], (device_count, 1, slot_count + 128))
    spread = lax.all_to_all(spread, AXES, split_axis=0, concat_axis=0, tiled=True)
    spread = once(spread[:, 0], layer_part(part_log))
    all_logs = spread[:, :slot_count]
    labels = spread[:, slot_count : slot_count + HEAD_DEV].reshape(slot_count).astype(jnp.int32)
    peak = jnp.max(all_logs, axis=0)
    log_total = peak + jnp.log(jnp.sum(jnp.exp(all_logs - peak), axis=0))
    is_label = vocab_ids[None, :] == labels[:, None]
    dlogits = (
        (jnp.exp(logits - log_total[:, None]) - is_label.astype(jnp.float32)) * inv_count
    ).astype(LOW)
    dhead_other = product_nt(dlogits, words_other).astype(LOW)
    dhead_mine = product_nt(dlogits, words_mine).astype(LOW)
    head_run = Transfer((dhead_mine, dhead_other), grid.scatter_steps(HEAD_DEV))
    words_grad = jnp.concatenate(
        grid.halves(product_tn(normed_mine, dlogits), product_tn(normed_other, dlogits))
    ).astype(LOW)
    head_run.step()
    head_run.step(words_grad)
    head_run.step()
    head_run.step()
    words_bias_grad = jnp.sum(dlogits, axis=0, dtype=jnp.float32)
    target_part = jnp.sum(jnp.where(is_label, logits, 0.0))
    loss_part = jnp.where(my_place == 0, jnp.sum(log_total), 0.0) - target_part
    dhead_normed = jnp.concatenate(grid.halves(*head_run.finish()), axis=1).astype(jnp.float32)
    dhead_act, head_gain_part, head_shift_part = norm_back(
        head_normal, head_inv, head_gain, dhead_normed
    )
    dinner = act_back(dhead_act)[0].astype(LOW)
    head_bias_part = jnp.sum(dinner, axis=0, dtype=jnp.float32)
    dhead_in = product_nt(dinner, head_full).astype(LOW)

    ddown_own, dresid_own, up_sums, own_sums = feed_back(
        dhead_in, resid_one, resid_two, normed_own, vectors, packed, up_offsets
    )
    group_grads = grid.gather_group(dresid_own)
    factors = lax.all_gather(
        jnp.concatenate([normed_own, ddown_own], axis=1), AXES, axis=0, tiled=True
    )
    out_term = product_tn(context_own, dresid_own).astype(LOW)
    head_term = product_tn(head_in, dinner).astype(LOW)
    both_mine, both_other = grid.halves(out_term, head_term)
    dresid_one = product(from_head, group_grads).astype(LOW)
    dcontext = product_nt(dresid_one, out_full).astype(LOW)
    dcontext_mine, dcontext_other = grid.halves(dcontext[:, :half], dcontext[:, half:])
    dqkv_other, sums_other = attention_back(
        queries_other,
        parts_other,
        dcontext_other,
        listed_seg,
        seg_row,
        pick_low,
    )
    other_term = product_tn(tokens, dqkv_other).astype(LOW)
    other_term = jnp.concatenate([other_term, both_other], axis=1)
    other_taken = grid.shift(other_term, (3, 3), 1)
    dqkv_mine, sums_mine = attention_back(
        queries_mine,
        parts_mine,
        dcontext_mine,
        listed_seg,
        seg_row,
        pick_low,
        [other_term],
    )
    mine_term = product_tn(tokens, dqkv_mine).astype(LOW)
    mine_term = jnp.concatenate([mine_term, both_mine], axis=1)
    weights_run = Transfer((mine_term, None), grid.scatter_steps(shard_rows, other_taken))
    words_grad = once(words_grad, mine_term)
    words_back = lax.all_to_all(
        words_grad.reshape(device_count, decoder.shape[0], part_vocab),
        AXES,
        split_axis=0,
        concat_axis=0,
        tiled=True,
    )
    weights_run.step()

    qkv_sums = jnp.concatenate(grid.halves(sums_mine, sums_other), axis=1)
    small = jnp.stack(
        [
            qkv_sums[0],
            qkv_sums[1],
            own_sums[5],
            own_sums[3],
            own_sums[4],
            own_sums[2],
            own_sums[0],
            own_sums[1],
            head_bias_part,
            head_gain_part,
            head_shift_part,
            jnp.full((model_width,), loss_part),
        ]
        + jnp.split(up_sums[0], ratio)
    )
    small = jnp.pad(small, ((0, 0), (0, 1024 - model_width)))
    is_here = jnp.arange(device_count) == my_place
    vocab_sums = jnp.where(is_here[:, None], words_bias_grad[None], 0.0).reshape(-1, 1024)
    small_run = Transfer(jnp.concatenate([small, vocab_sums]), grid.total_steps())
    small_run.step()
    weights_run.step(small_run.part, layer_part(mine_term))
    small_run.step()
    tokens_grad = product_tn(pick_low, dresid_one) + product_nt(dqkv_other, all_other[:, :qkv_width])
    tokens_grad = once(tokens_grad, layer_parts[-1]) + product_nt(dqkv_mine, all_mine[:, :qkv_width])

    rows_all, ddown_all = factors[:, :model_width], factors[:, model_width:]
    hidden, act_back = jax.vjp(gelu_exact, product(rows_all, my_columns) + my_offsets)
    dup_all = act_back(product_nt(ddown_all, down_weight))[0].astype(LOW)
    up_term = product_tn(rows_all, dup_all).astype(LOW).reshape(device_count, shard_rows, my_units)
    weights_run.step(small_run.part, tokens_grad)
    small_run.step()
    up_back = lax.all_to_all(up_term, AXES, split_axis=0, concat_axis=0, tiled=True)
    down_grad = product_tn(hidden.astype(LOW), ddown_all)
    up_grad = up_back.transpose(1, 0, 2).reshape(shard_rows, units).astype(jnp.float32)

    weights_run.step(up_term, small_run.part)
    mine, other = weights_run.finish()
    sums = small_run.finish()
    decoder_bias_grad = sums[12 + ratio :].reshape(-1)[:vocab_size]
    sums = sums[: 12 + ratio, :model_width]
    up_sums = sums[12:].reshape(ratio, device_count, shard_rows).transpose(1, 0, 2).reshape(-1)
    first, second = grid.halves(mine[:, :qkv_width], other[:, :qkv_width])
    qkv_grad = jnp.stack(
        [first.reshape(shard_rows, 3, half), second.reshape(shard_rows, 3, half)], axis=2
    )
    qkv_grad = qkv_grad.reshape(shard_rows, 3 * model_width).astype(jnp.float32)
    out_grad, head_grad = grid.halves(mine[:, qkv_width:], other[:, qkv_width:])
    decoder_grad = words_back.transpose(1, 0, 2).reshape(decoder.shape[0], -1)
    decoder_grad = decoder_grad[:, :vocab_size].astype(jnp.float32)
    return (
        jnp.concatenate(layer_parts),
        sums[11, 0] * inv_count,
        tokens_grad,
        qkv_grad,
        sums[0],
        sums[1],
        out_grad.astype(jnp.float32),
        sums[2],
        sums[3],
        sums[4],
        up_grad,
        up_sums,
        down_grad,
        sums[5],
        sums[6],
        sums[7],
        head_grad.astype(jnp.float32),
        sums[8],
        sums[9],
        sums[10],
        decoder_grad,
        decoder_bias_grad,
    )


def solution(mesh):
    cut, rows = P(("dp", "bal"), None), P(("dp", "bal"))
    whole = P()
    return jax.shard_map(
        per_device,
        mesh=mesh,
        in_specs=(
            cut, cut, rows, cut, rows, cut, whole, whole, cut, whole, whole, whole,
            cut, whole, cut, whole, whole, whole, cut, whole, whole, whole, cut, whole,
        ),
        out_specs=(
            cut, whole, cut, cut, whole, whole, cut, whole, whole, whole, cut,
            whole, cut, whole, whole, whole, cut, whole, whole, whole, cut, whole,
        ),
        check_vma=False,
    )
```

time: 580 us -> 452 us (0.78)
  waiting for transfers between devices: 238 us -> 118 us
  matrix products: 100 us -> 41.6 us
  Pallas kernels: 0 us -> 54.6 us
  starting transfers between devices: 121 us -> 70.7 us
  between operations: 7.07 us -> 32.2 us
  local copies, waits for them, and re-layouts: 49 us -> 70.4 us
    ppermute x87 -> x34, waiting for transfers between devices: 231 us -> 104 us  [shift(): return lax.ppermute(value, AXES, pairs)]
    ppermute x87 -> x34, starting transfers between devices: 102 us -> 39.4 us  [shift(): return lax.ppermute(value, AXES, pairs)]
    pallas_call x0 -> x8, Pallas kernels: none -> 54.6 us  [the longest x7 49 us: call_after(): return lambda *operands: call(*others, *operands)]
    dot_general x10 -> x11, matrix products: 39.9 us -> 12.8 us  [product(): return jnp.dot(left_mat, right_mat, preferred_element_type=jnp.float32)]
    unnamed x271 -> x264, local copies, waits for them, and re-layouts: 14.6 us -> 30.9 us
    dot_general x8 -> x0, matrix products: 15.2 us -> none  [the longest x1 6.1 us: per_device(): jnp.einsum('hqk,khd->qhd', attn_probs, value_rows, preferred_element_type...]
    sub x2 -> x0, matrix products: 14.1 us -> none  [attention_probs(): exp_scores = jnp.exp(masked - row_peak)]
    ppermute x0 -> x9, waiting for transfers between devices: none -> 8.88 us  [gather_group(): parts.append(lax.ppermute(rows, AXES, pairs))]
  transfers between devices with their start and end apart: 91 -> 50, of which waited for: 45 -> 19; matrix products, arithmetic and copies ran while one was open for 31% -> 24% of each run, Pallas kernels for 0% -> 10%
where the time goes in v2:
time: 452 us; the launch traced here: 444 us
  waiting for transfers between devices  118 us (26%)
  starting transfers between devices  70.7 us (16%)
  local copies, waits for them, and re-layouts  70.4 us (16%)
  other arithmetic  56.8 us (13%)
  Pallas kernels  54.6 us (12%)
  matrix products  41.6 us (9%)
  between operations  32.2 us (7%)
    ppermute x34, waiting for transfers between devices, shift(): return lax.ppermute(value, AXES, pairs)  104 us
    pallas_call x7, Pallas kernels, call_after(): return lambda *operands: call(*others, *operands)  49 us
    ppermute x34, starting transfers between devices, shift(): return lax.ppermute(value, AXES, pairs)  39.4 us
    unnamed x264, local copies, waits for them, and re-layouts  30.9 us
    dot_general x9, matrix products, product_tn(): lax.dot_general(left_mat, right_mat, (((0,), (0,)), ((), ())), preferred_...  18.1 us
    dot_general x11, matrix products, product(): return jnp.dot(left_mat, right_mat, preferred_element_type=jnp.float32)  12.8 us
    dot_general x6, matrix products, product_nt(): lax.dot_general(left_mat, right_mat, (((1,), (1,)), ((), ())), preferred_...  10.7 us
    convert_element_type x6, other arithmetic, total(): return out.astype(LOW)  9.12 us
  transfers between devices with their start and end apart: 50, of which 19 were waited for; matrix products, arithmetic and copies ran while one was open for 24% of the time, Pallas kernels for 10%

profile of v2, /device:TPU:0, one launch (start us, length us, event | category | flops | bytes accessed | tf_op | source)
XLA Modules:
  0.0 443.9 jit_solution(13693527693041921001)
XLA Ops:
  14.5 5.0 %collective-permute-start.6 = (bf16[2,24,1920]{2,1,0:T(8,128)(2,1)S(1)}, bf16[2,24,1920]{2,1,0:T(8,128)(2,1)S(1)}, u32[]{:S(2)}, u32[]{:S(2)}) collective-permute-start(bf16[2,24,1920]{2,1,0:T(8,128)(2,1)S(1)} %broadcast_select_fusion.14), channel_id=1, source_target_pairs={{0,24},{1,25},{2,26},{3,27},{4,28},{5,29},{6,30},{7,31},{8,0},{9,1... | collective-permute-start | bytes 552968 | tf_op jit(solution)/shard_map/ppermute | solution.py:93
  20.6 4.0 collective-permute-done.6
  24.7 16.9 %collective-permute-done.5 = bf16[2,24,1920]{2,1,0:T(8,128)(2,1)S(1)} collective-permute-done((bf16[2,24,1920]{2,1,0:T(8,128)(2,1)S(1)}, bf16[2,24,1920]{2,1,0:T(8,128)(2,1)S(1)}, u32[]{:S(2)}, u32[]{:S(2)}) %collective-permute-start.5) | collective-permute-done | bytes 184352 | tf_op jit(solution)/shard_map/ppermute | solution.py:93
  43.4 15.1 %collective-permute-done.7 = bf16[4,2,24,1920]{3,2,1,0:T(8,128)(2,1)S(1)} collective-permute-done((bf16[4,2,24,1920]{3,2,1,0:T(8,128)(2,1)S(1)}, bf16[4,2,24,1920]{3,2,1,0:T(8,128)(2,1)S(1)}, u32[]{:S(2)}, u32[]{:S(2)}) %collective-permute-start.7) | collective-permute-done | bytes 737312 | tf_op jit(solution)/shard_map/ppermute | solution.py:93
  63.0 23.2 %collective-permute-done.8 = bf16[2,4,2,24,1920]{4,3,2,0,1:T(8,128)(2,1)S(1)} collective-permute-done((bf16[2,4,2,24,1920]{4,3,2,0,1:T(8,128)(2,1)}, bf16[2,4,2,24,1920]{4,3,2,0,1:T(8,128)(2,1)S(1)}, u32[]{:S(2)}, u32[]{:S(2)}) %collective-permute-start.8) | collective-permute-done | bytes 1474592 | tf_op jit(solution)/shard_map/ppermute | solution.py:93
  86.3 2.4 fusion.6.refs_5_
  89.6 2.5 collective-permute-start.2
  93.2 5.0 %all-to-all-start = ((bf16[32,24,96]{2,1,0:T(8,128)(2,1)}), bf16[32,24,96]{2,1,0:T(8,128)(2,1)S(1)}, u32[]{:S(2)}, u32[]{:S(2)}) async-start(bf16[32,24,96]{2,1,0:T(8,128)(2,1)} %bitcast.309), calls=%async_computation | async-start | bytes 393216 | tf_op jit(solution)/shard_map/all_to_all | solution.py:775
  106.5 4.0 all-to-all-done
  111.1 5.0 %all-to-all-start.1 = ((bf16[32,24,1024]{2,1,0:T(8,128)(2,1)}), bf16[32,24,1024]{2,1,0:T(8,128)(2,1)S(1)}, u32[]{:S(2)}, u32[]{:S(2)}) async-start(bf16[32,24,1024]{2,1,0:T(8,128)(2,1)} %bitcast.316), calls=%async_computation.1 | async-start | bytes 3145728 | tf_op jit(solution)/shard_map/all_to_all | solution.py:770
  121.2 8.1 %shard_map.399 = (bf16[512,1152]{1,0:T(8,128)(2,1)S(1)}, bf16[512,384]{1,0:T(8,128)(2,1)S(1)}) custom-call(bf16[32,256]{1,0:T(8,128)(2,1)S(1)} %compare_convert_fusion.1.refs_0_, bf16[64,128]{1,0:T(8,128)(2,1)S(1)} %fusion.86.refs_1_, bf16[64,768]{1,0:T(8,128)(2,1)S(1)} %copy-done.20, bf16[32,24,1024]{2,1,0:T(8,128)(2,1)S(1)} %bitcast.317, ...), custom_call_target="tpu_custom_call" | custom-call | flops 1308622848 | bytes 3735552 | tf_op jit(solution)/shard_map/pallas_call | solution.py:336
  130.4 8.0 %shard_map.400 = (bf16[512,1152]{1,0:T(8,128)(2,1)S(1)}, bf16[512,384]{1,0:T(8,128)(2,1)S(1)}) custom-call(bf16[512,384]{1,0:T(8,128)(2,1)S(1)} %get-tuple-element.41.refs_0_, bf16[512,768]{1,0:T(8,128)(2,1)S(1)} %copy-done.5, bf16[768,1920]{1,0:T(8,128)(2,1)} %collective-permute-done.9.refs_2_, f32[1,1152]{1,0:T(1,128)S(1)} %bitcast.323, ...), custom_call_target="tpu_custom_call" | custom-call | flops 1308622848 | bytes 3735552 | tf_op jit(solution)/shard_map/pallas_call | solution.py:336
  143.8 2.2 collective-permute-done.12
  146.1 6.6 %collective-permute-done.11 = bf16[64,1536]{1,0:T(8,128)(2,1)S(1)} collective-permute-done((bf16[64,1536]{1,0:T(8,128)(2,1)S(1)}, bf16[64,1536]{1,0:T(8,128)(2,1)S(1)}, u32[]{:S(2)}, u32[]{:S(2)}) %collective-permute-start.11) | collective-permute-done | bytes 196640 | tf_op jit(solution)/shard_map/ppermute | solution.py:238
  154.6 3.7 copy-done
  163.2 4.6 %shard_map.401 = (bf16[32,768]{1,0:T(8,128)(2,1)S(1)}, bf16[32,768]{1,0:T(8,128)(2,1)S(1)}, f32[32,768]{1,0:T(8,128)S(1)}, f32[32,768]{1,0:T(8,128)S(1)}) custom-call(bf16[768,96]{1,0:T(8,128)(2,1)S(1)} %bitcast.318, bf16[32,24,1024]{2,1,0:T(8,128)(2,1)S(1)} %all-to-all-done.1.refs_1_, bf16[64,384]{1,0:T(8,128)(2,1)S(1)} %copy-done.23, ...), custom_call_target="tpu_custom_call" | custom-call | flops 301989888 | bytes 9437184 | tf_op jit(solution)/shard_map/pallas_call | solution.py:336
  167.8 2.9 fusion.113
  175.2 3.9 collective-permute-start.16
  199.0 4.7 %collective-permute-done.18 = bf16[2,4,2,32,384]{4,3,2,0,1:T(8,128)(2,1)S(1)} collective-permute-done((bf16[2,4,2,32,384]{4,3,2,0,1:T(8,128)(2,1)S(1)}, bf16[2,4,2,32,384]{4,3,2,0,1:T(8,128)(2,1)S(1)}, u32[]{:S(2)}, u32[]{:S(2)}) %collective-permute-start.18) | collective-permute-done | bytes 393248 | tf_op jit(solution)/shard_map/ppermute | solution.py:93
  211.8 4.4 all-to-all-start.2
  217.4 3.7 copy-done.1
  221.1 10.5 %shard_map.402 = (bf16[256,768]{1,0:T(8,128)(2,1)S(1)}, bf16[256,768]{1,0:T(8,128)(2,1)}, f32[256,768]{1,0:T(8,128)}, f32[256,768]{1,0:T(8,128)}) custom-call(f32[1024]{0:T(1024)S(1)} %log_add_fusion.1.refs_0_, bf16[256,768]{1,0:T(8,128)(2,1)S(1)} %get-tuple-element.106.refs_1_, bf16[256,768]{1,0:T(8,128)(2,1)S(1)} %copy-done.10, ...), custom_call_target="tpu_custom_call" | custom-call | flops 2415919104 | bytes 9437184 | tf_op jit(solution)/shard_map/pallas_call | solution.py:336
  234.2 4.5 %convert_reduce_fusion = (f32[1024]{0:T(1024)S(1)}, bf16[1024,1024]{0,1:T(8,128)(2,1)S(1)}, f32[]{:T(128)}) fusion(s32[1024]{0:T(1024)S(1)} %convert_element_type.560, s32[1024]{0:T(1024)S(1)} %copy-done.82, f32[1024,1024]{0,1:T(8,128)} %copy-done.44, f32[1024]{0:T(1024)S(1)} %get-tuple-element.80), kind=kLoop, calls=%fused_computation.6 | loop fusion | flops 10484735 | bytes 6307844 | tf_op jit(solution)/shard_map/reduce_sum | solution.py:842
  248.0 3.9 collective-permute-done.21
  253.9 3.9 collective-permute-done.22
  260.1 2.2 collective-permute-start.25
  276.0 3.7 copy-done.2
  279.7 5.5 %shard_map.403 = (bf16[32,768]{1,0:T(8,128)(2,1)S(1)}, bf16[32,768]{1,0:T(8,128)(2,1)S(1)}, f32[1,3072]{1,0:T(1,128)S(1)}, f32[8,768]{1,0:T(8,128)S(1)}) custom-call(bf16[32,768]{1,0:T(8,128)(2,1)S(1)} %convolution_convert_fusion.10.grad_ref, f32[32,768]{1,0:T(8,128)S(1)} %copy-done.32, f32[32,768]{1,0:T(8,128)S(1)} %copy-done.34, ...), custom_call_target="tpu_custom_call" | custom-call | flops 452984832 | bytes 9437184 | tf_op jit(solution)/shard_map/pallas_call | solution.py:478
  289.7 2.8 broadcast_select_fusion.3
  293.8 3.8 shard_map.404
  301.4 3.8 shard_map.405
  306.4 2.6 fusion.5
  312.6 4.8 %all-to-all-start.4 = ((bf16[32,24,1024]{2,1,0:T(8,128)(2,1)}), bf16[32,24,1024]{2,1,0:T(8,128)(2,1)}, u32[]{:S(2)}, u32[]{:S(2)}) async-start(bf16[32,24,1024]{2,1,0:T(8,128)(2,1)} %bitcast.325), calls=%async_computation.4 | async-start | bytes 3145728 | tf_op jit(solution)/shard_map/all_to_all | solution.py:890
  319.6 3.7 copy-done.3
  323.3 10.3 %shard_map.406 = (bf16[256,768]{1,0:T(8,128)(2,1)S(1)}, bf16[256,768]{1,0:T(8,128)(2,1)}, f32[256,768]{1,0:T(8,128)}, f32[256,768]{1,0:T(8,128)}) custom-call(bf16[768,1920]{1,0:T(8,128)(2,1)S(1)} %pad_maximum_fusion.1.refs_0_, bf16[256,768]{1,0:T(8,128)(2,1)S(1)} %get-tuple-element.105.refs_1_, bf16[256,768]{1,0:T(8,128)(2,1)S(1)} %copy-done.9, ...), custom_call_target="tpu_custom_call" | custom-call | flops 2415919104 | bytes 9437184 | tf_op jit(solution)/shard_map/pallas_call | solution.py:336
  335.4 2.7 fusion.9
  341.5 9.2 %collective-permute-done.31 = f32[48,1024]{1,0:T(8,128)S(1)} collective-permute-done((f32[48,1024]{1,0:T(8,128)S(1)}, f32[48,1024]{1,0:T(8,128)S(1)}, u32[]{:S(2)}, u32[]{:S(2)}) %collective-permute-start.31) | collective-permute-done | bytes 196640 | tf_op jit(solution)/shard_map/ppermute | solution.py:93
  351.1 3.8 add_convert_fusion
  356.0 2.7 add_add_fusion
  360.4 2.7 collective-permute-start.34
  371.6 11.2 %collective-permute-done.34 = f32[48,1024]{1,0:T(8,128)S(1)} collective-permute-done((f32[48,1024]{1,0:T(8,128)S(1)}, f32[48,1024]{1,0:T(8,128)S(1)}, u32[]{:S(2)}, u32[]{:S(2)}) %collective-permute-start.34) | collective-permute-done | bytes 196640 | tf_op jit(solution)/shard_map/ppermute | solution.py:93
  394.5 8.3 %collective-permute-done.38 = bf16[4,2,24,1920]{3,2,1,0:T(8,128)(2,1)S(1)} collective-permute-done((bf16[4,2,24,1920]{3,2,1,0:T(8,128)(2,1)S(1)}, bf16[4,2,24,1920]{3,2,1,0:T(8,128)(2,1)S(1)}, u32[]{:S(2)}, u32[]{:S(2)}) %collective-permute-start.38) | collective-permute-done | bytes 737312 | tf_op jit(solution)/shard_map/ppermute | solution.py:93
  403.7 2.2 fusion.48
  405.8 3.8 collective-permute-start.41
  409.7 2.8 fusion.21
  412.5 4.1 fusion.24
  419.6 5.1 %all-to-all-start.3 = ((bf16[32,24,96]{2,1,0:T(8,128)(2,1)}), bf16[32,24,96]{2,1,0:T(8,128)(2,1)}, u32[]{:S(2)}, u32[]{:S(2)}) async-start(bf16[32,24,96]{2,1,0:T(8,128)(2,1)} %bitcast.96), calls=%async_computation.3 | async-start | bytes 393216 | tf_op jit(solution)/shard_map/all_to_all | solution.py:933
  427.7 3.2 fusion.13
  (543 shorter events, 147.8 us)
Async XLA Ops:
  7.2 147.4 %all-gather.3.cloned.1.call-start = ((), (), s32[]{:S(2)}) async-start(), calls=%async_computation.5 | async-start | bytes 9732096 | tf_op jit(solution)/shard_map/all_gather | solution.py:715
  14.5 10.1 %collective-permute-start.6 = (bf16[2,24,1920]{2,1,0:T(8,128)(2,1)S(1)}, bf16[2,24,1920]{2,1,0:T(8,128)(2,1)S(1)}, u32[]{:S(2)}, u32[]{:S(2)}) collective-permute-start(bf16[2,24,1920]{2,1,0:T(8,128)(2,1)S(1)} %broadcast_select_fusion.14), channel_id=1, source_target_pairs={{0,24},{1,25},{2,26},{3,27},{4,28},{5,29},{6,30},{7,31},{8,0},{9,1... | collective-permute-start | bytes 552968 | tf_op jit(solution)/shard_map/ppermute | solution.py:93
  19.6 22.0 %collective-permute-start.5 = (bf16[2,24,1920]{2,1,0:T(8,128)(2,1)S(1)}, bf16[2,24,1920]{2,1,0:T(8,128)(2,1)S(1)}, u32[]{:S(2)}, u32[]{:S(2)}) collective-permute-start(bf16[2,24,1920]{2,1,0:T(8,128)(2,1)S(1)} %broadcast_select_fusion.14), channel_id=1, source_target_pairs={{0,16},{1,17},{2,18},{3,19},{4,20},{5,21},{6,22},{7,23},{8,24},{9,... | collective-permute-start | bytes 552968 | tf_op jit(solution)/shard_map/ppermute | solution.py:93
  19.6 22.0 %collective-permute-start.4 = (bf16[2,24,1920]{2,1,0:T(8,128)(2,1)S(1)}, bf16[2,24,1920]{2,1,0:T(8,128)(2,1)S(1)}, u32[]{:S(2)}, u32[]{:S(2)}) collective-permute-start(bf16[2,24,1920]{2,1,0:T(8,128)(2,1)S(1)} %broadcast_select_fusion.14), channel_id=1, source_target_pairs={{0,8},{1,9},{2,10},{3,11},{4,12},{5,13},{6,14},{7,15},{8,16},{9,17... | collective-permute-start | bytes 552968 | tf_op jit(solution)/shard_map/ppermute | solution.py:93
  41.8 16.7 %collective-permute-start.7 = (bf16[4,2,24,1920]{3,2,1,0:T(8,128)(2,1)S(1)}, bf16[4,2,24,1920]{3,2,1,0:T(8,128)(2,1)S(1)}, u32[]{:S(2)}, u32[]{:S(2)}) collective-permute-start(bf16[4,2,24,1920]{3,2,1,0:T(8,128)(2,1)S(1)} %select_select_fusion.1), channel_id=1, source_target_pairs={{0,4},{1,3},{2,6},{3,1},{4,0},{5,7},{6,2},{7,5},{8,12},{9,11},{10,... | collective-permute-start | bytes 2211848 | tf_op jit(solution)/shard_map/ppermute | solution.py:93
  59.8 26.4 %collective-permute-start.8 = (bf16[2,4,2,24,1920]{4,3,2,0,1:T(8,128)(2,1)}, bf16[2,4,2,24,1920]{4,3,2,0,1:T(8,128)(2,1)S(1)}, u32[]{:S(2)}, u32[]{:S(2)}) collective-permute-start(bf16[2,4,2,24,1920]{4,3,2,0,1:T(8,128)(2,1)} %broadcast_select_fusion), channel_id=1, source_target_pairs={{0,2},{1,5},{2,0},{3,7},{4,6},{5,1},{6,4},{7,3},{8,10},{9,13},{10,... | collective-permute-start | bytes 4423688 | tf_op jit(solution)/shard_map/ppermute | solution.py:93
  88.8 41.6 %collective-permute-start.9 = (bf16[768,1920]{1,0:T(8,128)(2,1)}, bf16[768,1920]{1,0:T(8,128)(2,1)}, u32[]{:S(2)}, u32[]{:S(2)}) collective-permute-start(bf16[768,1920]{1,0:T(8,128)(2,1)} %fusion.6.refs_5_), channel_id=1, source_target_pairs={{0,1},{1,0},{2,3},{3,2},{4,5},{5,4},{6,7},{7,6},{8,9},{9,8},{10,11... | collective-permute-start | bytes 8847368 | tf_op jit(solution)/shard_map/ppermute | solution.py:93
  89.6 16.6 %collective-permute-start.2 = (s32[1,128]{1,0:T(1,128)S(1)}, s32[1,128]{1,0:T(1,128)S(1)}, u32[]{:S(2)}, u32[]{:S(2)}) collective-permute-start(s32[1,128]{1,0:T(1,128)S(1)} %fusion.157), channel_id=1, source_target_pairs={{0,3},{1,2},{2,1},{3,0},{4,7},{5,6},{6,5},{7,4},{8,11},{9,10},{10,... | collective-permute-start | bytes 1544 | tf_op jit(solution)/shard_map/ppermute | solution.py:238
  92.1 14.1 %collective-permute-start.1 = (s32[1,128]{1,0:T(1,128)S(1)}, s32[1,128]{1,0:T(1,128)S(1)}, u32[]{:S(2)}, u32[]{:S(2)}) collective-permute-start(s32[1,128]{1,0:T(1,128)S(1)} %fusion.157), channel_id=1, source_target_pairs={{0,2},{1,3},{2,0},{3,1},{4,6},{5,7},{6,4},{7,5},{8,10},{9,11},{10,... | collective-permute-start | bytes 1544 | tf_op jit(solution)/shard_map/ppermute | solution.py:238
  92.1 14.1 %collective-permute-start = (s32[1,128]{1,0:T(1,128)S(1)}, s32[1,128]{1,0:T(1,128)S(1)}, u32[]{:S(2)}, u32[]{:S(2)}) collective-permute-start(s32[1,128]{1,0:T(1,128)S(1)} %fusion.157), channel_id=1, source_target_pairs={{0,1},{1,0},{2,3},{3,2},{4,5},{5,4},{6,7},{7,6},{8,9},{9,8},{10,11... | collective-permute-start | bytes 1544 | tf_op jit(solution)/shard_map/ppermute | solution.py:238
  93.2 17.2 %all-to-all-start = ((bf16[32,24,96]{2,1,0:T(8,128)(2,1)}), bf16[32,24,96]{2,1,0:T(8,128)(2,1)S(1)}, u32[]{:S(2)}, u32[]{:S(2)}) async-start(bf16[32,24,96]{2,1,0:T(8,128)(2,1)} %bitcast.309), calls=%async_computation | async-start | bytes 393216 | tf_op jit(solution)/shard_map/all_to_all | solution.py:775
  111.1 43.5 %all-to-all-start.1 = ((bf16[32,24,1024]{2,1,0:T(8,128)(2,1)}), bf16[32,24,1024]{2,1,0:T(8,128)(2,1)S(1)}, u32[]{:S(2)}, u32[]{:S(2)}) async-start(bf16[32,24,1024]{2,1,0:T(8,128)(2,1)} %bitcast.316), calls=%async_computation.1 | async-start | bytes 3145728 | tf_op jit(solution)/shard_map/all_to_all | solution.py:770
  139.1 7.0 %collective-permute-start.12 = (bf16[64,1536]{1,0:T(8,128)(2,1)S(1)}, bf16[64,1536]{1,0:T(8,128)(2,1)S(1)}, u32[]{:S(2)}, u32[]{:S(2)}) collective-permute-start(bf16[64,1536]{1,0:T(8,128)(2,1)S(1)} %pad_maximum_fusion.5), channel_id=1, source_target_pairs={{0,3},{1,2},{2,1},{3,0},{4,7},{5,6},{6,5},{7,4},{8,11},{9,10},{10,... | collective-permute-start | bytes 589832 | tf_op jit(solution)/shard_map/ppermute | solution.py:238
  140.8 11.9 %collective-permute-start.11 = (bf16[64,1536]{1,0:T(8,128)(2,1)S(1)}, bf16[64,1536]{1,0:T(8,128)(2,1)S(1)}, u32[]{:S(2)}, u32[]{:S(2)}) collective-permute-start(bf16[64,1536]{1,0:T(8,128)(2,1)S(1)} %pad_maximum_fusion.5), channel_id=1, source_target_pairs={{0,2},{1,3},{2,0},{3,1},{4,6},{5,7},{6,4},{7,5},{8,10},{9,11},{10,... | collective-permute-start | bytes 589832 | tf_op jit(solution)/shard_map/ppermute | solution.py:238
  141.2 11.5 %collective-permute-start.10 = (bf16[64,1536]{1,0:T(8,128)(2,1)S(1)}, bf16[64,1536]{1,0:T(8,128)(2,1)S(1)}, u32[]{:S(2)}, u32[]{:S(2)}) collective-permute-start(bf16[64,1536]{1,0:T(8,128)(2,1)S(1)} %pad_maximum_fusion.5), channel_id=1, source_target_pairs={{0,1},{1,0},{2,3},{3,2},{4,5},{5,4},{6,7},{7,6},{8,9},{9,8},{10,11... | collective-permute-start | bytes 589832 | tf_op jit(solution)/shard_map/ppermute | solution.py:238
  175.2 11.7 %collective-permute-start.16 = (bf16[2,32,384]{2,1,0:T(8,128)(2,1)}, bf16[2,32,384]{2,1,0:T(8,128)(2,1)}, u32[]{:S(2)}, u32[]{:S(2)}) collective-permute-start(bf16[2,32,384]{2,1,0:T(8,128)(2,1)} %broadcast_select_fusion.22), channel_id=1, source_target_pairs={{0,24},{1,25},{2,26},{3,27},{4,28},{5,29},{6,30},{7,31},{8,0},{9,1... | collective-permute-start | bytes 147464 | tf_op jit(solution)/shard_map/ppermute | solution.py:93
  179.1 7.9 %collective-permute-start.15 = (bf16[2,32,384]{2,1,0:T(8,128)(2,1)}, bf16[2,32,384]{2,1,0:T(8,128)(2,1)}, u32[]{:S(2)}, u32[]{:S(2)}) collective-permute-start(bf16[2,32,384]{2,1,0:T(8,128)(2,1)} %broadcast_select_fusion.22), channel_id=1, source_target_pairs={{0,16},{1,17},{2,18},{3,19},{4,20},{5,21},{6,22},{7,23},{8,24},{9,... | collective-permute-start | bytes 147464 | tf_op jit(solution)/shard_map/ppermute | solution.py:93
  179.1 7.9 %collective-permute-start.14 = (bf16[2,32,384]{2,1,0:T(8,128)(2,1)}, bf16[2,32,384]{2,1,0:T(8,128)(2,1)}, u32[]{:S(2)}, u32[]{:S(2)}) collective-permute-start(bf16[2,32,384]{2,1,0:T(8,128)(2,1)} %broadcast_select_fusion.22), channel_id=1, source_target_pairs={{0,8},{1,9},{2,10},{3,11},{4,12},{5,13},{6,14},{7,15},{8,16},{9,17... | collective-permute-start | bytes 147464 | tf_op jit(solution)/shard_map/ppermute | solution.py:93
  188.7 6.0 %collective-permute-start.17 = (bf16[4,2,32,384]{3,2,1,0:T(8,128)(2,1)}, bf16[4,2,32,384]{3,2,1,0:T(8,128)(2,1)}, u32[]{:S(2)}, u32[]{:S(2)}) collective-permute-start(bf16[4,2,32,384]{3,2,1,0:T(8,128)(2,1)} %select_select_fusion.2), channel_id=1, source_target_pairs={{0,4},{1,3},{2,6},{3,1},{4,0},{5,7},{6,2},{7,5},{8,12},{9,11},{10,... | collective-permute-start | bytes 589832 | tf_op jit(solution)/shard_map/ppermute | solution.py:93
  195.8 7.8 %collective-permute-start.18 = (bf16[2,4,2,32,384]{4,3,2,0,1:T(8,128)(2,1)S(1)}, bf16[2,4,2,32,384]{4,3,2,0,1:T(8,128)(2,1)S(1)}, u32[]{:S(2)}, u32[]{:S(2)}) collective-permute-start(bf16[2,4,2,32,384]{4,3,2,0,1:T(8,128)(2,1)S(1)} %broadcast_select_fusion.10), channel_id=1, source_target_pairs={{0,2},{1,5},{2,0},{3,7},{4,6},{5,1},{6,4},{7,3},{8,10},{9,13},{10,... | collective-permute-start | bytes 1179656 | tf_op jit(solution)/shard_map/ppermute | solution.py:93
  204.4 2.6 collective-permute-start.19
  211.8 21.6 %all-to-all-start.2 = ((f32[32,1,1152]{2,1,0:T(1,128)}), f32[32,1,1152]{2,1,0:T(1,128)S(1)}, u32[]{:S(2)}, u32[]{:S(2)}) async-start(f32[32,1,1152]{2,1,0:T(1,128)} %broadcast_in_dim.768), calls=%async_computation.2 | async-start | bytes 294912 | tf_op jit(solution)/shard_map/all_to_all | solution.py:822
  216.2 193.4 %all-gather.5.cloned.1.call-start = ((), (), s32[]{:S(2)}) async-start(), calls=%async_computation.6 | async-start | bytes 3244032 | tf_op jit(solution)/shard_map/all_gather | solution.py:857
  240.1 3.8 collective-permute-start.20
  244.1 7.8 %collective-permute-start.21 = (bf16[4,2,2,32,384]{4,3,2,1,0:T(8,128)(2,1)S(1)}, bf16[4,2,2,32,384]{4,3,2,1,0:T(8,128)(2,1)S(1)}, u32[]{:S(2)}, u32[]{:S(2)}) collective-permute-start(bf16[4,2,2,32,384]{4,3,2,1,0:T(8,128)(2,1)S(1)} %add_convert_fusion.2), channel_id=1, source_target_pairs={{0,2},{1,5},{2,0},{3,7},{4,6},{5,1},{6,4},{7,3},{8,10},{9,13},{10,... | collective-permute-start | bytes 1179656 | tf_op jit(solution)/shard_map/ppermute | solution.py:93
  252.1 5.7 %collective-permute-start.22 = (bf16[4,2,32,384]{3,2,1,0:T(8,128)(2,1)S(1)}, bf16[4,2,32,384]{3,2,1,0:T(8,128)(2,1)S(1)}, u32[]{:S(2)}, u32[]{:S(2)}) collective-permute-start(bf16[4,2,32,384]{3,2,1,0:T(8,128)(2,1)S(1)} %fusion.49), channel_id=1, source_target_pairs={{0,4},{1,3},{2,6},{3,1},{4,0},{5,7},{6,2},{7,5},{8,12},{9,11},{10,... | collective-permute-start | bytes 589832 | tf_op jit(solution)/shard_map/ppermute | solution.py:93
  258.5 8.6 %collective-permute-start.23 = (bf16[2,32,384]{2,1,0:T(8,128)(2,1)S(1)}, bf16[2,32,384]{2,1,0:T(8,128)(2,1)}, u32[]{:S(2)}, u32[]{:S(2)}) collective-permute-start(bf16[2,32,384]{2,1,0:T(8,128)(2,1)S(1)} %get-tuple-element.100), channel_id=1, source_target_pairs={{0,8},{1,9},{2,10},{3,11},{4,12},{5,13},{6,14},{7,15},{8,16},{9,17... | collective-permute-start | bytes 147464 | tf_op jit(solution)/shard_map/ppermute | solution.py:93
  260.1 6.9 %collective-permute-start.25 = (bf16[2,32,384]{2,1,0:T(8,128)(2,1)S(1)}, bf16[2,32,384]{2,1,0:T(8,128)(2,1)}, u32[]{:S(2)}, u32[]{:S(2)}) collective-permute-start(bf16[2,32,384]{2,1,0:T(8,128)(2,1)S(1)} %get-tuple-element.101), channel_id=1, source_target_pairs={{0,24},{1,25},{2,26},{3,27},{4,28},{5,29},{6,30},{7,31},{8,0},{9,1... | collective-permute-start | bytes 147464 | tf_op jit(solution)/shard_map/ppermute | solution.py:93
  262.3 5.1 %collective-permute-start.24 = (bf16[2,32,384]{2,1,0:T(8,128)(2,1)S(1)}, bf16[2,32,384]{2,1,0:T(8,128)(2,1)}, u32[]{:S(2)}, u32[]{:S(2)}) collective-permute-start(bf16[2,32,384]{2,1,0:T(8,128)(2,1)S(1)} %get-tuple-element.102), channel_id=1, source_target_pairs={{0,16},{1,17},{2,18},{3,19},{4,20},{5,21},{6,22},{7,23},{8,24},{9,... | collective-permute-start | bytes 147464 | tf_op jit(solution)/shard_map/ppermute | solution.py:93
  268.8 2.0 collective-permute-start.26
  285.3 7.2 %collective-permute-start.29 = (bf16[32,768]{1,0:T(8,128)(2,1)S(1)}, bf16[32,768]{1,0:T(8,128)(2,1)S(1)}, u32[]{:S(2)}, u32[]{:S(2)}) collective-permute-start(bf16[32,768]{1,0:T(8,128)(2,1)S(1)} %get-tuple-element.49), channel_id=1, source_target_pairs={{0,3},{1,2},{2,1},{3,0},{4,7},{5,6},{6,5},{7,4},{8,11},{9,10},{10,... | collective-permute-start | bytes 147464 | tf_op jit(solution)/shard_map/ppermute | solution.py:238
  287.1 5.4 %collective-permute-start.28 = (bf16[32,768]{1,0:T(8,128)(2,1)S(1)}, bf16[32,768]{1,0:T(8,128)(2,1)S(1)}, u32[]{:S(2)}, u32[]{:S(2)}) collective-permute-start(bf16[32,768]{1,0:T(8,128)(2,1)S(1)} %get-tuple-element.49), channel_id=1, source_target_pairs={{0,2},{1,3},{2,0},{3,1},{4,6},{5,7},{6,4},{7,5},{8,10},{9,11},{10,... | collective-permute-start | bytes 147464 | tf_op jit(solution)/shard_map/ppermute | solution.py:238
  287.5 5.1 %collective-permute-start.27 = (bf16[32,768]{1,0:T(8,128)(2,1)S(1)}, bf16[32,768]{1,0:T(8,128)(2,1)S(1)}, u32[]{:S(2)}, u32[]{:S(2)}) collective-permute-start(bf16[32,768]{1,0:T(8,128)(2,1)S(1)} %get-tuple-element.49), channel_id=1, source_target_pairs={{0,1},{1,0},{2,3},{3,2},{4,5},{5,4},{6,7},{7,6},{8,9},{9,8},{10,11... | collective-permute-start | bytes 147464 | tf_op jit(solution)/shard_map/ppermute | solution.py:238
  300.8 50.3 %collective-permute-start.36 = (bf16[768,1920]{1,0:T(8,128)(2,1)}, bf16[768,1920]{1,0:T(8,128)(2,1)}, u32[]{:S(2)}, u32[]{:S(2)}) collective-permute-start(bf16[768,1920]{1,0:T(8,128)(2,1)} %pad_maximum_fusion.refs_0_), channel_id=1, source_target_pairs={{0,1},{1,0},{2,3},{3,2},{4,5},{5,4},{6,7},{7,6},{8,9},{9,8},{10,11... | collective-permute-start | bytes 8847368 | tf_op jit(solution)/shard_map/ppermute | solution.py:93
  306.3 31.8 %collective-permute-start.30 = (f32[48,1024]{1,0:T(8,128)S(1)}, f32[48,1024]{1,0:T(8,128)}, u32[]{:S(2)}, u32[]{:S(2)}) collective-permute-start(f32[48,1024]{1,0:T(8,128)S(1)} %select_maximum_fusion), channel_id=1, source_target_pairs={{0,1},{1,0},{2,3},{3,2},{4,5},{5,4},{6,7},{7,6},{8,9},{9,8},{10,11... | collective-permute-start | bytes 589832 | tf_op jit(solution)/shard_map/ppermute | solution.py:93
  312.6 75.7 %all-to-all-start.4 = ((bf16[32,24,1024]{2,1,0:T(8,128)(2,1)}), bf16[32,24,1024]{2,1,0:T(8,128)(2,1)}, u32[]{:S(2)}, u32[]{:S(2)}) async-start(bf16[32,24,1024]{2,1,0:T(8,128)(2,1)} %bitcast.325), calls=%async_computation.4 | async-start | bytes 3145728 | tf_op jit(solution)/shard_map/all_to_all | solution.py:890
  339.1 11.6 %collective-permute-start.31 = (f32[48,1024]{1,0:T(8,128)S(1)}, f32[48,1024]{1,0:T(8,128)S(1)}, u32[]{:S(2)}, u32[]{:S(2)}) collective-permute-start(f32[48,1024]{1,0:T(8,128)S(1)} %fusion.107), channel_id=1, source_target_pairs={{0,2},{1,3},{2,0},{3,1},{4,6},{5,7},{6,4},{7,5},{8,10},{9,11},{10,... | collective-permute-start | bytes 589832 | tf_op jit(solution)/shard_map/ppermute | solution.py:93
  350.7 8.6 %collective-permute-start.32 = (f32[48,1024]{1,0:T(8,128)S(1)}, f32[48,1024]{1,0:T(8,128)S(1)}, u32[]{:S(2)}, u32[]{:S(2)}) collective-permute-start(f32[48,1024]{1,0:T(8,128)S(1)} %add.1034), channel_id=1, source_target_pairs={{0,4},{1,5},{2,6},{3,7},{4,0},{5,1},{6,2},{7,3},{8,12},{9,13},{10,... | collective-permute-start | bytes 589832 | tf_op jit(solution)/shard_map/ppermute | solution.py:93
  354.9 34.9 %collective-permute-start.37 = (bf16[4,2,2,24,1920]{4,3,2,1,0:T(8,128)(2,1)}, bf16[4,2,2,24,1920]{4,3,2,1,0:T(8,128)(2,1)}, u32[]{:S(2)}, u32[]{:S(2)}) collective-permute-start(bf16[4,2,2,24,1920]{4,3,2,1,0:T(8,128)(2,1)} %add_convert_fusion), channel_id=1, source_target_pairs={{0,2},{1,5},{2,0},{3,7},{4,6},{5,1},{6,4},{7,3},{8,10},{9,13},{10,... | collective-permute-start | bytes 4423688 | tf_op jit(solution)/shard_map/ppermute | solution.py:93
  359.3 12.2 %collective-permute-start.35 = (f32[48,1024]{1,0:T(8,128)S(1)}, f32[48,1024]{1,0:T(8,128)S(1)}, u32[]{:S(2)}, u32[]{:S(2)}) collective-permute-start(f32[48,1024]{1,0:T(8,128)S(1)} %add.1035), channel_id=1, source_target_pairs={{0,24},{1,25},{2,26},{3,27},{4,28},{5,29},{6,30},{7,31},{8,0},{9,1... | collective-permute-start | bytes 589832 | tf_op jit(solution)/shard_map/ppermute | solution.py:93
  360.4 22.3 %collective-permute-start.34 = (f32[48,1024]{1,0:T(8,128)S(1)}, f32[48,1024]{1,0:T(8,128)S(1)}, u32[]{:S(2)}, u32[]{:S(2)}) collective-permute-start(f32[48,1024]{1,0:T(8,128)S(1)} %add.1035), channel_id=1, source_target_pairs={{0,16},{1,17},{2,18},{3,19},{4,20},{5,21},{6,22},{7,23},{8,24},{9,... | collective-permute-start | bytes 589832 | tf_op jit(solution)/shard_map/ppermute | solution.py:93
  363.2 19.6 %collective-permute-start.33 = (f32[48,1024]{1,0:T(8,128)S(1)}, f32[48,1024]{1,0:T(8,128)S(1)}, u32[]{:S(2)}, u32[]{:S(2)}) collective-permute-start(f32[48,1024]{1,0:T(8,128)S(1)} %add.1035), channel_id=1, source_target_pairs={{0,8},{1,9},{2,10},{3,11},{4,12},{5,13},{6,14},{7,15},{8,16},{9,17... | collective-permute-start | bytes 589832 | tf_op jit(solution)/shard_map/ppermute | solution.py:93
  391.3 11.5 %collective-permute-start.38 = (bf16[4,2,24,1920]{3,2,1,0:T(8,128)(2,1)S(1)}, bf16[4,2,24,1920]{3,2,1,0:T(8,128)(2,1)S(1)}, u32[]{:S(2)}, u32[]{:S(2)}) collective-permute-start(bf16[4,2,24,1920]{3,2,1,0:T(8,128)(2,1)S(1)} %fusion.30), channel_id=1, source_target_pairs={{0,4},{1,3},{2,6},{3,1},{4,0},{5,7},{6,2},{7,5},{8,12},{9,11},{10,... | collective-permute-start | bytes 2211848 | tf_op jit(solution)/shard_map/ppermute | solution.py:93
  405.8 20.1 %collective-permute-start.39 = (bf16[2,24,1920]{2,1,0:T(8,128)(2,1)}, bf16[2,24,1920]{2,1,0:T(8,128)(2,1)}, u32[]{:S(2)}, u32[]{:S(2)}) collective-permute-start(bf16[2,24,1920]{2,1,0:T(8,128)(2,1)} %get-tuple-element.90), channel_id=1, source_target_pairs={{0,8},{1,9},{2,10},{3,11},{4,12},{5,13},{6,14},{7,15},{8,16},{9,17... | collective-permute-start | bytes 552968 | tf_op jit(solution)/shard_map/ppermute | solution.py:93
  405.8 20.2 %collective-permute-start.41 = (bf16[2,24,1920]{2,1,0:T(8,128)(2,1)}, bf16[2,24,1920]{2,1,0:T(8,128)(2,1)}, u32[]{:S(2)}, u32[]{:S(2)}) collective-permute-start(bf16[2,24,1920]{2,1,0:T(8,128)(2,1)} %get-tuple-element.91), channel_id=1, source_target_pairs={{0,24},{1,25},{2,26},{3,27},{4,28},{5,29},{6,30},{7,31},{8,0},{9,1... | collective-permute-start | bytes 552968 | tf_op jit(solution)/shard_map/ppermute | solution.py:93
  409.7 16.3 %collective-permute-start.40 = (bf16[2,24,1920]{2,1,0:T(8,128)(2,1)}, bf16[2,24,1920]{2,1,0:T(8,128)(2,1)}, u32[]{:S(2)}, u32[]{:S(2)}) collective-permute-start(bf16[2,24,1920]{2,1,0:T(8,128)(2,1)} %get-tuple-element.92), channel_id=1, source_target_pairs={{0,16},{1,17},{2,18},{3,19},{4,20},{5,21},{6,22},{7,23},{8,24},{9,... | collective-permute-start | bytes 552968 | tf_op jit(solution)/shard_map/ppermute | solution.py:93
  419.6 14.0 %all-to-all-start.3 = ((bf16[32,24,96]{2,1,0:T(8,128)(2,1)}), bf16[32,24,96]{2,1,0:T(8,128)(2,1)}, u32[]{:S(2)}, u32[]{:S(2)}) async-start(bf16[32,24,96]{2,1,0:T(8,128)(2,1)} %bitcast.96), calls=%async_computation.3 | async-start | bytes 393216 | tf_op jit(solution)/shard_map/all_to_all | solution.py:933
  427.5 3.5 collective-permute-start.42
  (131 other events, 1028.3 us)
Sparse Core Ops, SparseCore 0:
  12.7 101.0 all-gather.2
  289.8 71.3 all-gather.4

commit v3 on v2

v3 whole, which is shorter than its diff:
```python
import functools

import jax
import jax.numpy as jnp
import numpy as np
from jax import lax
from jax.experimental import pallas as pl
from jax.experimental.pallas import tpu as pltpu
from jax.sharding import PartitionSpec as P

HDIM = 64
HEAD_DEV = 32
MASK_DEV = 64


EPSILON = 1e-06
MASK_FILL = -1e30
AXES = ("dp", "bal")
LOW = jnp.bfloat16


def gelu_exact(values):
    return jax.nn.gelu(values, approximate=False)


def product(left_mat, right_mat):
    return jnp.dot(left_mat, right_mat, preferred_element_type=jnp.float32)


def product_tn(left_mat, right_mat):
    return lax.dot_general(
        left_mat, right_mat, (((0,), (0,)), ((), ())), preferred_element_type=jnp.float32
    )


def product_nt(left_mat, right_mat):
    return lax.dot_general(
        left_mat, right_mat, (((1,), (1,)), ((), ())), preferred_element_type=jnp.float32
    )


def norm_parts(hidden):
    average = jnp.mean(hidden, axis=-1, keepdims=True)
    centered = hidden - average
    inv_std = lax.rsqrt(jnp.mean(centered * centered, axis=-1, keepdims=True) + EPSILON)
    return centered * inv_std, inv_std


def norm_back(normal, inv_std, gain_vec, grad):
    scaled = grad * gain_vec
    first = jnp.mean(scaled, axis=-1, keepdims=True)
    second = jnp.mean(scaled * normal, axis=-1, keepdims=True)
    return (
        inv_std * (scaled - first - normal * second),
        jnp.sum(grad * normal, axis=0),
        jnp.sum(grad, axis=0),
    )


class Grid:
    def __init__(self, dp_size, bal_size):
        self.high = 4 if dp_size % 4 == 0 else 1
        self.low = dp_size // self.high
        self.wide = bal_size // 2
        self.sizes = (self.high, self.low, self.wide, 2)
        self.count = dp_size * bal_size
        dp_place, bal_place = lax.axis_index("dp"), lax.axis_index("bal")
        self.place = (
            dp_place // self.low,
            dp_place % self.low,
            bal_place // 2,
            bal_place % 2,
        )
        self.crossed = self.low == self.wide

    def index(self, spot):
        high, low, wide, core = spot
        return ((high * self.low + low) * self.wide + wide) * 2 + core

    def spots(self):
        for high in range(self.high):
            for low in range(self.low):
                for wide in range(self.wide):
                    for core in range(2):
                        yield (high, low, wide, core)

    def shift(self, value, axis_of, step):
        pairs = []
        for spot in self.spots():
            axis = axis_of[spot[3]]
            target = list(spot)
            target[axis] = (spot[axis] + step) % self.sizes[axis]
            pairs.append((self.index(spot), self.index(target)))
        self.sent = value
        return lax.ppermute(value, AXES, pairs)

    def own(self, axis_of):
        first, second = self.place[axis_of[0]], self.place[axis_of[1]]
        return first if axis_of[0] == axis_of[1] else jnp.where(self.place[3] == 0, first, second)

    def orders(self):
        return ((1, 2), (2, 1)) if self.crossed else ((1, 1), (2, 2))

    def gather_stage(self, value, axis_of):
        size = self.sizes[axis_of[0]]
        me = self.own(axis_of)
        parts = [value] + [self.shift(value, axis_of, step) for step in range(1, size)]

        def join(hold):
            rel = (me + hold - jnp.arange(size)) % size
            rel = rel.reshape((size,) + (1,) * value.ndim)
            out = parts[-1][None]
            for step in range(size - 2, -1, -1):
                out = jnp.where(rel == step, parts[step][None], out)
            return out

        return join

    def halves(self, first, second, hold=0):
        is_first = self.place[3] + hold == 0
        return lax.select(is_first, first, second), lax.select(is_first, second, first)

    def gather_steps(self, height):
        core = self.place[3]
        first, second = self.orders()

        def start(pair):
            keep, give = pair
            taken = self.shift(give, (3, 3), 1)

            def join(hold):
                is_own = (jnp.arange(2) == core + hold)[:, None, None]
                return jnp.where(is_own, keep[None], taken[None])

            return join

        def third(part):
            other = self.gather_stage(part, second)

            def straight(hold):
                joined = other(hold)
                out = joined.transpose(2, 1, 0, 3, 4, 5)
                if self.crossed:
                    turned = joined.transpose(2, 0, 1, 3, 4, 5)
                    out = lax.select(core == 0, out, turned)
                return out.reshape(self.count * height, part.shape[-1])

            return straight

        def last(mine):
            other = self.shift(mine, (3, 3), 1)
            return lambda hold: (mine, other)

        return [
            start,
            lambda part: self.gather_stage(part, (0, 0)),
            lambda part: self.gather_stage(part, first),
            third,
            last,
        ]

    def scatter_steps(self, height, taken=None):
        core = self.place[3]
        first, second = self.orders()

        def total(pieces, hold=0):
            out = jnp.asarray(hold).astype(jnp.float32)
            for piece in pieces:
                out = out + piece.astype(jnp.float32)
            return out.astype(LOW)

        def start(pair):
            keep, give = pair
            came = self.shift(give, (3, 3), 1) if taken is None else taken
            shape = (self.high, self.low, self.wide, 2, height, keep.shape[1])
            return lambda hold: ([keep.reshape(shape), came.reshape(shape)], hold)

        def stage(axis_of, piece, hold):
            size = self.sizes[axis_of[0]]
            moved = [self.shift(total(piece(step), hold), axis_of, step) for step in range(1, size)]
            return lambda hold: (piece(0) + moved, hold)

        def cut(given, axis_of, axis):
            parts, hold = given
            size, me = self.sizes[axis_of[0]], self.own(axis_of)

            def piece(step):
                spot = (me + step) % size
                return [lax.dynamic_index_in_dim(part, spot, axis, keepdims=False) for part in parts]

            return stage(axis_of, piece, hold)

        def one(given):
            parts, hold = given
            if not self.crossed:
                return cut(given, second, 2)
            size, me = self.wide, self.own(second)
            flat = [part.reshape(self.high, size * size, *part.shape[3:]) for part in parts]

            def piece(step, along):
                spot = (me + step) % size
                spot = jnp.where(core == 0, along * size + spot, spot * size + along)
                return [lax.dynamic_index_in_dim(part, spot, 1, keepdims=False) for part in flat]

            moved = [
                [self.shift(total(piece(step, along), hold), second, step) for step in range(1, size)]
                for along in range(size)
            ]
            return lambda hold: ([piece(0, along) + moved[along] for along in range(size)], hold)

        def two(given):
            if not self.crossed:
                return cut(given, first, 1)
            columns, hold = given
            size, me = self.low, self.own(first)

            def piece(step):
                spot = (me + step) % size
                out = columns[-1]
                for along in range(size - 2, -1, -1):
                    out = [lax.select(spot == along, *pair) for pair in zip(columns[along], out)]
                return out

            return stage(first, piece, hold)

        def last(given):
            parts, hold = given
            mine = total([lax.dynamic_index_in_dim(part, core, 0, keepdims=False) for part in parts])
            away = total(
                [lax.dynamic_index_in_dim(part, 1 - core, 0, keepdims=False) for part in parts], hold
            )
            other = self.shift(away, (3, 3), 1)
            return lambda hold: (mine, other)

        return [
            start,
            one,
            two,
            lambda given: cut(given, (0, 0), 0),
            last,
        ]

    def group(self):
        return [
            (self.place[2] - wide) % self.wide * 2 + (self.place[3] - core) % 2
            for wide in range(self.wide)
            for core in range(2)
        ]

    def gather_group(self, rows):
        parts = []
        for wide in range(self.wide):
            for core in range(2):
                if wide == 0 and core == 0:
                    parts.append(rows)
                    continue
                pairs = []
                for spot in self.spots():
                    target = (spot[0], spot[1], (spot[2] + wide) % self.wide, (spot[3] + core) % 2)
                    pairs.append((self.index(spot), self.index(target)))
                parts.append(lax.ppermute(rows, AXES, pairs))
        return parts


class Transfer:
    def __init__(self, part, steps):
        self.part = part
        self.steps = list(steps)
        self.join = self.steps.pop(0)(part)

    def step(self, *others):
        self.part = self.join(sum((nothing(other) for other in others), 0))
        self.join = self.steps.pop(0)(self.part)

    def finish(self, *others):
        while self.steps:
            self.step(*others)
            others = ()
        self.part = self.join(sum((nothing(other) for other in others), 0))
        return self.part


def nothing(value):
    hold = 0
    for piece in jax.tree.leaves(value):
        if piece.ndim:
            spot = piece[(0,) * piece.ndim]
            is_float = jnp.issubdtype(spot.dtype, jnp.floating)
            hold = hold + (spot != spot if is_float else spot < -1).astype(jnp.int32)
    return hold


def once(value, *others):
    for other in others:
        value = value + nothing(other).astype(value.dtype)
    return value


def erf_fast(value):
    value = jnp.clip(value, -3.832506856900711, 3.832506856900711)
    square = value * value
    top = jnp.float32(0.00022905065861350646)
    for number in (0.0034082910107109506, 0.050955695062380861, 0.18520832239976145, 1.128379143519084):
        top = top * square + number
    low = jnp.float32(-1.1791602954361697e-7)
    for number in (
        0.000023547966471313185,
        0.0010179625278914885,
        0.014070470171167667,
        0.11098505178285362,
        0.49746925110067538,
        1.0,
    ):
        low = low * square + number
    return value * top / low


def gelu_fast(value):
    return 0.5 * value * (1.0 + erf_fast(value * 0.7071067811865476))


def gelu_slope(value):
    bell = jnp.exp(value * value * -0.5) * 0.3989422804014327
    return 0.5 * (1.0 + erf_fast(value * 0.7071067811865476)) + value * bell


def call_after(kernel, others, in_specs, **settings):
    others = jax.tree.leaves(others)

    def run(*refs):
        kernel(*refs[len(others) :])

    call = pl.pallas_call(
        run, in_specs=[pl.BlockSpec(memory_space=pl.ANY)] * len(others) + in_specs, **settings
    )
    return lambda *operands: call(*others, *operands)


def load_weights(packed_ref, weights_ref, sems):
    count, _, width = weights_ref.shape
    copies = []
    order = [part * (count // 2) + block for block in range(count // 2) for part in range(2)]
    for block in order:
        source = packed_ref.at[:, block * width : (block + 1) * width]
        copies.append((block, pltpu.make_async_copy(source, weights_ref.at[block], sems.at[block])))
        copies[-1][1].start()
    return dict(copies)


def feed_forward_kernel(
    spot_out,
    context_ref,
    tokens_ref,
    out_ref,
    vectors_ref,
    up_bias_ref,
    packed_ref,
    layer_ref,
    normed_ref,
    one_ref,
    total_ref,
    weights_ref,
    sems,
):
    copies = load_weights(packed_ref, weights_ref, sems)
    blocks = len(copies) // 2
    width = tokens_ref.shape[1]
    resid = tokens_ref[spot_out, :].astype(jnp.float32)
    resid = resid + product(context_ref[spot_out, :], out_ref[...])
    resid = resid + vectors_ref[0:1, :]
    one_ref[...] = resid
    normed = norm_parts(resid)[0] * vectors_ref[1:2, :] + vectors_ref[2:3, :]
    normed = normed.astype(LOW)
    normed_ref[...] = normed
    total_ref[...] = normed.astype(jnp.float32) + vectors_ref[3:4, :]
    rows = total_ref.shape[0]
    parts = max(1, rows // 128)
    for block in range(blocks):
        copies[block].wait()
        copies[blocks + block].wait()
        bias = up_bias_ref[:, block * width : (block + 1) * width]
        for part in range(parts):
            spot = slice(part * (rows // parts), (part + 1) * (rows // parts))
            up = product(normed_ref[spot, :], weights_ref[block])
            hidden = gelu_fast(up + bias).astype(LOW)
            total_ref[spot, :] += product(hidden, weights_ref[blocks + block])
    layer = norm_parts(total_ref[...])[0] * vectors_ref[4:5, :] + vectors_ref[5:6, :]
    layer_ref[spot_out, :] = layer.astype(LOW)


def square_scratch(packed, width):
    count = packed.shape[1] // width
    return [pltpu.VMEM((count, width, width), LOW), pltpu.SemaphoreType.DMA((count,))]


def feed_forward_more_kernel(spot, into_ref, *refs):
    layer_ref = refs[6]
    layer_ref[: spot.start, :] = into_ref[: spot.start, :]
    feed_forward_kernel(spot, *refs)


def feed_forward(context, tokens, out_full, vectors, packed, up_bias, others, room, part=0, parts=1, into=None):
    rows, width = tokens.shape[0] // parts, tokens.shape[1]
    units = packed.shape[1] // 2
    spot = slice(part * rows, (part + 1) * rows)
    more = () if into is None else (into,)
    kernel = functools.partial(feed_forward_kernel, spot)
    if more:
        kernel = functools.partial(feed_forward_more_kernel, spot)
    others = jax.tree.leaves(others)
    return call_after(
        kernel,
        others,
        [pl.BlockSpec(memory_space=pltpu.VMEM)] * (5 + len(more))
        + [pl.BlockSpec(memory_space=pltpu.HBM)],
        out_shape=[
            jax.ShapeDtypeStruct((parts * rows, width), LOW),
            jax.ShapeDtypeStruct((rows, width), LOW),
            jax.ShapeDtypeStruct((rows, width), jnp.float32),
            jax.ShapeDtypeStruct((rows, width), jnp.float32),
        ],
        scratch_shapes=square_scratch(packed, width),
        compiler_params=pltpu.CompilerParams(vmem_limit_bytes=room * 1024 * 1024),
        cost_estimate=pl.CostEstimate(
            flops=4 * rows * width * units,
            bytes_accessed=4 * width * units,
            transcendentals=rows * units,
        ),
    )(*more, context, tokens, out_full, vectors, up_bias[None, :], packed)


def feed_back_kernel(
    grad_ref,
    one_ref,
    two_ref,
    normed_ref,
    vectors_ref,
    more_ref,
    up_bias_ref,
    packed_ref,
    send_ref,
    done_ref,
    total_ref,
    sums_ref,
    weights_ref,
    sems,
):
    copies = load_weights(packed_ref, weights_ref, sems)
    blocks = len(copies) // 2
    width = normed_ref.shape[1]
    sums_ref[...] = jnp.zeros_like(sums_ref)
    sums_ref[0:6, :] = more_ref[0:6, :]

    def norm_grad(resid, gain, grad, row):
        normal, inv_std = norm_parts(resid)
        dresid, gain_part, shift_part = norm_back(normal, inv_std, gain, grad)
        sums_ref[row : row + 1, :] = gain_part[None]
        sums_ref[row + 1 : row + 2, :] = shift_part[None]
        sums_ref[row + 2 : row + 3, :] = jnp.sum(
            dresid.astype(LOW).astype(jnp.float32), axis=0, keepdims=True
        )
        return dresid

    dtwo = norm_grad(two_ref[...], vectors_ref[4:5, :], grad_ref[...].astype(jnp.float32), 6)
    total_ref[...] = dtwo
    ddown = dtwo.astype(LOW)
    send_ref[:, :width] = ddown
    for block in range(blocks):
        copies[block].wait()
        copies[blocks + block].wait()
        spot = slice(block * width, (block + 1) * width)
        up = product(normed_ref[...], weights_ref[block]) + up_bias_ref[:, spot]
        dup = (gelu_slope(up) * product_nt(ddown, weights_ref[blocks + block])).astype(LOW)
        sums_ref[12 + block : 13 + block, :] = jnp.sum(
            dup.astype(jnp.float32), axis=0, keepdims=True
        )
        total_ref[...] += product_nt(dup, weights_ref[block])
    done_ref[...] = norm_grad(one_ref[...], vectors_ref[1:2, :], total_ref[...], 9).astype(LOW)
    half = width // 2
    send_ref[:16, width:] = sums_ref[:, :half].astype(LOW)
    send_ref[16:, width:] = sums_ref[:, half:].astype(LOW)


def feed_back(grad, resid_one, resid_two, normed, vectors, more, packed, up_bias, others):
    rows, width = normed.shape
    units = packed.shape[1] // 2
    return call_after(
        feed_back_kernel,
        others,
        [pl.BlockSpec(memory_space=pltpu.VMEM)] * 7
        + [pl.BlockSpec(memory_space=pltpu.HBM)],
        out_shape=[
            jax.ShapeDtypeStruct((rows, width + width // 2), LOW),
            jax.ShapeDtypeStruct((rows, width), LOW),
        ],
        scratch_shapes=[
            pltpu.VMEM((rows, width), jnp.float32),
            pltpu.VMEM((16, width), jnp.float32),
        ]
        + square_scratch(packed, width),
        compiler_params=pltpu.CompilerParams(vmem_limit_bytes=24 * 1024 * 1024),
        cost_estimate=pl.CostEstimate(
            flops=6 * rows * width * units,
            bytes_accessed=4 * width * units,
            transcendentals=rows * units,
        ),
    )(grad, resid_one, resid_two, normed, vectors, more, up_bias[None, :], packed)


def attention_kernel(
    tokens_ref, weight_ref, bias_ref, seg_column_ref, seg_ref, qkv_ref, context_ref
):
    width = context_ref.shape[1]
    rows = tokens_ref.shape[0]
    qkv = product(tokens_ref[...], weight_ref[:, : 3 * width])
    qkv_ref[...] = (qkv + bias_ref[...]).astype(LOW)
    block = rows // 2
    for head in range(width // HDIM):
        lanes = [slice(i * width + head * HDIM, i * width + (head + 1) * HDIM) for i in range(3)]
        key, value = qkv_ref[:, lanes[1]], qkv_ref[:, lanes[2]]
        for part in range(2):
            spot = slice(part * block, (part + 1) * block)
            query = qkv_ref[spot, lanes[0]] * jnp.asarray(HDIM ** (-0.5), LOW)
            scores = lax.dot_general(
                query, key, (((1,), (1,)), ((), ())), preferred_element_type=jnp.float32
            )
            scores = jnp.where(seg_column_ref[spot, :] == seg_ref[...], scores, MASK_FILL)
            exp_scores = jnp.exp(scores - jnp.max(scores, axis=-1, keepdims=True))
            probs = exp_scores * (1.0 / jnp.sum(exp_scores, axis=-1, keepdims=True))
            context_ref[spot, lanes[0]] = jnp.dot(
                probs.astype(LOW), value, preferred_element_type=jnp.float32
            ).astype(LOW)


def attention(tokens, weight, bias, seg_row, others=()):
    rows = tokens.shape[0]
    width = bias.shape[1] // 3
    return call_after(
        attention_kernel,
        others,
        [pl.BlockSpec(memory_space=pltpu.VMEM)] * 5,
        out_shape=[
            jax.ShapeDtypeStruct((rows, 3 * width), LOW),
            jax.ShapeDtypeStruct((rows, width), LOW),
        ],
        compiler_params=pltpu.CompilerParams(vmem_limit_bytes=24 * 1024 * 1024),
        cost_estimate=pl.CostEstimate(
            flops=2 * rows * width * (3 * tokens.shape[1] + 2 * rows),
            bytes_accessed=2 * rows * tokens.shape[1] + 2 * weight.size,
            transcendentals=rows * rows * width // HDIM,
        ),
    )(tokens, weight, bias, seg_row[:, None], seg_row[None, :])


def attention_back_kernel(
    scale, queries_ref, first_ref, second_ref, grad_ref, listed_seg_ref, seg_ref, pick_ref, turned_ref,
    beside_ref, first_grad_ref, first_term_ref, second_grad_ref, second_term_ref, sums_ref, dqueries_ref,
):
    same_seg = listed_seg_ref[...] == seg_ref[...]
    width = first_ref.shape[1] // 3
    sums_ref[...] = jnp.zeros_like(sums_ref)

    def dot(left, right, left_dim, right_dim):
        return lax.dot_general(
            left,
            right,
            (((left_dim,), (right_dim,)), ((), ())),
            preferred_element_type=jnp.float32,
        )

    halves = (
        (0, first_ref, first_grad_ref, first_term_ref),
        (1, second_ref, second_grad_ref, second_term_ref),
    )
    for half, qkv_ref, dqkv_ref, term_ref in halves:
        for head in range(width // HDIM):
            lanes = slice(half * width + head * HDIM, half * width + (head + 1) * HDIM)
            keys = slice(width + head * HDIM, width + (head + 1) * HDIM)
            values = slice(2 * width + head * HDIM, 2 * width + (head + 1) * HDIM)
            query, grad = queries_ref[:, lanes], grad_ref[:, lanes]
            key, value = qkv_ref[:, keys], qkv_ref[:, values]
            scores = jnp.where(same_seg, dot(query, key, 1, 1) * scale, MASK_FILL)
            exp_scores = jnp.exp(scores - jnp.max(scores, axis=-1, keepdims=True))
            probs = exp_scores / jnp.sum(exp_scores, axis=-1, keepdims=True)
            dprobs = dot(grad, value, 1, 1)
            dscores = probs * (dprobs - jnp.sum(probs * dprobs, axis=-1, keepdims=True))
            dscores = dscores.astype(LOW)
            dqueries_ref[:, lanes] = (dot(dscores, key, 1, 0) * scale).astype(LOW)
            dqkv_ref[:, keys] = (dot(dscores, query, 0, 0) * scale).astype(LOW)
            dqkv_ref[:, values] = dot(probs.astype(LOW), grad, 0, 0).astype(LOW)
        lanes = slice(half * width, (half + 1) * width)
        dqkv_ref[:, :width] = dot(pick_ref[...], dqueries_ref[:, lanes], 0, 0).astype(LOW)
        term_ref[:, : 3 * width] = product(turned_ref[...], dqkv_ref[...]).astype(LOW)
        term_ref[:, 3 * width :] = beside_ref[:, 2 * half * width : 2 * (half + 1) * width]
        sums_ref[0:1, lanes] = jnp.sum(
            dqueries_ref[:, lanes].astype(jnp.float32), axis=0, keepdims=True
        )
        sums_ref[1:2, lanes] = jnp.sum(
            dqkv_ref[:, 2 * width :].astype(jnp.float32), axis=0, keepdims=True
        )


def attention_back(queries, first, second, grad, listed_seg, seg_row, pick, turned, beside, others):
    listed = queries.shape[0]
    rows, width = first.shape
    term = (turned.shape[0], width + beside.shape[1] // 2)
    return call_after(
        functools.partial(attention_back_kernel, HDIM ** (-0.5)),
        others,
        [pl.BlockSpec(memory_space=pltpu.VMEM)] * 9,
        out_shape=[
            jax.ShapeDtypeStruct((rows, width), LOW),
            jax.ShapeDtypeStruct(term, LOW),
            jax.ShapeDtypeStruct((rows, width), LOW),
            jax.ShapeDtypeStruct(term, LOW),
            jax.ShapeDtypeStruct((8, queries.shape[1]), jnp.float32),
        ],
        scratch_shapes=[pltpu.VMEM(queries.shape, LOW)],
        compiler_params=pltpu.CompilerParams(vmem_limit_bytes=32 * 1024 * 1024),
        cost_estimate=pl.CostEstimate(
            flops=20 * listed * rows * width // 3 + 4 * turned.size * width,
            bytes_accessed=20 * rows * width // 3,
            transcendentals=2 * listed * rows * width // (3 * HDIM),
        ),
    )(queries, first, second, grad, listed_seg[:, None], seg_row[None, :], pick, turned, beside)


def heads_of(rows):
    return rows.reshape(rows.shape[0], rows.shape[1] // HDIM, HDIM)


def attention_probs(queries, key_rows, query_seg, key_seg):
    scores = jnp.einsum(
        "qhd,khd->hqk", queries, key_rows, preferred_element_type=jnp.float32
    ) * HDIM ** (-0.5)
    same_seg = query_seg[:, None] == key_seg[None, :]
    masked = jnp.where(same_seg[None], scores, MASK_FILL)
    row_peak = jnp.max(masked, axis=-1, keepdims=True)
    exp_scores = jnp.exp(masked - row_peak)
    return exp_scores / jnp.sum(exp_scores, axis=-1, keepdims=True)


def per_device(
    tokens,
    segment_ids,
    mlm_labels,
    mask_order,
    mask_count,
    qkv_weight,
    query_bias,
    value_bias,
    out_weight,
    out_bias,
    attn_gain,
    attn_shift,
    up_weight,
    up_bias,
    down_weight,
    down_bias,
    ffn_gain,
    ffn_shift,
    head_weight,
    head_bias,
    head_gain,
    head_shift,
    decoder,
    decoder_bias,
):
    model_width = tokens.shape[1]
    tok_rows = tokens.shape[0]
    vocab_size = decoder.shape[1]
    bal_size = lax.axis_size("bal")
    dp_size = lax.axis_size("dp")
    bal_place = lax.axis_index("bal")
    dp_place = lax.axis_index("dp")
    grid = Grid(dp_size, bal_size)
    device_count = dp_size * bal_size
    my_place = dp_place * bal_size + bal_place
    slot_count = HEAD_DEV * device_count
    inv_count = 1.0 / slot_count
    part_vocab = -(-(-(-vocab_size // device_count)) // 128) * 128
    seg_row = segment_ids[0]

    listed = mask_order[0, :MASK_DEV]
    pick_mat = listed[:, None] == jnp.arange(tok_rows)[None, :]
    pick_low = pick_mat.astype(LOW)

    def pick(rows):
        return product(pick_low, rows).astype(LOW)

    listed_ids = jnp.sum(jnp.where(pick_mat, mlm_labels[None, :], 0), axis=1)
    listed_seg = jnp.sum(jnp.where(pick_mat, seg_row[None, :], 0), axis=1)

    shard_rows = qkv_weight.shape[0]
    my_units = down_weight.shape[0]
    units = my_units * device_count
    ratio = my_units // shard_rows
    half = model_width // 2

    def unit_order(rows):
        split = rows.reshape(rows.shape[0], device_count, ratio, shard_rows)
        return split.transpose(0, 2, 1, 3).reshape(rows.shape[0], units)

    down_wide = down_weight.reshape(ratio, shard_rows, model_width).transpose(1, 0, 2)
    down_wide = down_wide.reshape(shard_rows, ratio * model_width)
    packed = lax.all_gather(
        jnp.concatenate([unit_order(up_weight), down_wide], axis=1), AXES, axis=0, tiled=True
    )
    up_offsets = unit_order(up_bias[None])[0]
    my_offsets = lax.dynamic_slice_in_dim(up_bias, my_place * my_units, my_units)

    def by_heads(rows):
        split = rows.reshape(rows.shape[0], 3, 2, half)
        return grid.halves(
            split[:, :, 0].reshape(rows.shape[0], 3 * half),
            split[:, :, 1].reshape(rows.shape[0], 3 * half),
        )

    def with_half(rows, half_rows):
        return [jnp.concatenate(pair, axis=1) for pair in zip(rows, half_rows)]

    weights_run = Transfer(
        with_half(by_heads(qkv_weight), grid.halves(out_weight, head_weight)),
        grid.gather_steps(shard_rows),
    )
    qkv_width = 3 * half
    weights_run.step()
    weights_run.step()
    weights_run.step()
    info = jnp.concatenate([listed_ids, mask_count, jnp.zeros((63,), jnp.int32)])
    info = grid.gather_group(info[None])
    weights_run.step()
    all_mine, all_other = weights_run.finish()
    out_full, head_full = grid.halves(all_mine[:, qkv_width:], all_other[:, qkv_width:])

    info = jnp.concatenate(info)
    group = jnp.stack(grid.group())
    counts = info[:, MASK_DEV]
    before = group[None, :] < group[:, None]
    starts = jnp.sum(jnp.where(before, counts[None, :], 0), axis=1)
    steps = jnp.arange(MASK_DEV)
    slot_of = jnp.where(steps[None] < counts[:, None], starts[:, None] + steps[None], -1)
    my_slots = bal_place * HEAD_DEV + jnp.arange(HEAD_DEV)
    is_mine = slot_of[None] == my_slots[:, None, None]
    my_labels = jnp.sum(jnp.where(is_mine, info[None, :, :MASK_DEV], 0), axis=(1, 2))
    to_head = is_mine.astype(LOW)
    group_slots = group[:, None] * HEAD_DEV + jnp.arange(HEAD_DEV)[None, :]
    from_head = (slot_of[0][:, None, None] == group_slots[None]).astype(LOW)

    def choose(choice, parts):
        total = product(choice[:, 0], parts[0])
        for index, part in enumerate(parts[1:], 1):
            total = total + product(choice[:, index], part)
        return total.astype(LOW)

    tokens_s = pick(tokens)

    padded = jnp.pad(decoder, ((0, 0), (0, part_vocab * device_count - vocab_size)))
    padded = padded.reshape(decoder.shape[0], device_count, part_vocab).transpose(1, 0, 2)
    bias_mine, bias_other = by_heads(
        jnp.concatenate([query_bias, jnp.zeros_like(query_bias), value_bias])[None]
    )
    parts_mine, context_mine = attention(
        tokens, all_mine, bias_mine, seg_row, [padded]
    )
    parts_other, context_other = attention(tokens, all_other, bias_other, seg_row, [context_mine])
    context = jnp.concatenate(grid.halves(context_mine, context_other), axis=1)
    words = lax.all_to_all(padded, AXES, split_axis=0, concat_axis=0, tiled=True)

    picked = [tokens_s, *grid.halves(pick(context_mine), pick(context_other))]
    group_rows = grid.gather_group(jnp.concatenate(picked, axis=1))
    listed_queries = jnp.concatenate(
        [pick(parts_mine[:, :half]), pick(parts_other[:, :half])], axis=1
    )
    slot_rows = choose(to_head, group_rows)
    tokens_own, context_own = slot_rows[:, :model_width], slot_rows[:, model_width:]
    vectors = jnp.stack(
        [out_bias, attn_gain, attn_shift, down_bias, ffn_gain, ffn_shift, out_bias, out_bias]
    )
    window = min(256, model_width)
    begin = jnp.minimum(my_place * shard_rows // 128 * 128, model_width - window)
    lanes = jnp.arange(window)[:, None] + begin - my_place * shard_rows
    unit_ids = np.arange(my_units)
    my_columns = jnp.zeros((model_width, my_units), jnp.float32)
    for block in range(ratio):
        piece = lax.dynamic_slice_in_dim(packed, block * model_width + begin, window, 1)
        wanted = np.where(unit_ids // shard_rows == block, unit_ids % shard_rows, -model_width)
        is_unit = lanes == jnp.asarray(wanted, jnp.int32)[None, :]
        my_columns = my_columns + product(piece, is_unit.astype(LOW))
    my_columns = my_columns.astype(LOW)


    def layer_part(part, others, room, into=None):
        return feed_forward(
            context, tokens, out_full, vectors, packed, up_offsets, others, room, part, 2, into
        )[0]

    head_in, normed_own, resid_one, resid_two = feed_forward(
        context_own, tokens_own, out_full, vectors, packed, up_offsets, [listed_queries], 24
    )

    rows_all = lax.all_gather(normed_own, AXES, axis=0, tiled=True)
    up_all = product(rows_all, my_columns) + my_offsets

    inner_rows = product(head_in, head_full) + head_bias
    head_act, act_back = jax.vjp(gelu_exact, inner_rows)
    head_normal, head_inv = norm_parts(head_act)
    head_normed = (head_normal * head_gain + head_shift).astype(LOW)
    head_run = Transfer(
        grid.halves(head_normed[:, :half], head_normed[:, half:]), grid.gather_steps(HEAD_DEV)
    )
    head_run.step(lax.dynamic_slice(words, (nothing(head_in), 0, 0), (1, 1, 1)))
    head_run.step()
    head_run.step()
    head_run.step()
    normed_mine, normed_other = head_run.finish()
    words = words.reshape(model_width, part_vocab)
    words_mine, words_other = grid.halves(words[:half], words[half:])
    padded_bias = jnp.pad(decoder_bias, (0, part_vocab * device_count - vocab_size))
    words_bias = lax.dynamic_slice_in_dim(padded_bias, my_place * part_vocab, part_vocab)
    logits = product(normed_mine, words_mine) + product(normed_other, words_other) + words_bias
    vocab_ids = my_place * part_vocab + jnp.arange(part_vocab)
    logits = jnp.where(vocab_ids[None, :] < vocab_size, logits, MASK_FILL)
    part_peak = jnp.max(logits, axis=1)
    part_log = part_peak + jnp.log(jnp.sum(jnp.exp(logits - part_peak[:, None]), axis=1))
    spread = jnp.concatenate(
        [part_log, my_labels.astype(jnp.float32), jnp.zeros((128 - HEAD_DEV,), jnp.float32)]
    )
    spread = jnp.broadcast_to(spread[None, None], (device_count, 1, slot_count + 128))
    spread = lax.all_to_all(spread, AXES, split_axis=0, concat_axis=0, tiled=True)
    spread = spread[:, 0]
    all_logs = spread[:, :slot_count]
    labels = spread[:, slot_count : slot_count + HEAD_DEV].reshape(slot_count).astype(jnp.int32)
    peak = jnp.max(all_logs, axis=0)
    log_total = peak + jnp.log(jnp.sum(jnp.exp(all_logs - peak), axis=0))
    is_label = vocab_ids[None, :] == labels[:, None]
    dlogits = (
        (jnp.exp(logits - log_total[:, None]) - is_label.astype(jnp.float32)) * inv_count
    ).astype(LOW)
    dhead_other = product_nt(dlogits, words_other).astype(LOW)
    dhead_mine = product_nt(dlogits, words_mine).astype(LOW)
    head_run = Transfer((dhead_mine, dhead_other), grid.scatter_steps(HEAD_DEV))
    words_terms = [product_tn(rows, dlogits).astype(LOW) for rows in (normed_mine, normed_other)]
    head_run.step()
    head_run.step()
    head_run.step()
    head_run.step()
    words_bias_grad = jnp.sum(dlogits, axis=0, dtype=jnp.float32)
    target_part = jnp.sum(jnp.where(is_label, logits, 0.0))
    loss_part = jnp.where(my_place == 0, jnp.sum(log_total), 0.0) - target_part
    dhead_normed = jnp.concatenate(grid.halves(*head_run.finish()), axis=1).astype(jnp.float32)
    dhead_act, head_gain_part, head_shift_part = norm_back(
        head_normal, head_inv, head_gain, dhead_normed
    )
    dinner = act_back(dhead_act)[0].astype(LOW)
    head_bias_part = jnp.sum(dinner, axis=0, dtype=jnp.float32)
    dhead_in = product_nt(dinner, head_full).astype(LOW)

    words_grad = jnp.concatenate(grid.halves(*words_terms, nothing(dhead_in))).astype(LOW)
    words_back = lax.all_to_all(
        words_grad.reshape(device_count, decoder.shape[0], part_vocab),
        AXES,
        split_axis=0,
        concat_axis=0,
        tiled=True,
    )

    loss_high = loss_part.astype(LOW).astype(jnp.float32)
    vocab_rows = jnp.pad(words_bias_grad, (0, 2 * model_width - part_vocab))
    more = jnp.stack(
        [
            head_bias_part,
            head_gain_part,
            head_shift_part,
            jnp.where(jnp.arange(model_width) < half, loss_high, loss_part - loss_high),
            vocab_rows[:model_width],
            vocab_rows[model_width:],
            head_bias_part,
            head_bias_part,
        ]
    )
    send, dresid_own = feed_back(
        dhead_in, resid_one, resid_two, normed_own, vectors, more, packed, up_offsets, [up_all]
    )
    group_grads = grid.gather_group(dresid_own)
    factors = lax.all_gather(send, AXES, axis=0, tiled=True)

    def two_parts(rows):
        high = rows.astype(LOW)
        return jnp.concatenate([high, (rows - high.astype(jnp.float32)).astype(LOW)])

    out_term = product_tn(context_own, dresid_own).astype(LOW)
    head_term = product_tn(head_in, dinner).astype(LOW)
    beside = jnp.concatenate(grid.halves(out_term, head_term), axis=1)
    dresid_one = choose(from_head, group_grads)
    dcontext = product_nt(dresid_one, out_full).astype(LOW)
    dcontext = jnp.concatenate(grid.halves(dcontext[:, :half], dcontext[:, half:]), axis=1)
    dqkv_mine, mine_term, dqkv_other, other_term, qkv_sums = attention_back(
        listed_queries,
        parts_mine,
        parts_other,
        dcontext,
        listed_seg,
        seg_row,
        pick_low,
        tokens.T,
        beside,
        [],
    )
    other_taken = grid.shift(other_term, (3, 3), 1)
    weights_run = Transfer((mine_term, None), grid.scatter_steps(shard_rows, other_taken))
    weights_run.step(words_back)
    first_part = layer_part(0, [grid.sent], 24)
    weights_run.step()
    second_part = layer_part(1, [grid.sent], 24, first_part)
    qkv_sums = grid.halves(qkv_sums[:2, :half], qkv_sums[:2, half:])
    qkv_sums = two_parts(jnp.concatenate(qkv_sums, axis=1))

    ddown_all = factors[:, :model_width]
    hidden, act_back = jax.vjp(gelu_exact, up_all)
    dup_all = act_back(product_nt(ddown_all, down_weight))[0].astype(LOW)
    up_term = product_tn(rows_all, dup_all).astype(LOW).reshape(device_count, shard_rows, my_units)
    weights_run.step()
    qkv_sums = qkv_sums.reshape(-1, my_units)
    qkv_sums = jnp.broadcast_to(qkv_sums[None], (device_count, *qkv_sums.shape))
    up_back = lax.all_to_all(
        jnp.concatenate([up_term, qkv_sums], axis=1), AXES, split_axis=0, concat_axis=0, tiled=True
    )
    down_grad = product_tn(hidden.astype(LOW), ddown_all)
    up_grad = up_back[:, :shard_rows].transpose(1, 0, 2).reshape(shard_rows, units)
    up_grad = up_grad.astype(jnp.float32)
    qkv_sums = jnp.sum(up_back[:, shard_rows:].astype(jnp.float32), axis=0)
    qkv_sums = jnp.sum(qkv_sums.reshape(2, 2, model_width), axis=0)

    tokens_grad = product_tn(pick_low, once(dresid_one, weights_run.part[0][-1]))
    tokens_grad = tokens_grad + product_nt(dqkv_other, all_other[:, :qkv_width])
    tokens_grad = tokens_grad + product_nt(dqkv_mine, all_mine[:, :qkv_width])
    weights_run.step()
    words_back = once(words_back, weights_run.part[0][-1])
    mine, other = weights_run.finish()
    sums = factors[:, model_width:].astype(jnp.float32).reshape(device_count, 2, 16, half)
    sums = jnp.concatenate([sums[:, 0], sums[:, 1]], axis=2)
    decoder_bias_grad = sums[:, 4:6].reshape(device_count, 2 * model_width)[:, :part_vocab]
    decoder_bias_grad = decoder_bias_grad.reshape(-1)[:vocab_size]
    sums = jnp.sum(sums, axis=0)
    up_sums = sums[12:].reshape(ratio, device_count, shard_rows).transpose(1, 0, 2).reshape(-1)
    first, second = grid.halves(mine[:, :qkv_width], other[:, :qkv_width])
    qkv_grad = jnp.stack(
        [first.reshape(shard_rows, 3, half), second.reshape(shard_rows, 3, half)], axis=2
    )
    qkv_grad = qkv_grad.reshape(shard_rows, 3 * model_width).astype(jnp.float32)
    out_grad, head_grad = grid.halves(mine[:, qkv_width:], other[:, qkv_width:])
    decoder_grad = words_back.transpose(1, 0, 2).reshape(decoder.shape[0], -1)
    decoder_grad = decoder_grad[:, :vocab_size].astype(jnp.float32)
    return (
        second_part,
        (sums[3, 0] + sums[3, half]) * inv_count,
        tokens_grad,
        qkv_grad,
        qkv_sums[0],
        qkv_sums[1],
        out_grad.astype(jnp.float32),
        sums[11],
        sums[9],
        sums[10],
        up_grad,
        up_sums,
        down_grad,
        sums[8],
        sums[6],
        sums[7],
        head_grad.astype(jnp.float32),
        sums[0],
        sums[1],
        sums[2],
        decoder_grad,
        decoder_bias_grad,
    )


def solution(mesh):
    cut, rows = P(("dp", "bal"), None), P(("dp", "bal"))
    whole = P()
    return jax.shard_map(
        per_device,
        mesh=mesh,
        in_specs=(
            cut, cut, rows, cut, rows, cut, whole, whole, cut, whole, whole, whole,
            cut, whole, cut, whole, whole, whole, cut, whole, whole, whole, cut, whole,
        ),
        out_specs=(
            cut, whole, cut, cut, whole, whole, cut, whole, whole, whole, cut,
            whole, cut, whole, whole, whole, cut, whole, whole, whole, cut, whole,
        ),
        check_vma=False,
    )
```

time: 452 us -> 406 us (0.90)
  local copies, waits for them, and re-layouts: 70.4 us -> 47.8 us
  starting transfers between devices: 70.7 us -> 57.3 us
  other arithmetic: 56.8 us -> 43.6 us
    unnamed x264 -> x214, local copies, waits for them, and re-layouts: 30.9 us -> 21.6 us
    pallas_call x7, Pallas kernels: 49 us -> 57.3 us  [call_after(): return lambda *operands: call(*others, *operands)]
    dot_general x11 -> x20, matrix products: 12.8 us -> 20.1 us  [product(): return jnp.dot(left_mat, right_mat, preferred_element_type=jnp.float32)]
    all_to_all x2 -> x1, starting transfers between devices: 10.1 us -> 3.58 us  [per_device(): lax.all_to_all(jnp.concatenate([up_term, qkv_sums], axis=1), AXES, split_...]
    ppermute x34 -> x30, starting transfers between devices: 39.4 us -> 33.6 us  [shift(): return lax.ppermute(value, AXES, pairs)]
    pallas_call x1 -> x0, Pallas kernels: 5.52 us -> none  [feed_back(): pl.pallas_call(feed_back_kernel, grid=(steps,), in_specs=[block, block, b...]
    all_to_all x1, waiting for transfers between devices: 0.01 us -> 5.52 us  [per_device(): lax.all_to_all(spread, AXES, split_axis=0, concat_axis=0, tiled=True)]
    dot_general x9 -> x7, matrix products: 18.1 us -> 13 us  [product_tn(): lax.dot_general(left_mat, right_mat, (((0,), (0,)), ((), ())), preferred_...]
  transfers between devices with their start and end apart: 50 -> 46, of which waited for: 19 -> 22; matrix products, arithmetic and copies ran while one was open for 24% -> 25% of each run, Pallas kernels for 10% -> 14%
where the time goes in v3:
time: 406 us; the launch traced here: 400 us
  waiting for transfers between devices  122 us (30%)
  starting transfers between devices  57.3 us (14%)
  Pallas kernels  57.3 us (14%)
  local copies, waits for them, and re-layouts  47.8 us (12%)
  matrix products  43.9 us (11%)
  other arithmetic  43.6 us (11%)
  between operations  28.3 us (7%)
    ppermute x30, waiting for transfers between devices, shift(): return lax.ppermute(value, AXES, pairs)  105 us
    pallas_call x7, Pallas kernels, call_after(): return lambda *operands: call(*others, *operands)  57.3 us
    ppermute x30, starting transfers between devices, shift(): return lax.ppermute(value, AXES, pairs)  33.6 us
    unnamed x214, local copies, waits for them, and re-layouts  21.6 us
    dot_general x20, matrix products, product(): return jnp.dot(left_mat, right_mat, preferred_element_type=jnp.float32)  20.1 us
    dot_general x7, matrix products, product_tn(): lax.dot_general(left_mat, right_mat, (((0,), (0,)), ((), ())), preferred_...  13 us
    ppermute x9, waiting for transfers between devices, gather_group(): parts.append(lax.ppermute(rows, AXES, pairs))  11 us
    dot_general x6, matrix products, product_nt(): lax.dot_general(left_mat, right_mat, (((1,), (1,)), ((), ())), preferred_...  10.8 us
  transfers between devices with their start and end apart: 46, of which 22 were waited for; matrix products, arithmetic and copies ran while one was open for 25% of the time, Pallas kernels for 14%

profile of v3, /device:TPU:0, one launch (start us, length us, event | category | flops | bytes accessed | tf_op | source)
XLA Modules:
  0.0 399.7 jit_solution(11460168746450055077)
XLA Ops:
  14.5 5.0 %collective-permute-start.3 = (bf16[2,24,1920]{2,1,0:T(8,128)(2,1)S(1)}, bf16[2,24,1920]{2,1,0:T(8,128)(2,1)S(1)}, u32[]{:S(2)}, u32[]{:S(2)}) collective-permute-start(bf16[2,24,1920]{2,1,0:T(8,128)(2,1)S(1)} %broadcast_select_fusion.20), channel_id=1, source_target_pairs={{0,24},{1,25},{2,26},{3,27},{4,28},{5,29},{6,30},{7,31},{8,0},{9,1... | collective-permute-start | bytes 552968 | tf_op jit(solution)/shard_map/ppermute | solution.py:95
  20.6 4.0 %collective-permute-done.3 = bf16[2,24,1920]{2,1,0:T(8,128)(2,1)S(1)} collective-permute-done((bf16[2,24,1920]{2,1,0:T(8,128)(2,1)S(1)}, bf16[2,24,1920]{2,1,0:T(8,128)(2,1)S(1)}, u32[]{:S(2)}, u32[]{:S(2)}) %collective-permute-start.3) | collective-permute-done | bytes 184352 | tf_op jit(solution)/shard_map/ppermute | solution.py:95
  24.7 16.9 %collective-permute-done.2 = bf16[2,24,1920]{2,1,0:T(8,128)(2,1)S(1)} collective-permute-done((bf16[2,24,1920]{2,1,0:T(8,128)(2,1)S(1)}, bf16[2,24,1920]{2,1,0:T(8,128)(2,1)S(1)}, u32[]{:S(2)}, u32[]{:S(2)}) %collective-permute-start.2) | collective-permute-done | bytes 184352 | tf_op jit(solution)/shard_map/ppermute | solution.py:95
  43.5 15.1 %collective-permute-done.4 = bf16[4,2,24,1920]{3,2,1,0:T(8,128)(2,1)S(1)} collective-permute-done((bf16[4,2,24,1920]{3,2,1,0:T(8,128)(2,1)S(1)}, bf16[4,2,24,1920]{3,2,1,0:T(8,128)(2,1)S(1)}, u32[]{:S(2)}, u32[]{:S(2)}) %collective-permute-start.4) | collective-permute-done | bytes 737312 | tf_op jit(solution)/shard_map/ppermute | solution.py:95
  63.2 22.9 %collective-permute-done.5 = bf16[2,4,2,24,1920]{4,3,2,0,1:T(8,128)(2,1)S(1)} collective-permute-done((bf16[2,4,2,24,1920]{4,3,2,0,1:T(8,128)(2,1)}, bf16[2,4,2,24,1920]{4,3,2,0,1:T(8,128)(2,1)S(1)}, u32[]{:S(2)}, u32[]{:S(2)}) %collective-permute-start.5) | collective-permute-done | bytes 1474592 | tf_op jit(solution)/shard_map/ppermute | solution.py:95
  87.3 2.8 fusion.4.refs_2_
  90.2 2.5 collective-permute-start.9
  94.4 5.0 %all-to-all-start = ((bf16[32,24,1024]{2,1,0:T(8,128)(2,1)}), bf16[32,24,1024]{2,1,0:T(8,128)(2,1)}, u32[]{:S(2)}, u32[]{:S(2)}) async-start(bf16[32,24,1024]{2,1,0:T(8,128)(2,1)} %bitcast.332), calls=%async_computation | async-start | bytes 3145728 | tf_op jit(solution)/shard_map/all_to_all | solution.py:768
  103.3 2.3 copy.262
  113.6 6.6 %shard_map.435 = (bf16[512,1152]{1,0:T(8,128)(2,1)S(1)}, bf16[512,384]{1,0:T(8,128)(2,1)S(1)}) custom-call(bf16[32,24,1024]{2,1,0:T(8,128)(2,1)S(1)} %bitcast.333, bf16[512,768]{1,0:T(8,128)(2,1)S(1)} %copy-done.4, bf16[768,1920]{1,0:T(8,128)(2,1)S(1)} %fusion.4.refs_2_, f32[1,1152]{1,0:T(1,128)S(1)} %bitcast.340, s32[512,1]{1,0:T(8,128)S(1)} %copy.252.refs_4_, ...), custom_call_target="tpu_custom_call" | custom-call | flops 1308622848 | bytes 3735552 | tf_op jit(solution)/shard_map/pallas_call | solution.py:336
  120.5 8.7 %shard_map.436 = (bf16[512,1152]{1,0:T(8,128)(2,1)S(1)}, bf16[512,384]{1,0:T(8,128)(2,1)S(1)}) custom-call(bf16[512,384]{1,0:T(8,128)(2,1)S(1)} %get-tuple-element.40.refs_0_, bf16[512,768]{1,0:T(8,128)(2,1)S(1)} %copy-done.5, bf16[768,1920]{1,0:T(8,128)(2,1)} %collective-permute-done.6.refs_2_, f32[1,1152]{1,0:T(1,128)S(1)} %bitcast.341, ...), custom_call_target="tpu_custom_call" | custom-call | flops 1308622848 | bytes 3735552 | tf_op jit(solution)/shard_map/pallas_call | solution.py:336
  135.9 7.0 %collective-permute-done.12 = bf16[64,1536]{1,0:T(8,128)(2,1)S(1)} collective-permute-done((bf16[64,1536]{1,0:T(8,128)(2,1)S(1)}, bf16[64,1536]{1,0:T(8,128)(2,1)S(1)}, u32[]{:S(2)}, u32[]{:S(2)}) %collective-permute-start.12) | collective-permute-done | bytes 196640 | tf_op jit(solution)/shard_map/ppermute | solution.py:261
  143.2 3.7 copy-done
  146.9 4.7 %shard_map.437 = (bf16[32,768]{1,0:T(8,128)(2,1)S(1)}, bf16[32,768]{1,0:T(8,128)(2,1)}, f32[32,768]{1,0:T(8,128)S(1)}, f32[32,768]{1,0:T(8,128)S(1)}) custom-call(bf16[64,768]{1,0:T(8,128)(2,1)S(1)} %pad_maximum_fusion.7.refs_0_, bf16[32,768]{1,0:T(8,128)(2,1)S(1)} %get-tuple-element.120.refs_1_, bf16[32,768]{1,0:T(8,128)(2,1)S(1)} %get-tuple-element.119.refs_2_, ...), custom_call_target="tpu_custom_call" | custom-call | flops 301989888 | bytes 9437184 | tf_op jit(solution)/shard_map/pallas_call | solution.py:336
  155.3 2.9 fusion.142
  160.2 3.6 collective-permute-start.16
  166.0 3.9 collective-permute-done.15
  171.5 4.2 %collective-permute-done.17 = bf16[4,2,32,384]{3,2,1,0:T(8,128)(2,1)S(1)} collective-permute-done((bf16[4,2,32,384]{3,2,1,0:T(8,128)(2,1)S(1)}, bf16[4,2,32,384]{3,2,1,0:T(8,128)(2,1)S(1)}, u32[]{:S(2)}, u32[]{:S(2)}) %collective-permute-start.17) | collective-permute-done | bytes 196640 | tf_op jit(solution)/shard_map/ppermute | solution.py:95
  177.7 6.0 %collective-permute-done.18 = bf16[2,4,2,32,384]{4,3,2,0,1:T(8,128)(2,1)S(1)} collective-permute-done((bf16[2,4,2,32,384]{4,3,2,0,1:T(8,128)(2,1)S(1)}, bf16[2,4,2,32,384]{4,3,2,0,1:T(8,128)(2,1)S(1)}, u32[]{:S(2)}, u32[]{:S(2)}) %collective-permute-start.18) | collective-permute-done | bytes 393248 | tf_op jit(solution)/shard_map/ppermute | solution.py:95
  185.2 2.6 broadcast_select_fusion.8
  190.4 2.8 fusion.148
  196.0 4.5 %all-to-all-start.1 = ((f32[32,1,1152]{2,1,0:T(1,128)}), f32[32,1,1152]{2,1,0:T(1,128)S(1)}, u32[]{:S(2)}, u32[]{:S(2)}) async-start(f32[32,1,1152]{2,1,0:T(1,128)} %broadcast_in_dim.541), calls=%async_computation.1 | async-start | bytes 294912 | tf_op jit(solution)/shard_map/all_to_all | solution.py:830
  203.5 5.5 %all-to-all-done.1 = f32[32,1,1152]{2,1,0:T(1,128)S(1)} async-done(((f32[32,1,1152]{2,1,0:T(1,128)}), f32[32,1,1152]{2,1,0:T(1,128)S(1)}, u32[]{:S(2)}, u32[]{:S(2)}) %all-to-all-start.1) | async-done | bytes 147488 | tf_op jit(solution)/shard_map/all_to_all | solution.py:830
  209.8 4.5 %convert_reduce_fusion = (f32[1024]{0:T(1024)S(1)}, bf16[1024,1024]{0,1:T(8,128)(2,1)S(1)}, f32[]{:T(128)}) fusion(s32[1024]{0:T(1024)S(1)} %convert_element_type.565, s32[1024]{0:T(1024)S(1)} %copy-done.63, f32[1024,1024]{0,1:T(8,128)} %copy-done.29, f32[1024]{0:T(1024)S(1)} %get-tuple-element.78), kind=kLoop, calls=%fused_computation.6 | loop fusion | flops 10484735 | bytes 6307844 | tf_op jit(solution)/shard_map/reduce_sum | solution.py:848
  216.1 2.2 convolution_add_fusion.4
  219.6 3.1 convolution_convert_fusion.2
  224.9 3.6 collective-permute-done.22
  228.5 2.2 collective-permute-done.21
  231.3 5.3 %collective-permute-done.23 = bf16[4,2,32,384]{3,2,1,0:T(8,128)(2,1)S(1)} collective-permute-done((bf16[4,2,32,384]{3,2,1,0:T(8,128)(2,1)S(1)}, bf16[4,2,32,384]{3,2,1,0:T(8,128)(2,1)S(1)}, u32[]{:S(2)}, u32[]{:S(2)}) %collective-permute-start.23) | collective-permute-done | bytes 196640 | tf_op jit(solution)/shard_map/ppermute | solution.py:95
  237.0 3.5 collective-permute-start.26
  243.1 2.4 collective-permute-done.25
  253.4 3.0 broadcast_select_fusion.7
  257.7 3.6 all-to-all-start.2
  261.5 2.4 convolution_add_fusion.2.refs_0_
  264.0 3.7 copy-done.1
  267.6 7.0 %shard_map.438 = (bf16[32,1152]{1,0:T(8,128)(2,1)S(1)}, bf16[32,768]{1,0:T(8,128)(2,1)S(1)}) custom-call(f32[1024,96]{1,0:T(8,128)S(1)} %convolution_add_fusion.2.refs_0_, bf16[32,768]{1,0:T(8,128)(2,1)S(1)} %convolution_convert_fusion.9.refs_1_, f32[32,768]{1,0:T(8,128)S(1)} %get-tuple-element.45.refs_2_, f32[32,768]{1,0:T(8,128)S(1)} %get-tuple-element.46.refs_3_, ...), custom_call_target="tpu_custom_call" | custom-call | flops 452984832 | bytes 9437184 | tf_op jit(solution)/shard_map/pallas_call | solution.py:336
  279.0 3.5 collective-permute-done.29
  283.5 11.2 %shard_map.439 = (bf16[512,1152]{1,0:T(8,128)(2,1)S(1)}, bf16[768,1920]{1,0:T(8,128)(2,1)S(1)}, bf16[512,1152]{1,0:T(8,128)(2,1)S(1)}, bf16[768,1920]{1,0:T(8,128)(2,1)}, f32[8,768]{1,0:T(8,128)S(1)}) custom-call(bf16[64,768]{1,0:T(8,128)(2,1)S(1)} %pad_maximum_fusion.7.refs_0_, bf16[512,1152]{1,0:T(8,128)(2,1)S(1)} %copy-done.24, ...), custom_call_target="tpu_custom_call" | custom-call | flops 2063597568 | bytes 3932160 | tf_op jit(solution)/shard_map/pallas_call | solution.py:336
  304.7 2.4 fusion.24
  309.3 3.2 fusion.9
  313.9 4.8 %collective-permute-done.32 = bf16[4,2,24,1920]{3,2,1,0:T(8,128)(2,1)S(1)} collective-permute-done((bf16[4,2,24,1920]{3,2,1,0:T(8,128)(2,1)S(1)}, bf16[4,2,24,1920]{3,2,1,0:T(8,128)(2,1)S(1)}, u32[]{:S(2)}, u32[]{:S(2)}) %collective-permute-start.32) | collective-permute-done | bytes 737312 | tf_op jit(solution)/shard_map/ppermute | solution.py:95
  318.8 9.2 %collective-permute-done.33 = bf16[4,2,24,1920]{3,2,1,0:T(8,128)(2,1)S(1)} collective-permute-done((bf16[4,2,24,1920]{3,2,1,0:T(8,128)(2,1)S(1)}, bf16[4,2,24,1920]{3,2,1,0:T(8,128)(2,1)S(1)}, u32[]{:S(2)}, u32[]{:S(2)}) %collective-permute-start.33) | collective-permute-done | bytes 737312 | tf_op jit(solution)/shard_map/ppermute | solution.py:95
  331.2 9.2 %shard_map.440 = (bf16[512,768]{1,0:T(8,128)(2,1)S(1)}, bf16[256,768]{1,0:T(8,128)(2,1)}, f32[256,768]{1,0:T(8,128)}, f32[256,768]{1,0:T(8,128)}) custom-call(bf16[4,2,24,1920]{3,2,1,0:T(8,128)(2,1)S(1)} %get-tuple-element.86.refs_0_, bf16[512,768]{1,0:T(8,128)(2,1)S(1)} %pad_maximum_fusion.3.refs_1_.refs_2_, bf16[512,768]{1,0:T(8,128)(2,1)S(1)} %copy-done.6, ...), custom_call_target="tpu_custom_call" | custom-call | flops 2415919104 | bytes 9437184 | tf_op jit(solution)/shard_map/pallas_call | solution.py:336
  340.4 10.1 %shard_map.441 = (bf16[512,768]{1,0:T(8,128)(2,1)}, bf16[256,768]{1,0:T(8,128)(2,1)}, f32[256,768]{1,0:T(8,128)}, f32[256,768]{1,0:T(8,128)}) custom-call(bf16[4,2,24,1920]{3,2,1,0:T(8,128)(2,1)S(1)} %fusion.12.refs_0_, bf16[512,768]{1,0:T(8,128)(2,1)S(1)} %get-tuple-element.50.refs_1_, bf16[512,768]{1,0:T(8,128)(2,1)S(1)} %pad_maximum_fusion.3.refs_1_.refs_2_, ...), custom_call_target="tpu_custom_call" | custom-call | flops 2415919104 | bytes 9437184 | tf_op jit(solution)/shard_map/pallas_call | solution.py:336
  353.5 3.9 collective-permute-start.35
  359.4 2.4 add_add_fusion
  365.0 3.4 convolution_convert_fusion.6
  371.8 3.6 all-to-all-start.3
  (479 shorter events, 115.3 us)
Async XLA Ops:
  7.2 136.0 %all-gather.4.cloned.1.call-start = ((), (), s32[]{:S(2)}) async-start(), calls=%async_computation.4 | async-start | bytes 9732096 | tf_op jit(solution)/shard_map/all_gather | solution.py:706
  13.0 1.5 collective-permute-start
  14.5 10.1 %collective-permute-start.3 = (bf16[2,24,1920]{2,1,0:T(8,128)(2,1)S(1)}, bf16[2,24,1920]{2,1,0:T(8,128)(2,1)S(1)}, u32[]{:S(2)}, u32[]{:S(2)}) collective-permute-start(bf16[2,24,1920]{2,1,0:T(8,128)(2,1)S(1)} %broadcast_select_fusion.20), channel_id=1, source_target_pairs={{0,24},{1,25},{2,26},{3,27},{4,28},{5,29},{6,30},{7,31},{8,0},{9,1... | collective-permute-start | bytes 552968 | tf_op jit(solution)/shard_map/ppermute | solution.py:95
  19.6 22.0 %collective-permute-start.2 = (bf16[2,24,1920]{2,1,0:T(8,128)(2,1)S(1)}, bf16[2,24,1920]{2,1,0:T(8,128)(2,1)S(1)}, u32[]{:S(2)}, u32[]{:S(2)}) collective-permute-start(bf16[2,24,1920]{2,1,0:T(8,128)(2,1)S(1)} %broadcast_select_fusion.20), channel_id=1, source_target_pairs={{0,16},{1,17},{2,18},{3,19},{4,20},{5,21},{6,22},{7,23},{8,24},{9,... | collective-permute-start | bytes 552968 | tf_op jit(solution)/shard_map/ppermute | solution.py:95
  19.6 22.0 %collective-permute-start.1 = (bf16[2,24,1920]{2,1,0:T(8,128)(2,1)S(1)}, bf16[2,24,1920]{2,1,0:T(8,128)(2,1)S(1)}, u32[]{:S(2)}, u32[]{:S(2)}) collective-permute-start(bf16[2,24,1920]{2,1,0:T(8,128)(2,1)S(1)} %broadcast_select_fusion.20), channel_id=1, source_target_pairs={{0,8},{1,9},{2,10},{3,11},{4,12},{5,13},{6,14},{7,15},{8,16},{9,17... | collective-permute-start | bytes 552968 | tf_op jit(solution)/shard_map/ppermute | solution.py:95
  41.9 16.7 %collective-permute-start.4 = (bf16[4,2,24,1920]{3,2,1,0:T(8,128)(2,1)S(1)}, bf16[4,2,24,1920]{3,2,1,0:T(8,128)(2,1)S(1)}, u32[]{:S(2)}, u32[]{:S(2)}) collective-permute-start(bf16[4,2,24,1920]{3,2,1,0:T(8,128)(2,1)S(1)} %select_select_fusion.1), channel_id=1, source_target_pairs={{0,4},{1,3},{2,6},{3,1},{4,0},{5,7},{6,2},{7,5},{8,12},{9,11},{10,... | collective-permute-start | bytes 2211848 | tf_op jit(solution)/shard_map/ppermute | solution.py:95
  59.9 26.2 %collective-permute-start.5 = (bf16[2,4,2,24,1920]{4,3,2,0,1:T(8,128)(2,1)}, bf16[2,4,2,24,1920]{4,3,2,0,1:T(8,128)(2,1)S(1)}, u32[]{:S(2)}, u32[]{:S(2)}) collective-permute-start(bf16[2,4,2,24,1920]{4,3,2,0,1:T(8,128)(2,1)} %broadcast_select_fusion), channel_id=1, source_target_pairs={{0,2},{1,5},{2,0},{3,7},{4,6},{5,1},{6,4},{7,3},{8,10},{9,13},{10,... | collective-permute-start | bytes 4423688 | tf_op jit(solution)/shard_map/ppermute | solution.py:95
  62.8 66.4 %copy-start.60 = (s32[64]{0:T(128)}, s32[64]{0:T(128)S(1)}, u32[]{:S(2)}) copy-start(s32[64]{0:T(128)S(1)} %slice_bitcast_fusion.20) | copy-start | bytes 772
  90.1 30.4 %collective-permute-start.6 = (bf16[768,1920]{1,0:T(8,128)(2,1)S(1)}, bf16[768,1920]{1,0:T(8,128)(2,1)}, u32[]{:S(2)}, u32[]{:S(2)}) collective-permute-start(bf16[768,1920]{1,0:T(8,128)(2,1)S(1)} %fusion.4.refs_2_), channel_id=1, source_target_pairs={{0,1},{1,0},{2,3},{3,2},{4,5},{5,4},{6,7},{7,6},{8,9},{9,8},{10,11... | collective-permute-start | bytes 8847368 | tf_op jit(solution)/shard_map/ppermute | solution.py:95
  90.2 20.1 %collective-permute-start.9 = (s32[1,128]{1,0:T(1,128)S(1)}, s32[1,128]{1,0:T(1,128)S(1)}, u32[]{:S(2)}, u32[]{:S(2)}) collective-permute-start(s32[1,128]{1,0:T(1,128)S(1)} %add_bitcast_fusion.1), channel_id=1, source_target_pairs={{0,3},{1,2},{2,1},{3,0},{4,7},{5,6},{6,5},{7,4},{8,11},{9,10},{10,... | collective-permute-start | bytes 1544 | tf_op jit(solution)/shard_map/ppermute | solution.py:261
  92.8 17.5 %collective-permute-start.8 = (s32[1,128]{1,0:T(1,128)S(1)}, s32[1,128]{1,0:T(1,128)S(1)}, u32[]{:S(2)}, u32[]{:S(2)}) collective-permute-start(s32[1,128]{1,0:T(1,128)S(1)} %add_bitcast_fusion.1), channel_id=1, source_target_pairs={{0,2},{1,3},{2,0},{3,1},{4,6},{5,7},{6,4},{7,5},{8,10},{9,11},{10,... | collective-permute-start | bytes 1544 | tf_op jit(solution)/shard_map/ppermute | solution.py:261
  92.8 17.6 %collective-permute-start.7 = (s32[1,128]{1,0:T(1,128)S(1)}, s32[1,128]{1,0:T(1,128)S(1)}, u32[]{:S(2)}, u32[]{:S(2)}) collective-permute-start(s32[1,128]{1,0:T(1,128)S(1)} %add_bitcast_fusion.1), channel_id=1, source_target_pairs={{0,1},{1,0},{2,3},{3,2},{4,5},{5,4},{6,7},{7,6},{8,9},{9,8},{10,11... | collective-permute-start | bytes 1544 | tf_op jit(solution)/shard_map/ppermute | solution.py:261
  94.4 59.0 %all-to-all-start = ((bf16[32,24,1024]{2,1,0:T(8,128)(2,1)}), bf16[32,24,1024]{2,1,0:T(8,128)(2,1)}, u32[]{:S(2)}, u32[]{:S(2)}) async-start(bf16[32,24,1024]{2,1,0:T(8,128)(2,1)} %bitcast.332), calls=%async_computation | async-start | bytes 3145728 | tf_op jit(solution)/shard_map/all_to_all | solution.py:768
  99.4 162.1 %all-gather.6.cloned.1.call-start = ((), (), s32[]{:S(2)}) async-start(), calls=%async_computation.5 | async-start | bytes 1622016 | tf_op jit(solution)/shard_map/all_gather | solution.py:802
  105.6 110.5 %copy-start.56 = (s32[256]{0:T(256)}, s32[256]{0:T(256)S(1)}, u32[]{:S(2)}) copy-start(s32[256]{0:T(256)S(1)} %add_subtract_fusion) | copy-start | bytes 3076
  130.4 12.6 %collective-permute-start.11 = (bf16[64,1536]{1,0:T(8,128)(2,1)S(1)}, bf16[64,1536]{1,0:T(8,128)(2,1)S(1)}, u32[]{:S(2)}, u32[]{:S(2)}) collective-permute-start(bf16[64,1536]{1,0:T(8,128)(2,1)S(1)} %pad_maximum_fusion.6), channel_id=1, source_target_pairs={{0,2},{1,3},{2,0},{3,1},{4,6},{5,7},{6,4},{7,5},{8,10},{9,11},{10,... | collective-permute-start | bytes 589832 | tf_op jit(solution)/shard_map/ppermute | solution.py:261
  132.1 3.6 collective-permute-start.10
  132.1 10.8 %collective-permute-start.12 = (bf16[64,1536]{1,0:T(8,128)(2,1)S(1)}, bf16[64,1536]{1,0:T(8,128)(2,1)S(1)}, u32[]{:S(2)}, u32[]{:S(2)}) collective-permute-start(bf16[64,1536]{1,0:T(8,128)(2,1)S(1)} %pad_maximum_fusion.6), channel_id=1, source_target_pairs={{0,3},{1,2},{2,1},{3,0},{4,7},{5,6},{6,5},{7,4},{8,11},{9,10},{10,... | collective-permute-start | bytes 589832 | tf_op jit(solution)/shard_map/ppermute | solution.py:261
  158.6 1.6 collective-permute-start.13
  160.2 5.7 %collective-permute-start.16 = (bf16[2,32,384]{2,1,0:T(8,128)(2,1)S(1)}, bf16[2,32,384]{2,1,0:T(8,128)(2,1)S(1)}, u32[]{:S(2)}, u32[]{:S(2)}) collective-permute-start(bf16[2,32,384]{2,1,0:T(8,128)(2,1)S(1)} %broadcast_select_fusion.27), channel_id=1, source_target_pairs={{0,24},{1,25},{2,26},{3,27},{4,28},{5,29},{6,30},{7,31},{8,0},{9,1... | collective-permute-start | bytes 147464 | tf_op jit(solution)/shard_map/ppermute | solution.py:95
  163.8 6.0 %collective-permute-start.15 = (bf16[2,32,384]{2,1,0:T(8,128)(2,1)S(1)}, bf16[2,32,384]{2,1,0:T(8,128)(2,1)S(1)}, u32[]{:S(2)}, u32[]{:S(2)}) collective-permute-start(bf16[2,32,384]{2,1,0:T(8,128)(2,1)S(1)} %broadcast_select_fusion.27), channel_id=1, source_target_pairs={{0,16},{1,17},{2,18},{3,19},{4,20},{5,21},{6,22},{7,23},{8,24},{9,... | collective-permute-start | bytes 147464 | tf_op jit(solution)/shard_map/ppermute | solution.py:95
  163.8 6.0 %collective-permute-start.14 = (bf16[2,32,384]{2,1,0:T(8,128)(2,1)S(1)}, bf16[2,32,384]{2,1,0:T(8,128)(2,1)S(1)}, u32[]{:S(2)}, u32[]{:S(2)}) collective-permute-start(bf16[2,32,384]{2,1,0:T(8,128)(2,1)S(1)} %broadcast_select_fusion.27), channel_id=1, source_target_pairs={{0,8},{1,9},{2,10},{3,11},{4,12},{5,13},{6,14},{7,15},{8,16},{9,17... | collective-permute-start | bytes 147464 | tf_op jit(solution)/shard_map/ppermute | solution.py:95
  170.0 5.7 %collective-permute-start.17 = (bf16[4,2,32,384]{3,2,1,0:T(8,128)(2,1)S(1)}, bf16[4,2,32,384]{3,2,1,0:T(8,128)(2,1)S(1)}, u32[]{:S(2)}, u32[]{:S(2)}) collective-permute-start(bf16[4,2,32,384]{3,2,1,0:T(8,128)(2,1)S(1)} %select_select_fusion.2), channel_id=1, source_target_pairs={{0,4},{1,3},{2,6},{3,1},{4,0},{5,7},{6,2},{7,5},{8,12},{9,11},{10,... | collective-permute-start | bytes 589832 | tf_op jit(solution)/shard_map/ppermute | solution.py:95
  175.8 7.8 %collective-permute-start.18 = (bf16[2,4,2,32,384]{4,3,2,0,1:T(8,128)(2,1)S(1)}, bf16[2,4,2,32,384]{4,3,2,0,1:T(8,128)(2,1)S(1)}, u32[]{:S(2)}, u32[]{:S(2)}) collective-permute-start(bf16[2,4,2,32,384]{4,3,2,0,1:T(8,128)(2,1)S(1)} %broadcast_select_fusion.13), channel_id=1, source_target_pairs={{0,2},{1,5},{2,0},{3,7},{4,6},{5,1},{6,4},{7,3},{8,10},{9,13},{10,... | collective-permute-start | bytes 1179656 | tf_op jit(solution)/shard_map/ppermute | solution.py:95
  185.2 5.1 %collective-permute-start.19 = (bf16[1024,384]{1,0:T(8,128)(2,1)}, bf16[1024,384]{1,0:T(8,128)(2,1)}, u32[]{:S(2)}, u32[]{:S(2)}) collective-permute-start(bf16[1024,384]{1,0:T(8,128)(2,1)} %fusion.22), channel_id=1, source_target_pairs={{0,1},{1,0},{2,3},{3,2},{4,5},{5,4},{6,7},{7,6},{8,9},{9,8},{10,11... | collective-permute-start | bytes 2359304 | tf_op jit(solution)/shard_map/ppermute | solution.py:95
  196.0 13.0 %all-to-all-start.1 = ((f32[32,1,1152]{2,1,0:T(1,128)}), f32[32,1,1152]{2,1,0:T(1,128)S(1)}, u32[]{:S(2)}, u32[]{:S(2)}) async-start(f32[32,1,1152]{2,1,0:T(1,128)} %broadcast_in_dim.541), calls=%async_computation.1 | async-start | bytes 294912 | tf_op jit(solution)/shard_map/all_to_all | solution.py:830
  215.6 7.0 %collective-permute-start.20 = (bf16[1024,384]{1,0:T(8,128)(2,1)S(1)}, bf16[1024,384]{1,0:T(8,128)(2,1)S(1)}, u32[]{:S(2)}, u32[]{:S(2)}) collective-permute-start(bf16[1024,384]{1,0:T(8,128)(2,1)S(1)} %convolution_convert_fusion.4), channel_id=1, source_target_pairs={{0,1},{1,0},{2,3},{3,2},{4,5},{5,4},{6,7},{7,6},{8,9},{9,8},{10,11... | collective-permute-start | bytes 2359304 | tf_op jit(solution)/shard_map/ppermute | solution.py:95
  222.8 5.7 %collective-permute-start.22 = (bf16[4,2,32,384]{3,2,1,0:T(8,128)(2,1)S(1)}, bf16[4,2,32,384]{3,2,1,0:T(8,128)(2,1)S(1)}, u32[]{:S(2)}, u32[]{:S(2)}) collective-permute-start(bf16[4,2,32,384]{3,2,1,0:T(8,128)(2,1)S(1)} %get-tuple-element.100), channel_id=1, source_target_pairs={{0,2},{1,5},{2,0},{3,7},{4,6},{5,1},{6,4},{7,3},{8,10},{9,13},{10,... | collective-permute-start | bytes 589832 | tf_op jit(solution)/shard_map/ppermute | solution.py:95
  223.2 7.5 %collective-permute-start.21 = (bf16[4,2,32,384]{3,2,1,0:T(8,128)(2,1)S(1)}, bf16[4,2,32,384]{3,2,1,0:T(8,128)(2,1)S(1)}, u32[]{:S(2)}, u32[]{:S(2)}) collective-permute-start(bf16[4,2,32,384]{3,2,1,0:T(8,128)(2,1)S(1)} %get-tuple-element.101), channel_id=1, source_target_pairs={{0,2},{1,5},{2,0},{3,7},{4,6},{5,1},{6,4},{7,3},{8,10},{9,13},{10,... | collective-permute-start | bytes 589832 | tf_op jit(solution)/shard_map/ppermute | solution.py:95
  230.8 5.7 %collective-permute-start.23 = (bf16[4,2,32,384]{3,2,1,0:T(8,128)(2,1)S(1)}, bf16[4,2,32,384]{3,2,1,0:T(8,128)(2,1)S(1)}, u32[]{:S(2)}, u32[]{:S(2)}) collective-permute-start(bf16[4,2,32,384]{3,2,1,0:T(8,128)(2,1)S(1)} %fusion.37), channel_id=1, source_target_pairs={{0,4},{1,3},{2,6},{3,1},{4,0},{5,7},{6,2},{7,5},{8,12},{9,11},{10,... | collective-permute-start | bytes 589832 | tf_op jit(solution)/shard_map/ppermute | solution.py:95
  236.7 6.5 %collective-permute-start.24 = (bf16[2,32,384]{2,1,0:T(8,128)(2,1)S(1)}, bf16[2,32,384]{2,1,0:T(8,128)(2,1)S(1)}, u32[]{:S(2)}, u32[]{:S(2)}) collective-permute-start(bf16[2,32,384]{2,1,0:T(8,128)(2,1)S(1)} %get-tuple-element.106), channel_id=1, source_target_pairs={{0,8},{1,9},{2,10},{3,11},{4,12},{5,13},{6,14},{7,15},{8,16},{9,17... | collective-permute-start | bytes 147464 | tf_op jit(solution)/shard_map/ppermute | solution.py:95
  237.0 6.1 %collective-permute-start.26 = (bf16[2,32,384]{2,1,0:T(8,128)(2,1)S(1)}, bf16[2,32,384]{2,1,0:T(8,128)(2,1)S(1)}, u32[]{:S(2)}, u32[]{:S(2)}) collective-permute-start(bf16[2,32,384]{2,1,0:T(8,128)(2,1)S(1)} %get-tuple-element.107), channel_id=1, source_target_pairs={{0,24},{1,25},{2,26},{3,27},{4,28},{5,29},{6,30},{7,31},{8,0},{9,1... | collective-permute-start | bytes 147464 | tf_op jit(solution)/shard_map/ppermute | solution.py:95
  240.5 5.0 %collective-permute-start.25 = (bf16[2,32,384]{2,1,0:T(8,128)(2,1)S(1)}, bf16[2,32,384]{2,1,0:T(8,128)(2,1)S(1)}, u32[]{:S(2)}, u32[]{:S(2)}) collective-permute-start(bf16[2,32,384]{2,1,0:T(8,128)(2,1)S(1)} %get-tuple-element.108), channel_id=1, source_target_pairs={{0,16},{1,17},{2,18},{3,19},{4,20},{5,21},{6,22},{7,23},{8,24},{9,... | collective-permute-start | bytes 147464 | tf_op jit(solution)/shard_map/ppermute | solution.py:95
  245.5 1.8 collective-permute-start.27
  257.7 44.3 %all-to-all-start.2 = ((bf16[32,24,1024]{2,1,0:T(8,128)(2,1)}), bf16[32,24,1024]{2,1,0:T(8,128)(2,1)}, u32[]{:S(2)}, u32[]{:S(2)}) async-start(bf16[32,24,1024]{2,1,0:T(8,128)(2,1)} %bitcast.342), calls=%async_computation.2 | async-start | bytes 3145728 | tf_op jit(solution)/shard_map/all_to_all | solution.py:860
  261.3 100.6 %all-gather.8.cloned.1.call-start = ((), (), s32[]{:S(2)}) async-start(), calls=%async_computation.6 | async-start | bytes 2433024 | tf_op jit(solution)/shard_map/all_gather | solution.py:886
  274.6 4.1 %collective-permute-start.30 = (bf16[32,768]{1,0:T(8,128)(2,1)S(1)}, bf16[32,768]{1,0:T(8,128)(2,1)S(1)}, u32[]{:S(2)}, u32[]{:S(2)}) collective-permute-start(bf16[32,768]{1,0:T(8,128)(2,1)S(1)} %get-tuple-element.47), channel_id=1, source_target_pairs={{0,3},{1,2},{2,1},{3,0},{4,7},{5,6},{6,5},{7,4},{8,11},{9,10},{10,... | collective-permute-start | bytes 147464 | tf_op jit(solution)/shard_map/ppermute | solution.py:261
  276.0 6.5 %collective-permute-start.29 = (bf16[32,768]{1,0:T(8,128)(2,1)S(1)}, bf16[32,768]{1,0:T(8,128)(2,1)S(1)}, u32[]{:S(2)}, u32[]{:S(2)}) collective-permute-start(bf16[32,768]{1,0:T(8,128)(2,1)S(1)} %get-tuple-element.47), channel_id=1, source_target_pairs={{0,2},{1,3},{2,0},{3,1},{4,6},{5,7},{6,4},{7,5},{8,10},{9,11},{10,... | collective-permute-start | bytes 147464 | tf_op jit(solution)/shard_map/ppermute | solution.py:261
  276.6 1.5 collective-permute-start.28
  298.9 5.7 %collective-permute-start.31 = (bf16[768,1920]{1,0:T(8,128)(2,1)}, bf16[768,1920]{1,0:T(8,128)(2,1)}, u32[]{:S(2)}, u32[]{:S(2)}) collective-permute-start(bf16[768,1920]{1,0:T(8,128)(2,1)} %get-tuple-element.49), channel_id=1, source_target_pairs={{0,1},{1,0},{2,3},{3,2},{4,5},{5,4},{6,7},{7,6},{8,9},{9,8},{10,11... | collective-permute-start | bytes 8847368 | tf_op jit(solution)/shard_map/ppermute | solution.py:95
  307.1 11.7 %collective-permute-start.32 = (bf16[4,2,24,1920]{3,2,1,0:T(8,128)(2,1)S(1)}, bf16[4,2,24,1920]{3,2,1,0:T(8,128)(2,1)S(1)}, u32[]{:S(2)}, u32[]{:S(2)}) collective-permute-start(bf16[4,2,24,1920]{3,2,1,0:T(8,128)(2,1)S(1)} %get-tuple-element.87), channel_id=1, source_target_pairs={{0,2},{1,5},{2,0},{3,7},{4,6},{5,1},{6,4},{7,3},{8,10},{9,13},{10,... | collective-permute-start | bytes 2211848 | tf_op jit(solution)/shard_map/ppermute | solution.py:95
  307.8 20.1 %collective-permute-start.33 = (bf16[4,2,24,1920]{3,2,1,0:T(8,128)(2,1)S(1)}, bf16[4,2,24,1920]{3,2,1,0:T(8,128)(2,1)S(1)}, u32[]{:S(2)}, u32[]{:S(2)}) collective-permute-start(bf16[4,2,24,1920]{3,2,1,0:T(8,128)(2,1)S(1)} %get-tuple-element.86.refs_0_), channel_id=1, source_target_pairs={{0,2},{1,5},{2,0},{3,7},{4,6},{5,1},{6,4},{7,3},{8,10},{9,13},{10,... | collective-permute-start | bytes 2211848 | tf_op jit(solution)/shard_map/ppermute | solution.py:95
  329.9 20.7 %collective-permute-start.34 = (bf16[4,2,24,1920]{3,2,1,0:T(8,128)(2,1)S(1)}, bf16[4,2,24,1920]{3,2,1,0:T(8,128)(2,1)S(1)}, u32[]{:S(2)}, u32[]{:S(2)}) collective-permute-start(bf16[4,2,24,1920]{3,2,1,0:T(8,128)(2,1)S(1)} %fusion.12.refs_0_), channel_id=1, source_target_pairs={{0,4},{1,3},{2,6},{3,1},{4,0},{5,7},{6,2},{7,5},{8,12},{9,11},{10,... | collective-permute-start | bytes 2211848 | tf_op jit(solution)/shard_map/ppermute | solution.py:95
  353.5 30.6 %collective-permute-start.35 = (bf16[2,24,1920]{2,1,0:T(8,128)(2,1)}, bf16[2,24,1920]{2,1,0:T(8,128)(2,1)}, u32[]{:S(2)}, u32[]{:S(2)}) collective-permute-start(bf16[2,24,1920]{2,1,0:T(8,128)(2,1)} %get-tuple-element.91), channel_id=1, source_target_pairs={{0,8},{1,9},{2,10},{3,11},{4,12},{5,13},{6,14},{7,15},{8,16},{9,17... | collective-permute-start | bytes 552968 | tf_op jit(solution)/shard_map/ppermute | solution.py:95
  357.4 22.6 %collective-permute-start.37 = (bf16[2,24,1920]{2,1,0:T(8,128)(2,1)}, bf16[2,24,1920]{2,1,0:T(8,128)(2,1)}, u32[]{:S(2)}, u32[]{:S(2)}) collective-permute-start(bf16[2,24,1920]{2,1,0:T(8,128)(2,1)} %get-tuple-element.92), channel_id=1, source_target_pairs={{0,24},{1,25},{2,26},{3,27},{4,28},{5,29},{6,30},{7,31},{8,0},{9,1... | collective-permute-start | bytes 552968 | tf_op jit(solution)/shard_map/ppermute | solution.py:95
  357.4 26.7 %collective-permute-start.36 = (bf16[2,24,1920]{2,1,0:T(8,128)(2,1)}, bf16[2,24,1920]{2,1,0:T(8,128)(2,1)}, u32[]{:S(2)}, u32[]{:S(2)}) collective-permute-start(bf16[2,24,1920]{2,1,0:T(8,128)(2,1)} %get-tuple-element.93), channel_id=1, source_target_pairs={{0,16},{1,17},{2,18},{3,19},{4,20},{5,21},{6,22},{7,23},{8,24},{9,... | collective-permute-start | bytes 552968 | tf_op jit(solution)/shard_map/ppermute | solution.py:95
  371.8 17.9 %all-to-all-start.3 = ((bf16[32,56,96]{2,1,0:T(8,128)(2,1)}), bf16[32,56,96]{2,1,0:T(8,128)(2,1)S(1)}, u32[]{:S(2)}, u32[]{:S(2)}) async-start(bf16[32,56,96]{2,1,0:T(8,128)(2,1)} %pad_maximum_fusion.4), calls=%async_computation.3 | async-start | bytes 917504 | tf_op jit(solution)/shard_map/all_to_all | solution.py:926
  385.7 2.2 collective-permute-start.38
  (102 other events, 951.0 us)
Sparse Core Ops, SparseCore 0:
  12.7 107.5 all-gather.3
  188.0 55.6 all-gather.5
  299.1 57.0 all-gather.7
